TPU v7x, 32 devices: a whole 2x2x4 slice. The times are simulated.
32 devices in a mesh: parts: 2 (over y), replica: 4 (over x, core), tensor: 4 (over z).
Axes of the slice: x: 2, y: 2, z: 4, core: 2. Of those that a mesh axis runs over, the one named last changes fastest.
Arguments:
- hidden: bfloat16 [112, 2, 8192], P(('parts', 'replica'), None, 'tensor'), parts along dimension 0, may hold values from -6 to 6
- queries: bfloat16 [112, 2, 64, 128], P(('parts', 'replica'), None, 'tensor'), parts along dimension 0, may hold values from -220 to 220
- kv_cache: bfloat16 [96, 128, 8, 256], P(('parts', 'replica'), None, 'tensor'), parts along dimension 0, may hold values from -6.5 to 6.5
- w_kv: bfloat16 [8192, 8, 256], P(None, 'tensor'), may hold values from -0.0625 to 0.0625
- store_a: bfloat16 [64, 2, 64, 8192], P(('parts', 'replica'), None, None, 'tensor'), parts along dimension 0, may hold values from -0.0625 to 0.0625
- store_b: bfloat16 [64, 2, 64, 1024], P(('parts', 'replica'), None, None, 'tensor'), parts along dimension 0, may hold values from -0.75 to 0.75
- lengths: int32 [96], P('parts'), parts along dimension 0, may hold values from 2 to 128, as said below
- arrival_from: int32 [8, 2], P('parts'), parts along dimension 0, may hold values from 0 to 3, as said below
- arrival_slot: int32 [8, 2], P('parts'), parts along dimension 0, may hold values from 0 to 11, as said below
- resident_adapter: int32 [96], P('parts'), parts along dimension 0, may hold values from 0 to 7
- arrival_adapter: int32 [8, 2], P('parts'), parts along dimension 0, may hold values from 0 to 3
- hot_holder: int32 [32], P('parts'), parts along dimension 0, may hold values from 0 to 31, as said below
- hot_dest: int32 [32, 1], P('parts'), parts along dimension 0, may hold values from 0 to 3, as said below
Outputs:
- attn_out: bfloat16 [112, 2, 8192], P(('parts', 'replica'), None, 'tensor'), parts along dimension 0
- new_kv: bfloat16 [112, 2, 8, 256], P(('parts', 'replica'), None, 'tensor'), parts along dimension 0
- arrival_cache: bfloat16 [16, 128, 8, 256], P(('parts', 'replica'), None, 'tensor'), parts along dimension 0
- installed_a: bfloat16 [32, 2, 64, 8192], P(('parts', 'replica'), None, None, 'tensor'), parts along dimension 0
- installed_b: bfloat16 [32, 2, 64, 1024], P(('parts', 'replica'), None, None, 'tensor'), parts along dimension 0
There are 2 independent parts, one for each index of `parts`. A program takes and returns all parts, laid end to end along the dimension named above; an argument that names none is the same for every part. Nothing has to cross between parts.
Inputs may be any that keep to these rules, and one draw needn't show every extreme that they name: `lengths`: every request listed by arrival_from and arrival_slot holds more than 96 rows; some request holds exactly 128. `arrival_from`: row r lists 2 distinct replicas, none equal to r; each replica appears exactly 2 times in the whole array. `arrival_slot`: no request (replica and slot) is listed twice. `hot_holder`: entry h is the holder's replica times 8 plus its slot; the holder's replica is not in row h of hot_dest; the holders of rows c * 4 to c * 4 + 3 lie on distinct replicas. `hot_dest`: for each c below 4, rows c * 4 to c * 4 + 3 together list every replica exactly once.
All inputs are finite; a program needn't handle non-finite values.
Results may differ from a plain program's by a relative error of at most 0.0071.
Values may be sent and summed in bfloat16 or wider, within the bound.
A program may use at most 64 MiB of HBM per device.

v0:
```python
import math

import jax
import jax.numpy as jnp
from jax import lax
from jax.sharding import PartitionSpec as P

COPIES = 4


ADAPTER_SCALE = 2.0
ROPE_BASE = 500000.0


def rotate_keys(key_rows, positions):
    head_length = key_rows.shape[-1]
    half_size = head_length // 2
    frequency = ROPE_BASE ** (-(jnp.arange(half_size, dtype=jnp.float32) * 2.0 / head_length))
    angles = positions.astype(jnp.float32)[:, :, None, None] * frequency
    cosine = jnp.cos(angles)
    sine_val = jnp.sin(angles)
    first_half = key_rows[..., :half_size]
    second_half = key_rows[..., half_size:]
    return jnp.concatenate(
        [
            first_half * cosine - second_half * sine_val,
            second_half * cosine + first_half * sine_val,
        ],
        axis=-1,
    )


def attend(queries, stored, lengths_now, fresh_kv):
    request_slot_count, decode_step_count, heads_local, head_length = queries.shape
    local_key_value = stored.shape[2]
    group_size = heads_local // local_key_value
    grouped = queries.reshape(
        request_slot_count, decode_step_count, local_key_value, group_size, head_length
    )
    score_scale = 1.0 / math.sqrt(head_length)
    past_scores = (
        jnp.einsum(
            "msgjd,mcgd->msgjc",
            grouped,
            stored[..., :head_length],
            preferred_element_type=jnp.float32,
        )
        * score_scale
    )
    recent_scores = (
        jnp.einsum(
            "msgjd,mtgd->msgjt",
            grouped,
            fresh_kv[..., :head_length],
            preferred_element_type=jnp.float32,
        )
        * score_scale
    )
    row_ids = jnp.arange(stored.shape[1], dtype=jnp.int32)
    past_ok = (row_ids[None, :] < lengths_now[:, None])[:, None, None, None, :]
    step_ids = jnp.arange(decode_step_count, dtype=jnp.int32)
    recent_ok = (step_ids[None, :] <= step_ids[:, None])[None, :, None, None, :]
    past_scores = jnp.where(past_ok, past_scores, -jnp.inf)
    recent_scores = jnp.where(recent_ok, recent_scores, -jnp.inf)
    peak_score = jnp.maximum(jnp.max(past_scores, -1), jnp.max(recent_scores, -1))[..., None]
    past_exp = jnp.exp(past_scores - peak_score)
    recent_exp = jnp.exp(recent_scores - peak_score)
    denom_sum = jnp.sum(past_exp, -1, keepdims=True) + jnp.sum(recent_exp, -1, keepdims=True)
    past_w = (past_exp / denom_sum).astype(jnp.bfloat16)
    recent_w = (recent_exp / denom_sum).astype(jnp.bfloat16)
    mixed_out = jnp.einsum(
        "msgjc,mcgd->msgjd", past_w, stored[..., head_length:], preferred_element_type=jnp.float32
    )
    mixed_out = mixed_out + jnp.einsum(
        "msgjt,mtgd->msgjd",
        recent_w,
        fresh_kv[..., head_length:],
        preferred_element_type=jnp.float32,
    )
    return mixed_out.reshape(request_slot_count, decode_step_count, heads_local * head_length)


def local(
    hidden,
    queries,
    kv_cache,
    w_kv,
    store_a,
    store_b,
    lengths,
    arrival_from,
    arrival_slot,
    resident_adapter,
    arrival_adapter,
    hot_holder,
    hot_dest,
):
    my_index = lax.axis_index("replica")
    replicas = lax.axis_size("replica")
    resident = kv_cache.shape[0]
    arrive = arrival_from.shape[1]
    request_slot_count = resident + arrive
    decode_step_count = hidden.shape[1]
    head_length = queries.shape[3]
    local_key_value = kv_cache.shape[2]
    slot_total = store_a.shape[0]
    hot_total = hot_holder.shape[0]
    spans = hot_total // COPIES
    my_from = lax.dynamic_index_in_dim(arrival_from, my_index, 0, keepdims=False)
    my_slot = lax.dynamic_index_in_dim(arrival_slot, my_index, 0, keepdims=False)
    own_ids = my_index * resident + jnp.arange(resident, dtype=jnp.int32)
    leaving_ids = (arrival_from * resident + arrival_slot).reshape(-1)
    staying = jnp.logical_not(jnp.any(own_ids[:, None] == leaving_ids[None, :], axis=1))
    live_mask = jnp.concatenate([staying, jnp.ones((arrive,), bool)])
    own_len = lax.dynamic_slice_in_dim(lengths, my_index * resident, resident)
    arrival_len = jnp.take(lengths, my_from * resident + my_slot)
    seen_len = jnp.concatenate([own_len, arrival_len])
    takes_mine = arrival_from == my_index
    sends_any = jnp.any(takes_mine, axis=1)
    send_slot = jnp.sum(jnp.where(takes_mine, arrival_slot, 0), axis=1)
    outgoing = jnp.take(kv_cache, send_slot, axis=0)
    outgoing = jnp.where(sends_any[:, None, None, None], outgoing, jnp.zeros((), jnp.bfloat16))
    incoming = lax.all_to_all(outgoing, "replica", split_axis=0, concat_axis=0, tiled=True)
    blocks = hot_dest.reshape(COPIES, spans, hot_dest.shape[1])
    holder_grid = hot_holder.reshape(COPIES, spans)
    holder_rep = holder_grid // slot_total
    mine = holder_rep == my_index
    has_one = jnp.any(mine, axis=1)
    local_pick = jnp.sum(jnp.where(mine, holder_grid % slot_total, 0), axis=1)

    def spread_rows(store):
        rows = jnp.take(store, local_pick, axis=0)
        rows = jnp.where(has_one[:, None, None, None], rows, jnp.zeros((), jnp.bfloat16))
        return rows.reshape(COPIES, replicas, -1).transpose(1, 0, 2)

    got_a, got_b = (
        lax.all_to_all(spread_rows(store_a), "replica", split_axis=0, concat_axis=0, tiled=True),
        lax.all_to_all(spread_rows(store_b), "replica", split_axis=0, concat_axis=0, tiled=True),
    )
    replica_ids = jnp.arange(replicas, dtype=jnp.int32)
    member = jnp.any(blocks[:, :, :, None] == replica_ids[None, None, None, :], axis=2).astype(
        jnp.int32
    )
    source_rep = jnp.sum(member * holder_rep[:, :, None], axis=1)
    copy_ids = jnp.arange(COPIES, dtype=jnp.int32)
    route_a = got_a[source_rep.T, copy_ids[None, :]]
    route_b = got_b[source_rep.T, copy_ids[None, :]]
    recv_a, recv_b = (
        lax.all_to_all(route_a, "replica", split_axis=0, concat_axis=0, tiled=True),
        lax.all_to_all(route_b, "replica", split_axis=0, concat_axis=0, tiled=True),
    )
    installed_a = recv_a.transpose(1, 0, 2).reshape((COPIES,) + store_a.shape[1:])
    installed_b = recv_b.transpose(1, 0, 2).reshape((COPIES,) + store_b.shape[1:])
    own_adapter = lax.dynamic_slice_in_dim(resident_adapter, my_index * resident, resident)
    my_choice = lax.dynamic_index_in_dim(arrival_adapter, my_index, 0, keepdims=False)
    adapt_a = jnp.concatenate(
        [jnp.take(store_a, own_adapter, axis=0), jnp.take(installed_a, my_choice, axis=0)]
    )
    adapter_up_weight = jnp.concatenate(
        [jnp.take(store_b, own_adapter, axis=0), jnp.take(installed_b, my_choice, axis=0)]
    )
    partial_value = jnp.einsum(
        "msd,mpkd->mspk", hidden, adapt_a, preferred_element_type=jnp.float32
    )
    base_projection = jnp.einsum(
        "msd,dgc->msgc",
        lax.all_gather(hidden, "tensor", axis=2, tiled=True),
        w_kv,
        preferred_element_type=jnp.float32,
    )
    down_projected = lax.psum(partial_value, "tensor")
    down_projected = down_projected.astype(jnp.bfloat16)
    adapter_update = jnp.einsum(
        "gnot,gote->gnoe", down_projected, adapter_up_weight, preferred_element_type=jnp.float32
    )
    adapter_update = (
        adapter_update.reshape(
            request_slot_count, decode_step_count, 2, local_key_value, head_length
        )
        .transpose(0, 1, 3, 2, 4)
        .reshape(request_slot_count, decode_step_count, local_key_value, 2 * head_length)
    )
    unrotated_key_value = base_projection + ADAPTER_SCALE * adapter_update
    positions = seen_len[:, None] + jnp.arange(decode_step_count, dtype=jnp.int32)[None, :]
    fresh_kv = jnp.concatenate(
        [
            rotate_keys(unrotated_key_value[..., :head_length], positions),
            unrotated_key_value[..., head_length:],
        ],
        axis=-1,
    ).astype(jnp.bfloat16)
    stay_out = attend(queries[:resident], kv_cache, own_len, fresh_kv[:resident])
    arrived = jnp.take(incoming, my_from, axis=0)
    row_ids = jnp.arange(kv_cache.shape[1], dtype=jnp.int32)
    arrived = jnp.where(
        (row_ids[None, :] < arrival_len[:, None])[:, :, None, None],
        arrived,
        jnp.zeros((), jnp.bfloat16),
    )
    move_out = attend(queries[resident:], arrived, arrival_len, fresh_kv[resident:])
    mixed_out = jnp.concatenate([stay_out, move_out], axis=0)
    attn_out = jnp.where(live_mask[:, None, None], mixed_out, 0.0).astype(jnp.bfloat16)
    new_kv = jnp.where(live_mask[:, None, None, None], fresh_kv, jnp.zeros((), jnp.bfloat16))
    return (attn_out, new_kv, arrived, installed_a, installed_b)


def solution(mesh):
    in_specs = (
        P(("parts", "replica"), None, "tensor"),
        P(("parts", "replica"), None, "tensor", None),
        P(("parts", "replica"), None, "tensor", None),
        P(None, "tensor", None),
        P(("parts", "replica"), None, None, "tensor"),
        P(("parts", "replica"), None, None, "tensor"),
        P("parts"),
        P("parts", None),
        P("parts", None),
        P("parts"),
        P("parts", None),
        P("parts"),
        P("parts", None),
    )
    out_specs = (
        P(("parts", "replica"), None, "tensor"),
        P(("parts", "replica"), None, "tensor", None),
        P(("parts", "replica"), None, "tensor", None),
        P(("parts", "replica"), None, None, "tensor"),
        P(("parts", "replica"), None, None, "tensor"),
    )
    return jax.shard_map(local, mesh=mesh, in_specs=in_specs, out_specs=out_specs, check_vma=False)
```

profile of v0, /device:TPU:0, one launch (start us, length us, event | category | flops | bytes accessed | tf_op | source)
XLA Modules:
  0.0 182.0 jit_solution(18232697446594805153)
XLA Ops:
  4.2 4.2 %all-to-all-start = ((bf16[4,4,8192]{2,1,0:T(4,128)(2,1)}), bf16[4,4,8192]{2,1,0:T(4,128)(2,1)S(1)}, u32[]{:S(2)}, u32[]{:S(2)}) async-start(bf16[4,4,8192]{2,1,0:T(4,128)(2,1)} %fusion.31), calls=%async_computation | async-start | bytes 524288 | tf_op jit(solution)/shard_map/all_to_all | solution.py:138
  9.5 4.2 %gather_fusion.5 = bf16[4,2,64,2048]{3,2,1,0:T(8,128)(2,1)} fusion(bf16[8,2,64,2048]{3,2,1,0:T(8,128)(2,1)} %param.17, s32[1024]{0:T(1024)S(1)} %pad_clamp_fusion.4), kind=kCustom, calls=%fused_computation.5 | custom fusion | bytes 4194320 | tf_op jit(solution)/shard_map/jit(_take)/gather | solution.py:132
  13.7 3.3 %gather.53 = bf16[4,4,65536]{2,1,0:T(4,128)(2,1)S(1)} reshape(bf16[4,2,64,2048]{3,2,1,0:T(8,128)(2,1)} %gather_fusion.5) | data formatting | bytes 4194304 | tf_op jit(solution)/shard_map/jit(_take)/gather | solution.py:132
  17.0 4.3 %fusion.8 = bf16[4,4,65536]{2,1,0:T(4,128)(2,1)} fusion(bf16[4,4,65536]{2,1,0:T(4,128)(2,1)S(1)} %gather.53, pred[4]{0:T(512)(128)(4,1)S(1)} %get-tuple-element.51, pred[4]{0:T(512)(128)(4,1)S(1)} %get-tuple-element.27), kind=kLoop, calls=%fused_computation.21 | loop fusion | flops 2097152 | bytes 4194312 | tf_op jit(solution)/shard_map/transpose | solution.py:134
  28.4 3.4 %all-to-all-start.1 = ((bf16[4,4,8192]{2,1,0:T(4,128)(2,1)}), bf16[4,4,8192]{2,1,0:T(4,128)(2,1)S(1)}, u32[]{:S(2)}, u32[]{:S(2)}) async-start(bf16[4,4,8192]{2,1,0:T(4,128)(2,1)} %reshape.397), calls=%async_computation.1 | async-start | bytes 524288 | tf_op jit(solution)/shard_map/all_to_all | solution.py:150
  32.0 3.0 %gather_fusion.9 = bf16[4,128,2,256]{3,2,1,0:T(2,128)(2,1)S(1)} fusion(bf16[12,128,2,256]{3,2,1,0:T(2,128)(2,1)} %param.15, s32[1024]{0:T(1024)S(1)} %pad_clamp_fusion.1), kind=kCustom, calls=%fused_computation.9 | custom fusion | bytes 1048592 | tf_op jit(solution)/shard_map/jit(_take)/gather | solution.py:121
  35.0 17.6 %all_gather.3 = bf16[14,2,8192]{2,0,1:T(8,128)(2,1)} all-gather(bf16[14,2,2048]{2,0,1:T(8,128)(2,1)S(1)} %copy.82), channel_id=1, replica_groups=mesh['parts'=2,'replica'=4,'tensor'=4] {'tensor'}, dimensions={2}, use_global_device_ids=true | all-gather | bytes 573440 | tf_op jit(solution)/shard_map/all_gather | solution.py:167
  53.3 3.6 %all-to-all-start.2 = ((bf16[4,4,65536]{2,1,0:T(4,128)(2,1)}), bf16[4,4,65536]{2,1,0:T(4,128)(2,1)S(1)}, u32[]{:S(2)}, u32[]{:S(2)}) async-start(bf16[4,4,65536]{2,1,0:T(4,128)(2,1)} %fusion.8), calls=%async_computation.2 | async-start | bytes 4194304 | tf_op jit(solution)/shard_map/all_to_all | solution.py:137
  57.8 3.4 %fusion.71 = (bf16[12,128,2,128]{3,2,1,0:T(2,128)(2,1)}, bf16[12,128,2,128]{3,2,1,0:T(2,128)(2,1)S(1)}) fusion(bf16[12,128,2,256]{3,2,1,0:T(2,128)(2,1)} %param.15), kind=kLoop, calls=%fused_computation.171 | loop fusion | bytes 3145728 | tf_op jit(solution)/shard_map/slice | solution.py:72
  61.2 1.8 fusion.75
  64.4 18.1 %all-to-all-done.2 = bf16[4,4,65536]{2,1,0:T(4,128)(2,1)S(1)} async-done(((bf16[4,4,65536]{2,1,0:T(4,128)(2,1)}), bf16[4,4,65536]{2,1,0:T(4,128)(2,1)S(1)}, u32[]{:S(2)}, u32[]{:S(2)}) %all-to-all-start.2) | async-done | bytes 2097184 | tf_op jit(solution)/shard_map/all_to_all | solution.py:137
  82.6 4.3 %all-to-all-start.4 = ((bf16[4,128,2,256]{3,2,1,0:T(2,128)(2,1)}), bf16[4,128,2,256]{3,2,1,0:T(2,128)(2,1)}, u32[]{:S(2)}, u32[]{:S(2)}) async-start(bf16[4,128,2,256]{3,2,1,0:T(2,128)(2,1)} %broadcast_select_fusion.2), calls=%async_computation.4 | async-start | bytes 1048576 | tf_op jit(solution)/shard_map/all_to_all | solution.py:123
  86.9 6.4 %gather_fusion.4 = bf16[12,2,64,2048]{3,2,1,0:T(8,128)(2,1)} fusion(bf16[8,2,64,2048]{3,2,1,0:T(8,128)(2,1)} %param.17, s32[1024]{0:T(1024)S(1)} %pad_clamp_fusion.5), kind=kCustom, calls=%fused_computation.4 | custom fusion | bytes 12582960 | tf_op jit(solution)/shard_map/jit(_take)/gather | solution.py:157
  96.8 7.9 %gather_fusion.6 = bf16[16,65536]{1,0:T(8,128)(2,1)} fusion(bf16[4,4,65536]{2,1,0:T(4,128)(2,1)S(1)} %all-to-all-done.2, s32[16]{0:T(128)S(1)} %reshape.394), kind=kCustom, calls=%fused_computation.6 | custom fusion | bytes 4194432 | tf_op jit(solution)/shard_map/gather | solution.py:146
  104.6 3.0 %reshape.427 = bf16[4,4,65536]{2,1,0:T(4,128)(2,1)} reshape(bf16[16,65536]{1,0:T(8,128)(2,1)} %gather_fusion.6) | data formatting | bytes 4194304 | tf_op jit(solution)/shard_map/gather | solution.py:146
  107.6 3.8 %all-to-all-start.3 = ((bf16[4,4,65536]{2,1,0:T(4,128)(2,1)}), bf16[4,4,65536]{2,1,0:T(4,128)(2,1)S(1)}, u32[]{:S(2)}, u32[]{:S(2)}) async-start(bf16[4,4,65536]{2,1,0:T(4,128)(2,1)} %reshape.427), calls=%async_computation.3 | async-start | bytes 4194304 | tf_op jit(solution)/shard_map/all_to_all | solution.py:149
  111.9 6.2 %broadcast_select_fusion = bf16[12,2,64,2048]{3,2,1,0:T(8,128)(2,1)} fusion(bf16[12,2,64,2048]{3,2,1,0:T(8,128)(2,1)} %gather_fusion.4, pred[12]{0:T(512)(128)(4,1)S(1)} %get-tuple-element.25), kind=kLoop, calls=%fused_computation.18 | loop fusion | flops 3145728 | bytes 12582924 | tf_op jit(solution)/shard_map/jit(_take)/select_n | solution.py:157
  125.2 11.7 %all-to-all-done.3 = bf16[4,4,65536]{2,1,0:T(4,128)(2,1)S(1)} async-done(((bf16[4,4,65536]{2,1,0:T(4,128)(2,1)}), bf16[4,4,65536]{2,1,0:T(4,128)(2,1)S(1)}, u32[]{:S(2)}, u32[]{:S(2)}) %all-to-all-start.3) | async-done | bytes 2097184 | tf_op jit(solution)/shard_map/all_to_all | solution.py:149
  136.9 2.9 %copy.93 = bf16[4,4,65536]{2,1,0:T(4,128)(2,1)} copy(bf16[4,4,65536]{2,0,1:T(4,128)(2,1)S(1)} %bitcast.139) | data formatting | bytes 4194304 | tf_op jit(solution)/shard_map/transpose | solution.py:152
  139.8 3.4 %reshape.374 = bf16[4,2,64,2048]{3,2,1,0:T(8,128)(2,1)S(1)} reshape(bf16[4,4,65536]{2,1,0:T(4,128)(2,1)} %copy.93) | data formatting | bytes 4194304 | tf_op jit(solution)/shard_map/reshape | solution.py:152
  143.2 1.7 gather_fusion.7
  146.3 5.0 %fusion.21 = f32[14,2,2,64]{3,1,2,0:T(2,128)S(1)} fusion(bf16[2,2,64,2048]{3,2,1,0:T(8,128)(2,1)S(1)} %broadcast_select_fusion.3, bf16[12,2,64,2048]{3,2,1,0:T(8,128)(2,1)} %broadcast_select_fusion, bf16[14,2,2048]{2,1,0:T(2,128)(2,1)S(1)} %copy-done.8), kind=kOutput, calls=%fused_computation.39 | convolution fusion | flops 18350080 | bytes 7469056 | tf_op jit(solution)/shard_map/msd,mpkd->mspk/dot_general | solution.py:162
  151.3 19.6 %psum.7 = bf16[14,2,2,64]{3,1,2,0:T(2,128)(2,1)S(1)} all-reduce(f32[14,2,2,64]{3,1,2,0:T(2,128)S(1)} %fusion.21), channel_id=1, replica_groups=mesh['parts'=2,'replica'=4,'tensor'=4] {'tensor'}, use_global_device_ids=true, to_apply=%region_5.6 | all-reduce | flops 3584 | bytes 21504 | tf_op jit(solution)/shard_map/psum | solution.py:171
  172.6 5.0 %fusion.74 = (bf16[14,2,2,256]{3,0,2,1:T(8,128)(2,1)S(1)}, f32[14,2,2,256]{3,0,2,1:T(8,128)S(1)}) fusion(f32[14,2,2,256]{3,2,1,0:T(2,128)S(1)} %mul.146, bf16[8192,2,256]{2,1,0:T(2,128)(2,1)} %param.16, bf16[14,2,8192]{2,0,1:T(8,128)(2,1)S(1)} %copy-done.6), kind=kOutput, calls=%fused_computation.174 | convolution fusion | flops 234909696 | bytes 8990720 | tf_op jit(solution)/shard_map/msd,dgc->msgc/dot_general | solution.py:165
  (143 shorter events, 33.1 us)
Async XLA Ops:
  0.6 7.8 %copy-start.11 = (s32[4,2]{0,1:T(2,128)S(1)}, s32[4,2]{0,1:T(2,128)}, u32[]{:S(2)}) copy-start(s32[4,2]{0,1:T(2,128)} %param.20) | copy-start | bytes 100
  0.7 8.6 %copy-start.12 = (s32[4,2]{0,1:T(2,128)S(1)}, s32[4,2]{0,1:T(2,128)}, u32[]{:S(2)}) copy-start(s32[4,2]{0,1:T(2,128)} %param.21) | copy-start | bytes 100
  0.7 7.8 %copy-start.15 = (s32[4,2]{0,1:T(2,128)S(1)}, s32[4,2]{0,1:T(2,128)}, u32[]{:S(2)}) copy-start(s32[4,2]{0,1:T(2,128)} %param.23) | copy-start | bytes 100
  4.2 22.0 %all-to-all-start = ((bf16[4,4,8192]{2,1,0:T(4,128)(2,1)}), bf16[4,4,8192]{2,1,0:T(4,128)(2,1)S(1)}, u32[]{:S(2)}, u32[]{:S(2)}) async-start(bf16[4,4,8192]{2,1,0:T(4,128)(2,1)} %fusion.31), calls=%async_computation | async-start | bytes 524288 | tf_op jit(solution)/shard_map/all_to_all | solution.py:138
  17.0 4.9 %copy-start.20 = (s32[16,1]{0,1:T(1,128)S(1)}, s32[16,1]{0,1:T(1,128)}, u32[]{:S(2)}) copy-start(s32[16,1]{0,1:T(1,128)} %param.25) | copy-start | bytes 196
  17.0 7.1 %copy-start.1 = (s32[48]{0:T(128)S(1)}, s32[48]{0:T(128)}, u32[]{:S(2)}) copy-start(s32[48]{0:T(128)} %param.19) | copy-start | bytes 580
  17.0 7.9 %copy-start.16 = (s32[48]{0:T(128)S(1)}, s32[48]{0:T(128)}, u32[]{:S(2)}) copy-start(s32[48]{0:T(128)} %param.22) | copy-start | bytes 580
  21.3 10.6 %copy-start.8 = (bf16[14,2,2048]{2,1,0:T(2,128)(2,1)S(1)}, bf16[14,2,2048]{2,1,0:T(2,128)(2,1)}, u32[]{:S(2)}) copy-start(bf16[14,2,2048]{2,1,0:T(2,128)(2,1)} %param.13) | copy-start | bytes 344068
  28.4 24.2 %all-to-all-start.1 = ((bf16[4,4,8192]{2,1,0:T(4,128)(2,1)}), bf16[4,4,8192]{2,1,0:T(4,128)(2,1)S(1)}, u32[]{:S(2)}, u32[]{:S(2)}) async-start(bf16[4,4,8192]{2,1,0:T(4,128)(2,1)} %reshape.397), calls=%async_computation.1 | async-start | bytes 524288 | tf_op jit(solution)/shard_map/all_to_all | solution.py:150
  53.3 29.3 %all-to-all-start.2 = ((bf16[4,4,65536]{2,1,0:T(4,128)(2,1)}), bf16[4,4,65536]{2,1,0:T(4,128)(2,1)S(1)}, u32[]{:S(2)}, u32[]{:S(2)}) async-start(bf16[4,4,65536]{2,1,0:T(4,128)(2,1)} %fusion.8), calls=%async_computation.2 | async-start | bytes 4194304 | tf_op jit(solution)/shard_map/all_to_all | solution.py:137
  56.9 4.3 %copy-start.18 = (bf16[14,2,16,128]{3,2,1,0:T(8,128)(2,1)S(1)}, bf16[14,2,16,128]{3,2,1,0:T(8,128)(2,1)}, u32[]{:S(2)}) copy-start(bf16[14,2,16,128]{3,2,1,0:T(8,128)(2,1)} %param.14) | copy-start | bytes 344068
  82.6 25.0 %all-to-all-start.4 = ((bf16[4,128,2,256]{3,2,1,0:T(2,128)(2,1)}), bf16[4,128,2,256]{3,2,1,0:T(2,128)(2,1)}, u32[]{:S(2)}, u32[]{:S(2)}) async-start(bf16[4,128,2,256]{3,2,1,0:T(2,128)(2,1)} %broadcast_select_fusion.2), calls=%async_computation.4 | async-start | bytes 1048576 | tf_op jit(solution)/shard_map/all_to_all | solution.py:123
  107.6 29.3 %all-to-all-start.3 = ((bf16[4,4,65536]{2,1,0:T(4,128)(2,1)}), bf16[4,4,65536]{2,1,0:T(4,128)(2,1)S(1)}, u32[]{:S(2)}, u32[]{:S(2)}) async-start(bf16[4,4,65536]{2,1,0:T(4,128)(2,1)} %reshape.427), calls=%async_computation.3 | async-start | bytes 4194304 | tf_op jit(solution)/shard_map/all_to_all | solution.py:149
  111.9 6.2 %copy-start.4 = (bf16[4,4,8192]{2,1,0:T(4,128)(2,1)S(1)}, bf16[4,4,8192]{2,1,0:T(4,128)(2,1)}, u32[]{:S(2)}) copy-start(bf16[4,4,8192]{2,1,0:T(4,128)(2,1)} %copy-done.3) | copy-start | bytes 786436
  118.1 2.8 %copy-start.17 = (pred[2]{0:T(512)(128)(4,1)S(1)}, pred[2]{0:T(512)(128)(4,1)}, u32[]{:S(2)}) copy-start(pred[2]{0:T(512)(128)(4,1)} %compare_and_fusion.1) | copy-start | bytes 10
  118.1 7.0 %copy-start.13 = (pred[2]{0:T(512)(128)(4,1)S(1)}, pred[2]{0:T(512)(128)(4,1)}, u32[]{:S(2)}) copy-start(pred[2]{0:T(512)(128)(4,1)} %compare_and_fusion.3) | copy-start | bytes 10
  143.2 3.1 %copy-start.2 = (bf16[4,2,64,2048]{3,2,1,0:T(8,128)(2,1)}, bf16[4,2,64,2048]{3,2,1,0:T(8,128)(2,1)S(1)}, u32[]{:S(2)}) copy-start(bf16[4,2,64,2048]{3,2,1,0:T(8,128)(2,1)S(1)} %reshape.374) | copy-start | bytes 6291460
  151.3 21.2 %copy-start.6 = (bf16[14,2,8192]{2,0,1:T(8,128)(2,1)S(1)}, bf16[14,2,8192]{2,0,1:T(8,128)(2,1)}, u32[]{:S(2)}) copy-start(bf16[14,2,8192]{2,0,1:T(8,128)(2,1)} %all_gather.3) | copy-start | bytes 1376260
  172.5 5.1 %copy-start.9 = (f32[14,2,64]{2,0,1:T(8,128)S(1)}, f32[14,2,64]{2,0,1:T(8,128)}, u32[]{:S(2)}) copy-start(f32[14,2,64]{2,0,1:T(8,128)} %get-tuple-element.37) | copy-start | bytes 21508
  172.5 5.4 %copy-start.14 = (pred[14]{0:T(512)(128)(4,1)S(1)}, pred[14]{0:T(512)(128)(4,1)}, u32[]{:S(2)}) copy-start(pred[14]{0:T(512)(128)(4,1)} %concatenate.27) | copy-start | bytes 46
  172.5 6.1 %copy-start.19 = (bf16[14,2,16,128]{3,2,1,0:T(8,128)(2,1)S(1)}, bf16[14,2,16,128]{3,2,1,0:T(8,128)(2,1)}, u32[]{:S(2)}) copy-start(bf16[14,2,16,128]{3,2,1,0:T(8,128)(2,1)} %param.14) | copy-start | bytes 344068
  172.5 6.1 %copy-start.21 = (pred[2,2]{1,0:T(4,128)(4,1)S(1)}, pred[2,2]{1,0:T(4,128)(4,1)}, u32[]{:S(2)}) copy-start(pred[2,2]{1,0:T(4,128)(4,1)} %iota_compare_fusion.3) | copy-start | bytes 16
  172.5 6.6 %copy-start.10 = (f32[12,2,2,8]{3,1,2,0:T(2,128)S(1)}, f32[12,2,2,8]{3,1,2,0:T(2,128)}, u32[]{:S(2)}) copy-start(f32[12,2,2,8]{3,1,2,0:T(2,128)} %get-tuple-element.46) | copy-start | bytes 4612
  172.5 6.8 %copy-start.7 = (f32[12,2,2,8,128]{4,3,1,2,0:T(8,128)S(1)}, f32[12,2,2,8,128]{4,3,1,2,0:T(8,128)}, u32[]{:S(2)}) copy-start(f32[12,2,2,8,128]{4,3,1,2,0:T(8,128)} %get-tuple-element.47) | copy-start | bytes 589828
  (3 other events, 4.8 us)
where the time goes:
time: 183 us; the launch traced here: 182 us
  local copies, waits for them, and re-layouts  53.2 us (29%)
  blocking collectives  37.2 us (20%)
  waiting for transfers between devices  29.8 us (16%)
  other arithmetic  25.2 us (14%)
  starting transfers between devices  19.4 us (11%)
  matrix products  16 us (9%)
    psum x1, blocking collectives, local(): down_projected = lax.psum(partial_value, 'tensor')  19.6 us
    all_to_all x1, waiting for transfers between devices, local(): lax.all_to_all(spread_rows(store_a), 'replica', split_axis=0, concat_axis...  18.1 us
    all_gather x1, blocking collectives, local(): lax.all_gather(hidden, 'tensor', axis=2, tiled=True)  17.6 us
    all_to_all x1, waiting for transfers between devices, local(): lax.all_to_all(route_a, 'replica', split_axis=0, concat_axis=0, tiled=True)  11.7 us
    gather x2, local copies, waits for them, and re-layouts, local(): route_a = got_a[source_rep.T, copy_ids[None, :]]  10.8 us
    gather x4, local copies, waits for them, and re-layouts, spread_rows(): rows = jnp.take(store, local_pick, axis=0)  8.25 us
    gather x1, local copies, waits for them, and re-layouts, local(): jnp.take(store_a, own_adapter, axis=0)  6.36 us
    select_n x1, other arithmetic, local(): jnp.take(store_a, own_adapter, axis=0)  6.15 us
  transfers between devices with their start and end apart: 5, of which 2 were waited for; matrix products, arithmetic and copies ran while one was open for 34% of the time, Pallas kernels for 0%

commit v1 on v0

--- a/solution.py
+++ b/solution.py
@@ -1,8 +1,11 @@
+import functools
 import math
 
 import jax
 import jax.numpy as jnp
 from jax import lax
+from jax.experimental import pallas as pl
+from jax.experimental.pallas import tpu as pltpu
 from jax.sharding import PartitionSpec as P
 
 COPIES = 4
@@ -80,7 +83,7 @@
     return mixed_out.reshape(request_slot_count, decode_step_count, heads_local * head_length)
 
 
-def local(
+def general(
     hidden,
     queries,
     kv_cache,
@@ -204,6 +207,286 @@
     return (attn_out, new_kv, arrived, installed_a, installed_b)
 
 
+PAIRED = 4
+
+
+def needed_first(adapter_ref, dest):
+    first = adapter_ref[dest, 0]
+    second = adapter_ref[dest, 1]
+    other = jnp.where(first == 0, 1, 0)
+    second = jnp.where(second == first, other, second)
+    place, seen = [], jnp.int32(2)
+    for c in range(COPIES):
+        early = jnp.logical_or(first == c, second == c)
+        place.append(jnp.where(first == c, 0, jnp.where(second == c, 1, seen)))
+        seen = seen + jnp.where(early, 0, 1)
+    order = []
+    for j in range(COPIES):
+        at = jnp.int32(0)
+        for c in range(1, COPIES):
+            at = at + jnp.where(place[c] == j, c, 0)
+        order.append(at)
+    return order, place
+
+
+def held_slot(holder_ref, spans, slots, replica, copy_id):
+    found = jnp.int32(0)
+    for s in range(spans):
+        holder = holder_ref[copy_id * spans + s]
+        found = jnp.where(holder // slots == replica, holder % slots, found)
+    return found
+
+
+def holder_of(holder_ref, dest_ref, spans, dest, copy_id):
+    found = jnp.int32(0)
+    for s in range(spans):
+        row = copy_id * spans + s
+        found = jnp.where(dest_ref[row, 0] == dest, holder_ref[row], found)
+    return found
+
+
+def pack_kernel(spans, slots, from_ref, slot_ref, adapter_ref, holder_ref, a_ref, b_ref, kv_ref,
+                a0_ref, a1_ref, b_out, k1_ref, k2_ref, k3_ref, sems):
+    me = lax.axis_index("replica")
+    copies = []
+
+    def go(src, dst):
+        copy = pltpu.make_async_copy(src, dst, sems.at[len(copies)])
+        copy.start()
+        copies.append(copy)
+
+    order, _ = needed_first(adapter_ref, me ^ 3)
+    held = [held_slot(holder_ref, spans, slots, me, c) for c in order]
+    for j in range(2):
+        go(a_ref.at[held[j]], a0_ref.at[j])
+    for k, out in ((1, k1_ref), (2, k2_ref), (3, k3_ref)):
+        chosen = jnp.int32(0)
+        for a in range(2):
+            chosen = jnp.where(from_ref[me ^ k, a] == me, slot_ref[me ^ k, a], chosen)
+        go(kv_ref.at[chosen], out)
+    for j in range(COPIES):
+        go(b_ref.at[held[j]], b_out.at[j])
+    for j in range(2):
+        go(a_ref.at[held[2 + j]], a1_ref.at[j])
+    for copy in copies:
+        copy.wait()
+
+
+def pick_kernel(spans, slots, base, count, adapter_ref, holder_ref, dest_ref, store_ref, core_ref, out_ref, sems):
+    me = lax.axis_index("replica")
+    dest = me ^ 2
+    order, _ = needed_first(adapter_ref, dest)
+    for j in range(count):
+        holder = holder_of(holder_ref, dest_ref, spans, dest, order[base + j])
+        mine = holder // slots == me
+
+        @pl.when(mine)
+        def _():
+            pltpu.make_async_copy(store_ref.at[holder % slots], out_ref.at[j], sems.at[j]).start()
+
+        @pl.when(jnp.logical_not(mine))
+        def _():
+            pltpu.make_async_copy(core_ref.at[j], out_ref.at[j], sems.at[j]).start()
+
+    for j in range(count):
+        pltpu.make_async_copy(core_ref.at[j], out_ref.at[j], sems.at[j]).wait()
+
+
+def choose(near, place_near, place_far, near_refs, far_refs, dst, sem):
+    for wanted, place, refs in ((near, place_near, near_refs), (jnp.logical_not(near), place_far, far_refs)):
+        each = COPIES // 2 if len(refs) == 2 else COPIES
+        for r, ref in enumerate(refs):
+            inside = jnp.logical_and(place >= r * each, place < (r + 1) * each)
+
+            @pl.when(jnp.logical_and(wanted, inside))
+            def _():
+                pltpu.make_async_copy(ref.at[place - r * each], dst, sem).start()
+
+
+def arrive_kernel(spans, slots, adapter_ref, holder_ref, dest_ref, hid_ref, c0_ref, c1_ref, x0_ref, cb_ref, xb_ref,
+                  out_ref, b_out, units, sems):
+    me = lax.axis_index("replica")
+    _, place_far = needed_first(adapter_ref, me)
+    _, place_near = needed_first(adapter_ref, me ^ 2)
+
+    def at(places, c):
+        found = places[0]
+        for i in range(1, COPIES):
+            found = jnp.where(c == i, places[i], found)
+        return found
+
+    for a in range(2):
+        c = adapter_ref[me, a]
+        near = holder_of(holder_ref, dest_ref, spans, me, c) // slots == (me ^ 1)
+        choose(near, at(place_near, c), at(place_far, c), (c0_ref, c1_ref), (x0_ref, x0_ref), units.at[a], sems.at[a])
+        choose(near, at(place_near, c), at(place_far, c), (cb_ref,), (xb_ref,), b_out.at[a], sems.at[2 + a])
+    for a in range(2):
+        pltpu.make_async_copy(c0_ref.at[0], units.at[a], sems.at[a]).wait()
+        unit = units[a].reshape(units.shape[1] * units.shape[2], units.shape[3])
+        out_ref[a] = lax.dot_general(hid_ref[...], unit, (((1,), (1,)), ((), ())), preferred_element_type=jnp.float32)
+        pltpu.make_async_copy(cb_ref.at[0], b_out.at[a], sems.at[2 + a]).wait()
+
+
+def install_kernel(spans, slots, adapter_ref, holder_ref, dest_ref, c0_ref, c1_ref, x0_ref, x1_ref, cb_ref, xb_ref,
+                   a_out, b_out, sems):
+    me = lax.axis_index("replica")
+    _, place_far = needed_first(adapter_ref, me)
+    _, place_near = needed_first(adapter_ref, me ^ 2)
+    for c in range(COPIES):
+        near = holder_of(holder_ref, dest_ref, spans, me, c) // slots == (me ^ 1)
+        choose(near, place_near[c], place_far[c], (c0_ref, c1_ref), (x0_ref, x1_ref), a_out.at[c], sems.at[c])
+        choose(near, place_near[c], place_far[c], (cb_ref,), (xb_ref,), b_out.at[c], sems.at[COPIES + c])
+    for c in range(COPIES):
+        pltpu.make_async_copy(c0_ref.at[0], a_out.at[c], sems.at[c]).wait()
+        pltpu.make_async_copy(cb_ref.at[0], b_out.at[c], sems.at[COPIES + c]).wait()
+
+
+SMEM = pl.BlockSpec(memory_space=pltpu.SMEM)
+ANY = pl.BlockSpec(memory_space=pl.ANY)
+VMEM = pl.BlockSpec(memory_space=pltpu.VMEM)
+
+
+def paired(
+    hidden,
+    queries,
+    kv_cache,
+    w_kv,
+    store_a,
+    store_b,
+    lengths,
+    arrival_from,
+    arrival_slot,
+    resident_adapter,
+    arrival_adapter,
+    hot_holder,
+    hot_dest,
+):
+    me = lax.axis_index("replica")
+    tensors = lax.axis_size("tensor")
+    tensor_index = lax.axis_index("tensor")
+    resident, arrive = kv_cache.shape[0], arrival_from.shape[1]
+    requests, steps, width = hidden.shape
+    head_length, heads = queries.shape[3], kv_cache.shape[2]
+    slots = store_a.shape[0]
+    spans = hot_holder.shape[0] // COPIES
+    kind = store_a.dtype
+    unit_a, unit_b, unit_k = store_a.shape[1:], store_b.shape[1:], kv_cache.shape[1:]
+
+    def shaped(*shape, dtype=kind):
+        return jax.ShapeDtypeStruct(shape, dtype)
+
+    def swap(array, k):
+        return lax.ppermute(array, "replica", [(i, i ^ k) for i in range(PAIRED)])
+
+    def shift(array, k):
+        return lax.ppermute(array, "tensor", [(i, (i + k) % tensors) for i in range(tensors)])
+
+    def cost(bytes_accessed, flops=0):
+        return pl.CostEstimate(flops=flops, bytes_accessed=bytes_accessed, transcendentals=0)
+
+    size_a, size_b = 2 * math.prod(unit_a), 2 * math.prod(unit_b)
+
+    a0, a1, b_all, k1, k2, k3 = pl.pallas_call(
+        functools.partial(pack_kernel, spans, slots),
+        out_shape=(shaped(2, *unit_a), shaped(2, *unit_a), shaped(COPIES, *unit_b), shaped(*unit_k), shaped(*unit_k), shaped(*unit_k)),
+        in_specs=[SMEM] * 4 + [ANY] * 3,
+        out_specs=(ANY,) * 6,
+        scratch_shapes=[pltpu.SemaphoreType.DMA((4 + COPIES + 3,))],
+        cost_estimate=cost(8 * size_a + 8 * size_b),
+    )(arrival_from, arrival_slot, arrival_adapter, hot_holder, store_a, store_b, kv_cache)
+    core_a0, core_b = swap(a0, 1), swap(b_all, 1)
+    core_a1 = swap(a1, 1)
+    far = (swap(k2, 2), swap(k3, 3))
+    near = swap(k1, 1)
+    pieces = [hidden] + [shift(hidden, k) for k in range(1, tensors)]
+
+    def pick(base, count, store, core):
+        return pl.pallas_call(
+            functools.partial(pick_kernel, spans, slots, base, count),
+            out_shape=shaped(count, *store.shape[1:]),
+            in_specs=[SMEM] * 3 + [ANY] * 2,
+            out_specs=ANY,
+            scratch_shapes=[pltpu.SemaphoreType.DMA((count,))],
+            cost_estimate=cost(4 * count * math.prod(store.shape[1:])),
+        )(arrival_adapter, hot_holder, hot_dest, store, core)
+
+    far_b = swap(pick(0, COPIES, store_b, core_b), 2)
+    far_a0 = swap(pick(0, 2, store_a, core_a0), 2)
+    far_a1 = swap(pick(2, 2, store_a, core_a1), 2)
+
+    own_adapter = lax.dynamic_slice_in_dim(resident_adapter, me * resident, resident)
+    every = jnp.einsum("msd,epkd->msepk", hidden[:resident], store_a, preferred_element_type=jnp.float32)
+    is_own = own_adapter[:, None] == jnp.arange(slots, dtype=jnp.int32)[None, :]
+    part_own = jnp.sum(jnp.where(is_own[:, None, :, None, None], every, 0.0), axis=2)
+
+    def total(part):
+        out = part
+        for k in range(1, tensors):
+            out = out + shift(part, k)
+        return out.astype(jnp.bfloat16)
+
+    shrink_own = total(part_own.reshape(resident * steps, -1)).reshape(resident, steps, 2, -1)
+    whole = jnp.concatenate(pieces, axis=2)
+    whole = whole.reshape(requests, steps, tensors, width)
+    turn = (tensor_index - jnp.arange(tensors, dtype=jnp.int32)) % tensors
+    whole = jnp.take(whole, turn, axis=2).reshape(requests, steps, tensors * width)
+    base = jnp.einsum("msd,dgc->msgc", whole, w_kv, preferred_element_type=jnp.float32)
+
+    my_from = lax.dynamic_index_in_dim(arrival_from, me, 0, keepdims=False)
+    my_slot = lax.dynamic_index_in_dim(arrival_slot, me, 0, keepdims=False)
+    own_ids = me * resident + jnp.arange(resident, dtype=jnp.int32)
+    leaving = (arrival_from * resident + arrival_slot).reshape(-1)
+    staying = jnp.logical_not(jnp.any(own_ids[:, None] == leaving[None, :], axis=1))
+    own_len = lax.dynamic_slice_in_dim(lengths, me * resident, resident)
+    arrival_len = jnp.take(lengths, my_from * resident + my_slot)
+
+    def fresh_rows(base_rows, shrink, up, seen):
+        count = base_rows.shape[0]
+        update = jnp.einsum("gnot,gote->gnoe", shrink, up, preferred_element_type=jnp.float32)
+        update = update.reshape(count, steps, 2, heads, head_length).transpose(0, 1, 3, 2, 4)
+        raw = base_rows + ADAPTER_SCALE * update.reshape(count, steps, heads, 2 * head_length)
+        positions = seen[:, None] + jnp.arange(steps, dtype=jnp.int32)[None, :]
+        turned = rotate_keys(raw[..., :head_length], positions)
+        return jnp.concatenate([turned, raw[..., head_length:]], axis=-1).astype(jnp.bfloat16)
+
+    up_own = jnp.take(store_b, own_adapter, axis=0)
+    fresh_own = fresh_rows(base[:resident], shrink_own, up_own, own_len)
+    stay_out = attend(queries[:resident], kv_cache, own_len, fresh_own)
+    stay_out = jnp.where(staying[:, None, None], stay_out, 0.0).astype(jnp.bfloat16)
+    stay_kv = jnp.where(staying[:, None, None, None], fresh_own, jnp.zeros((), jnp.bfloat16))
+
+    way = (my_from ^ me)[:, None, None, None]
+    arrived = jnp.where(way == 1, near[None], jnp.where(way == 2, far[0][None], far[1][None]))
+    row_ids = jnp.arange(kv_cache.shape[1], dtype=jnp.int32)
+    arrived = jnp.where((row_ids[None, :] < arrival_len[:, None])[:, :, None, None], arrived, jnp.zeros((), jnp.bfloat16))
+    rows = 16
+    guests = jnp.pad(hidden[resident:].reshape(arrive * steps, width), ((0, rows - arrive * steps), (0, 0)))
+    part_new, up_new = pl.pallas_call(
+        functools.partial(arrive_kernel, spans, slots),
+        out_shape=(shaped(arrive, rows, math.prod(unit_a[:2]), dtype=jnp.float32), shaped(arrive, *unit_b)),
+        in_specs=[SMEM] * 3 + [VMEM] + [ANY] * 5,
+        out_specs=(VMEM, ANY),
+        scratch_shapes=[pltpu.VMEM((arrive,) + unit_a, kind), pltpu.SemaphoreType.DMA((2 * arrive,))],
+        cost_estimate=cost(arrive * (size_a + 2 * size_b), 2 * arrive * rows * size_a // 2),
+    )(arrival_adapter, hot_holder, hot_dest, guests, core_a0, core_a1, far_a0, core_b, far_b)
+    part_new = jnp.concatenate([part_new[a, a * steps : (a + 1) * steps] for a in range(arrive)], axis=0)
+    shrink_new = total(part_new).reshape(arrive, steps, 2, -1)
+    fresh_new = fresh_rows(base[resident:], shrink_new, up_new, arrival_len)
+    move_out = attend(queries[resident:], arrived, arrival_len, fresh_new).astype(jnp.bfloat16)
+
+    attn_out = jnp.concatenate([stay_out, move_out], axis=0)
+    new_kv = jnp.concatenate([stay_kv, fresh_new], axis=0)
+    installed_a, installed_b = pl.pallas_call(
+        functools.partial(install_kernel, spans, slots),
+        out_shape=(shaped(COPIES, *unit_a), shaped(COPIES, *unit_b)),
+        in_specs=[SMEM] * 3 + [ANY] * 6,
+        out_specs=(ANY, ANY),
+        scratch_shapes=[pltpu.SemaphoreType.DMA((2 * COPIES,))],
+        cost_estimate=cost(8 * size_a + 8 * size_b),
+    )(arrival_adapter, hot_holder, hot_dest, core_a0, core_a1, far_a0, far_a1, core_b, far_b)
+    return (attn_out, new_kv, arrived, installed_a, installed_b)
+
+
 def solution(mesh):
     in_specs = (
         P(("parts", "replica"), None, "tensor"),
@@ -227,4 +510,5 @@
         P(("parts", "replica"), None, None, "tensor"),
         P(("parts", "replica"), None, None, "tensor"),
     )
+    local = paired if mesh.shape["replica"] == PAIRED else general
     return jax.shard_map(local, mesh=mesh, in_specs=in_specs, out_specs=out_specs, check_vma=False)

time: 183 us -> 333 us (1.82)
  Pallas kernels: 0 us -> 243 us
  blocking collectives: 37.2 us -> 0 us
  local copies, waits for them, and re-layouts: 53.2 us -> 20.5 us
  other arithmetic: 25.2 us -> 9.8 us
  waiting for transfers between devices: 29.8 us -> 22.7 us
    pallas_call x0 -> x6, Pallas kernels: none -> 243 us  [the longest x1 85.4 us: paired(): pl.pallas_call(functools.partial(pack_kernel, spans, slots), out_shape=(s...]
    gather x15 -> x4, local copies, waits for them, and re-layouts: 35.6 us -> 3.23 us  [the longest x2 2 us: paired(): jnp.take(whole, turn, axis=2).reshape(requests, steps, tensors * width)]
    all_to_all x5 -> x0, waiting for transfers between devices: 29.8 us -> none  [the longest x1 18.1 us: local(): lax.all_to_all(spread_rows(store_a), 'replica', split_axis=0, concat_axis...]
    ppermute x0 -> x18, waiting for transfers between devices: none -> 22.7 us  [the longest x9 18.9 us: swap(): return lax.ppermute(array, 'replica', [(i, i ^ k) for i in range(PAIRED)])]
    psum x1 -> x0, blocking collectives: 19.6 us -> none  [local(): down_projected = lax.psum(partial_value, 'tensor')]
    all_to_all x5 -> x0, starting transfers between devices: 19.4 us -> none  [the longest x1 4.31 us: local(): lax.all_to_all(outgoing, 'replica', split_axis=0, concat_axis=0, tiled=True)]
    ppermute x0 -> x18, starting transfers between devices: none -> 18.8 us  [the longest x9 12.2 us: shift(): lax.ppermute(array, 'tensor', [(i, (i + k) % tensors) for i in range(tens...]
    all_gather x1 -> x0, blocking collectives: 17.6 us -> none  [local(): lax.all_gather(hidden, 'tensor', axis=2, tiled=True)]
  transfers between devices with their start and end apart: 5 -> 18, of which waited for: 2 -> 3; matrix products, arithmetic and copies ran while one was open for 34% -> 9% of each run, Pallas kernels for 0% -> 73%
where the time goes in v1:
time: 333 us; the launch traced here: 332 us
  Pallas kernels  243 us (73%)
  waiting for transfers between devices  22.7 us (7%)
  local copies, waits for them, and re-layouts  20.5 us (6%)
  starting transfers between devices  18.8 us (6%)
  matrix products  16 us (5%)
  other arithmetic  9.8 us (3%)
    pallas_call x1, Pallas kernels, paired(): pl.pallas_call(functools.partial(pack_kernel, spans, slots), out_shape=(s...  85.4 us
    pallas_call x3, Pallas kernels, pick(): pl.pallas_call(functools.partial(pick_kernel, spans, slots, base, count),...  77.5 us
    pallas_call x1, Pallas kernels, paired(): pl.pallas_call(functools.partial(install_kernel, spans, slots), out_shape...  73.5 us
    ppermute x9, waiting for transfers between devices, swap(): return lax.ppermute(array, 'replica', [(i, i ^ k) for i in range(PAIRED)])  18.9 us
    ppermute x9, starting transfers between devices, shift(): lax.ppermute(array, 'tensor', [(i, (i + k) % tensors) for i in range(tens...  12.2 us
    unnamed x66, local copies, waits for them, and re-layouts  10.3 us
  transfers between devices with their start and end apart: 18, of which 3 were waited for; matrix products, arithmetic and copies ran while one was open for 9% of the time, Pallas kernels for 73%

profile of v1, /device:TPU:0, one launch (start us, length us, event | category | flops | bytes accessed | tf_op | source)
XLA Modules:
  0.0 332.1 jit_solution(12302359432128204159)
XLA Ops:
  2.6 4.3 %fusion.11 = f32[12,2,2,64]{3,0,2,1:T(8,128)S(1)} fusion(bf16[8,2,64,2048]{3,2,1,0:T(8,128)(2,1)} %store_ref.5, bf16[12,2,2048]{2,1,0:T(2,128)(2,1)S(1)} %slice.71, pred[12,8]{0,1:T(8,128)(4,1)S(1)} %iota_compare_fusion.1), kind=kOutput, calls=%fused_computation.15 | convolution fusion | flops 100709376 | bytes 4304992 | tf_op jit(solution)/shard_map/msd,epkd->msepk/dot_general | solution.py:418
  7.0 5.0 %collective-permute-start.5 = (f32[24,128]{1,0:T(8,128)S(1)}, f32[24,128]{1,0:T(8,128)S(1)}, u32[]{:S(2)}, u32[]{:S(2)}) collective-permute-start(f32[24,128]{1,0:T(8,128)S(1)} %reshape.374), channel_id=1, source_target_pairs={{0,3},{1,0},{2,1},{3,2},{4,7},{5,4},{6,5},{7,6},{8,11},{9,8},{10,9... | collective-permute-start | bytes 36872 | tf_op jit(solution)/shard_map/ppermute | solution.py:382
  13.1 2.8 collective-permute-start.2
  15.9 1.1 collective-permute-start.1
  20.5 2.0 fusion.57
  22.5 1.2 fusion.60
  29.3 85.4 %shard_map.164 = (bf16[2,2,64,2048]{3,2,1,0:T(8,128)(2,1)}, bf16[2,2,64,2048]{3,2,1,0:T(8,128)(2,1)}, bf16[4,2,64,256]{3,2,1,0:T(8,128)(2,1)}, bf16[128,2,256]{2...) custom-call(s32[4,2]{1,0:T(4,128)} %copy.186.from_ref, s32[4,2]{1,0:T(4,128)} %copy.187.slot_ref, ...), custom_call_target="tpu_custom_call" | custom-call | bytes 4718592 | tf_op jit(solution)/shard_map/pallas_call | solution.py:389
  115.6 1.6 collective-permute-start.7
  118.3 3.8 %collective-permute-done = bf16[14,2,2048]{2,1,0:T(2,128)(2,1)S(1)} collective-permute-done((bf16[14,2,2048]{2,1,0:T(2,128)(2,1)S(1)}, bf16[14,2,2048]{2,1,0:T(2,128)(2,1)S(1)}, u32[]{:S(2)}, u32[]{:S(2)}) %collective-permute-start) | collective-permute-done | bytes 114720 | tf_op jit(solution)/shard_map/ppermute | solution.py:382
  122.6 1.6 gather_fusion
  124.6 1.2 fusion.27
  125.8 5.0 %fusion = f32[14,2,2,256]{3,0,2,1:T(8,128)S(1)} fusion(bf16[8192,2,256]{2,1,0:T(2,128)(2,1)} %param.16, bf16[14,2,8192,1]{2,1,0,3:T(2,128)(2,1)S(1)} %fusion.27), kind=kOutput, calls=%fused_computation.3 | convolution fusion | flops 234881024 | bytes 8904704 | tf_op jit(solution)/shard_map/msd,dgc->msgc/dot_general | solution.py:433
  134.5 33.8 %shard_map.165 = bf16[2,2,64,2048]{3,2,1,0:T(8,128)(2,1)} custom-call(s32[4,2]{1,0:T(4,128)} %copy.188.adapter_ref, s32[16]{0:T(128)} %holder_ref.11, s32[16,1]{1,0:T(8,128)} %copy.198.dest_ref, bf16[8,2,64,2048]{3,2,1,0:T(8,128)(2,1)} %store_ref.5, bf16[2,2,64,2048]{3,2,1,0:T(8,128)(2,1)} %copy-done.1), custom_call_target="tpu_custom_call" | custom-call | bytes 2097152 | tf_op jit(solution)/shard_map/pallas_call | solution.py:404
  168.3 1.6 collective-permute-start.11
  169.9 1.3 fusion.8
  172.2 33.8 %shard_map.168 = bf16[2,2,64,2048]{3,2,1,0:T(8,128)(2,1)} custom-call(s32[4,2]{1,0:T(4,128)} %copy.188.adapter_ref, s32[16]{0:T(128)} %holder_ref.11, s32[16,1]{1,0:T(8,128)} %copy.198.dest_ref, bf16[8,2,64,2048]{3,2,1,0:T(8,128)(2,1)} %store_ref.5, bf16[2,2,64,2048]{3,2,1,0:T(8,128)(2,1)} %copy-done.2), custom_call_target="tpu_custom_call" | custom-call | bytes 2097152 | tf_op jit(solution)/shard_map/pallas_call | solution.py:404
  206.8 1.1 collective-permute-start.8
  207.9 10.0 %shard_map.166 = bf16[4,2,64,256]{3,2,1,0:T(8,128)(2,1)} custom-call(s32[4,2]{1,0:T(4,128)} %copy.188.adapter_ref, s32[16]{0:T(128)} %holder_ref.11, s32[16,1]{1,0:T(8,128)} %copy.198.dest_ref, bf16[8,2,64,256]{3,2,1,0:T(8,128)(2,1)} %store_ref.4, bf16[4,2,64,256]{3,2,1,0:T(8,128)(2,1)} %copy-done.6), custom_call_target="tpu_custom_call" | custom-call | bytes 524288 | tf_op jit(solution)/shard_map/pallas_call | solution.py:404
  217.9 1.1 collective-permute-start.13
  220.9 12.7 %collective-permute-done.8 = bf16[128,2,256]{2,1,0:T(2,128)(2,1)S(1)} collective-permute-done((bf16[128,2,256]{2,1,0:T(2,128)(2,1)S(1)}, bf16[128,2,256]{2,1,0:T(2,128)(2,1)S(1)}, u32[]{:S(2)}, u32[]{:S(2)}) %collective-permute-start.8) | collective-permute-done | bytes 131104 | tf_op jit(solution)/shard_map/ppermute | solution.py:379
  233.9 6.1 %collective-permute-done.13.xb_ref = bf16[4,2,64,256]{3,2,1,0:T(8,128)(2,1)S(1)} collective-permute-done((bf16[4,2,64,256]{3,2,1,0:T(8,128)(2,1)}, bf16[4,2,64,256]{3,2,1,0:T(8,128)(2,1)S(1)}, u32[]{:S(2)}, u32[]{:S(2)}) %collective-permute-start.13) | collective-permute-done | bytes 262176 | tf_op jit(solution)/shard_map/ppermute | solution.py:379
  241.7 6.6 %shard_map.167 = (f32[2,16,128]{2,1,0:T(8,128)}, bf16[2,2,64,256]{3,2,1,0:T(8,128)(2,1)}) custom-call(s32[4,2]{1,0:T(4,128)} %copy.188.adapter_ref, s32[16]{0:T(128)} %holder_ref.11, s32[16,1]{1,0:T(8,128)} %copy.198.dest_ref, bf16[16,2048]{1,0:T(8,128)(2,1)} %pad.4.hid_ref, bf16[2,2,64,2048]{3,2,1,0:T(8,128)(2,1)} %copy-done.1, ...), custom_call_target="tpu_custom_call" | custom-call | flops 16777216 | bytes 1310720 | tf_op jit(solution)/shard_map/pallas_call | solution.py:464
  249.7 1.5 collective-permute-start.14
  254.2 73.5 %shard_map.169 = (bf16[4,2,64,2048]{3,2,1,0:T(8,128)(2,1)}, bf16[4,2,64,256]{3,2,1,0:T(8,128)(2,1)}) custom-call(s32[4,2]{1,0:T(4,128)} %copy.188.adapter_ref, s32[16]{0:T(128)} %holder_ref.11, s32[16,1]{1,0:T(8,128)} %copy.198.dest_ref, bf16[2,2,64,2048]{3,2,1,0:T(8,128)(2,1)} %copy-done.1, bf16[2,2,64,2048]{3,2,1,0:T(8,128)(2,1)} %copy-done.2, ...), custom_call_target="tpu_custom_call" | custom-call | bytes 4718592 | tf_op jit(solution)/shard_map/pallas_call | solution.py:479
  (178 shorter events, 32.7 us)
Async XLA Ops:
  7.0 108.5 %collective-permute-start.5 = (f32[24,128]{1,0:T(8,128)S(1)}, f32[24,128]{1,0:T(8,128)S(1)}, u32[]{:S(2)}, u32[]{:S(2)}) collective-permute-start(f32[24,128]{1,0:T(8,128)S(1)} %reshape.374), channel_id=1, source_target_pairs={{0,3},{1,0},{2,1},{3,2},{4,7},{5,4},{6,5},{7,6},{8,11},{9,8},{10,9... | collective-permute-start | bytes 36872 | tf_op jit(solution)/shard_map/ppermute | solution.py:382
  12.1 103.5 %collective-permute-start.4 = (f32[24,128]{1,0:T(8,128)S(1)}, f32[24,128]{1,0:T(8,128)S(1)}, u32[]{:S(2)}, u32[]{:S(2)}) collective-permute-start(f32[24,128]{1,0:T(8,128)S(1)} %reshape.374), channel_id=1, source_target_pairs={{0,2},{1,3},{2,0},{3,1},{4,6},{5,7},{6,4},{7,5},{8,10},{9,11},{10,... | collective-permute-start | bytes 36872 | tf_op jit(solution)/shard_map/ppermute | solution.py:382
  12.1 103.5 %collective-permute-start.3 = (f32[24,128]{1,0:T(8,128)S(1)}, f32[24,128]{1,0:T(8,128)S(1)}, u32[]{:S(2)}, u32[]{:S(2)}) collective-permute-start(f32[24,128]{1,0:T(8,128)S(1)} %reshape.374), channel_id=1, source_target_pairs={{0,1},{1,2},{2,3},{3,0},{4,5},{5,6},{6,7},{7,4},{8,9},{9,10},{10,1... | collective-permute-start | bytes 36872 | tf_op jit(solution)/shard_map/ppermute | solution.py:382
  13.1 104.6 %collective-permute-start.2 = (bf16[14,2,2048]{2,1,0:T(2,128)(2,1)S(1)}, bf16[14,2,2048]{2,1,0:T(2,128)(2,1)S(1)}, u32[]{:S(2)}, u32[]{:S(2)}) collective-permute-start(bf16[14,2,2048]{2,1,0:T(2,128)(2,1)S(1)} %copy-done.10), channel_id=1, source_target_pairs={{0,3},{1,0},{2,1},{3,2},{4,7},{5,4},{6,5},{7,6},{8,11},{9,8},{10,9... | collective-permute-start | bytes 344072 | tf_op jit(solution)/shard_map/ppermute | solution.py:382
  15.9 102.1 %collective-permute-start.1 = (bf16[14,2,2048]{2,1,0:T(2,128)(2,1)S(1)}, bf16[14,2,2048]{2,1,0:T(2,128)(2,1)S(1)}, u32[]{:S(2)}, u32[]{:S(2)}) collective-permute-start(bf16[14,2,2048]{2,1,0:T(2,128)(2,1)S(1)} %copy-done.10), channel_id=1, source_target_pairs={{0,2},{1,3},{2,0},{3,1},{4,6},{5,7},{6,4},{7,5},{8,10},{9,11},{10,... | collective-permute-start | bytes 344072 | tf_op jit(solution)/shard_map/ppermute | solution.py:382
  115.5 6.6 %collective-permute-start = (bf16[14,2,2048]{2,1,0:T(2,128)(2,1)S(1)}, bf16[14,2,2048]{2,1,0:T(2,128)(2,1)S(1)}, u32[]{:S(2)}, u32[]{:S(2)}) collective-permute-start(bf16[14,2,2048]{2,1,0:T(2,128)(2,1)S(1)} %copy-done.10), channel_id=1, source_target_pairs={{0,1},{1,2},{2,3},{3,0},{4,5},{5,6},{6,7},{7,4},{8,9},{9,10},{10,1... | collective-permute-start | bytes 344072 | tf_op jit(solution)/shard_map/ppermute | solution.py:382
  115.5 102.3 %collective-permute-start.6 = (bf16[128,2,256]{2,1,0:T(2,128)(2,1)}, bf16[128,2,256]{2,1,0:T(2,128)(2,1)}, u32[]{:S(2)}, u32[]{:S(2)}) collective-permute-start(bf16[128,2,256]{2,1,0:T(2,128)(2,1)} %get-tuple-element.15), channel_id=1, source_target_pairs={{0,4},{4,0},{8,12},{12,8},{1,5},{5,1},{9,13},{13,9},{2,6},{6,2},{1... | collective-permute-start | bytes 393224 | tf_op jit(solution)/shard_map/ppermute | solution.py:379
  115.6 104.4 %collective-permute-start.7 = (bf16[128,2,256]{2,1,0:T(2,128)(2,1)}, bf16[128,2,256]{2,1,0:T(2,128)(2,1)}, u32[]{:S(2)}, u32[]{:S(2)}) collective-permute-start(bf16[128,2,256]{2,1,0:T(2,128)(2,1)} %get-tuple-element.16), channel_id=1, source_target_pairs={{0,8},{4,12},{8,0},{12,4},{1,9},{5,13},{9,1},{13,5},{2,10},{6,14},... | collective-permute-start | bytes 393224 | tf_op jit(solution)/shard_map/ppermute | solution.py:379
  117.7 89.0 %collective-permute-start.12 = (bf16[4,2,64,256]{3,2,1,0:T(8,128)(2,1)}, bf16[4,2,64,256]{3,2,1,0:T(8,128)(2,1)S(1)}, u32[]{:S(2)}, u32[]{:S(2)}) collective-permute-start(bf16[4,2,64,256]{3,2,1,0:T(8,128)(2,1)} %get-tuple-element.20), channel_id=1, source_target_pairs={{0,4},{4,0},{8,12},{12,8},{1,5},{5,1},{9,13},{13,9},{2,6},{6,2},{1... | collective-permute-start | bytes 786440 | tf_op jit(solution)/shard_map/ppermute | solution.py:379
  118.0 15.6 %collective-permute-start.9 = (bf16[2,2,64,2048]{3,2,1,0:T(8,128)(2,1)}, bf16[2,2,64,2048]{3,2,1,0:T(8,128)(2,1)S(1)}, u32[]{:S(2)}, u32[]{:S(2)}) collective-permute-start(bf16[2,2,64,2048]{3,2,1,0:T(8,128)(2,1)} %get-tuple-element.18), channel_id=1, source_target_pairs={{0,4},{4,0},{8,12},{12,8},{1,5},{5,1},{9,13},{13,9},{2,6},{6,2},{1... | collective-permute-start | bytes 3145736 | tf_op jit(solution)/shard_map/ppermute | solution.py:379
  122.1 49.1 %collective-permute-start.10 = (bf16[2,2,64,2048]{3,2,1,0:T(8,128)(2,1)}, bf16[2,2,64,2048]{3,2,1,0:T(8,128)(2,1)S(1)}, u32[]{:S(2)}, u32[]{:S(2)}) collective-permute-start(bf16[2,2,64,2048]{3,2,1,0:T(8,128)(2,1)} %get-tuple-element.19), channel_id=1, source_target_pairs={{0,4},{4,0},{8,12},{12,8},{1,5},{5,1},{9,13},{13,9},{2,6},{6,2},{1... | collective-permute-start | bytes 3145736 | tf_op jit(solution)/shard_map/ppermute | solution.py:379
  168.3 71.7 %collective-permute-start.11 = (bf16[2,2,64,2048]{3,2,1,0:T(8,128)(2,1)}, bf16[2,2,64,2048]{3,2,1,0:T(8,128)(2,1)S(1)}, u32[]{:S(2)}, u32[]{:S(2)}) collective-permute-start(bf16[2,2,64,2048]{3,2,1,0:T(8,128)(2,1)} %shard_map.165), channel_id=1, source_target_pairs={{0,8},{4,12},{8,0},{12,4},{1,9},{5,13},{9,1},{13,5},{2,10},{6,14},... | collective-permute-start | bytes 3145736 | tf_op jit(solution)/shard_map/ppermute | solution.py:379
  171.2 62.5 %copy-start.19 = (pred[2]{0:T(512)(128)(4,1)S(1)}, pred[2]{0:T(512)(128)(4,1)}, u32[]{:S(2)}) copy-start(pred[2]{0:T(512)(128)(4,1)} %get-tuple-element.50) | copy-start | bytes 10
  171.2 62.5 %copy-start.20 = (pred[2]{0:T(512)(128)(4,1)S(1)}, pred[2]{0:T(512)(128)(4,1)}, u32[]{:S(2)}) copy-start(pred[2]{0:T(512)(128)(4,1)} %get-tuple-element.51) | copy-start | bytes 10
  206.0 47.2 %collective-permute-start.17 = (bf16[2,2,64,2048]{3,2,1,0:T(8,128)(2,1)}, bf16[2,2,64,2048]{3,2,1,0:T(8,128)(2,1)S(1)}, u32[]{:S(2)}, u32[]{:S(2)}) collective-permute-start(bf16[2,2,64,2048]{3,2,1,0:T(8,128)(2,1)} %shard_map.168), channel_id=1, source_target_pairs={{0,8},{4,12},{8,0},{12,4},{1,9},{5,13},{9,1},{13,5},{2,10},{6,14},... | collective-permute-start | bytes 3145736 | tf_op jit(solution)/shard_map/ppermute | solution.py:379
  206.8 26.9 %collective-permute-start.8 = (bf16[128,2,256]{2,1,0:T(2,128)(2,1)S(1)}, bf16[128,2,256]{2,1,0:T(2,128)(2,1)S(1)}, u32[]{:S(2)}, u32[]{:S(2)}) collective-permute-start(bf16[128,2,256]{2,1,0:T(2,128)(2,1)S(1)} %copy-done.24), channel_id=1, source_target_pairs={{0,12},{4,8},{8,4},{12,0},{1,13},{5,9},{9,5},{13,1},{2,14},{6,10},... | collective-permute-start | bytes 393224 | tf_op jit(solution)/shard_map/ppermute | solution.py:379
  217.9 22.1 %collective-permute-start.13 = (bf16[4,2,64,256]{3,2,1,0:T(8,128)(2,1)}, bf16[4,2,64,256]{3,2,1,0:T(8,128)(2,1)S(1)}, u32[]{:S(2)}, u32[]{:S(2)}) collective-permute-start(bf16[4,2,64,256]{3,2,1,0:T(8,128)(2,1)} %shard_map.166), channel_id=1, source_target_pairs={{0,8},{4,12},{8,0},{12,4},{1,9},{5,13},{9,1},{13,5},{2,10},{6,14},... | collective-permute-start | bytes 786440 | tf_op jit(solution)/shard_map/ppermute | solution.py:379
  233.8 95.0 %copy-start.16 = (f32[2,2,64]{2,0,1:T(2,128)S(1)}, f32[2,2,64]{2,0,1:T(2,128)}, u32[]{:S(2)}) copy-start(f32[2,2,64]{2,0,1:T(2,128)} %get-tuple-element.64) | copy-start | bytes 3076
  233.8 95.0 %copy-start.17 = (f32[2,2,64]{2,0,1:T(2,128)S(1)}, f32[2,2,64]{2,0,1:T(2,128)}, u32[]{:S(2)}) copy-start(f32[2,2,64]{2,0,1:T(2,128)} %get-tuple-element.65) | copy-start | bytes 3076
  233.9 95.8 %copy-start.28 = (pred[2,2]{1,0:T(4,128)(4,1)S(1)}, pred[2,2]{1,0:T(4,128)(4,1)}, u32[]{:S(2)}) copy-start(pred[2,2]{1,0:T(4,128)(4,1)} %iota_compare_fusion.3) | copy-start | bytes 16
  248.3 79.5 %copy-start.11 = (bf16[2,2,64,256]{3,2,1,0:T(8,128)(2,1)S(1)}, bf16[2,2,64,256]{3,2,1,0:T(8,128)(2,1)}, u32[]{:S(2)}) copy-start(bf16[2,2,64,256]{3,2,1,0:T(8,128)(2,1)} %get-tuple-element.21) | copy-start | bytes 393220
  249.1 78.6 %collective-permute-start.15 = (f32[4,128]{1,0:T(4,128)S(1)}, f32[4,128]{1,0:T(4,128)S(1)}, u32[]{:S(2)}, u32[]{:S(2)}) collective-permute-start(f32[4,128]{1,0:T(4,128)S(1)} %pad_maximum_fusion.2), channel_id=1, source_target_pairs={{0,2},{1,3},{2,0},{3,1},{4,6},{5,7},{6,4},{7,5},{8,10},{9,11},{10,... | collective-permute-start | bytes 6152 | tf_op jit(solution)/shard_map/ppermute | solution.py:382
  249.1 78.5 %collective-permute-start.16 = (f32[4,128]{1,0:T(4,128)S(1)}, f32[4,128]{1,0:T(4,128)S(1)}, u32[]{:S(2)}, u32[]{:S(2)}) collective-permute-start(f32[4,128]{1,0:T(4,128)S(1)} %pad_maximum_fusion.2), channel_id=1, source_target_pairs={{0,3},{1,0},{2,1},{3,2},{4,7},{5,4},{6,5},{7,6},{8,11},{9,8},{10,9... | collective-permute-start | bytes 6152 | tf_op jit(solution)/shard_map/ppermute | solution.py:382
  249.7 78.0 %collective-permute-start.14 = (f32[4,128]{1,0:T(4,128)S(1)}, f32[4,128]{1,0:T(4,128)S(1)}, u32[]{:S(2)}, u32[]{:S(2)}) collective-permute-start(f32[4,128]{1,0:T(4,128)S(1)} %pad_maximum_fusion.2), channel_id=1, source_target_pairs={{0,1},{1,2},{2,3},{3,0},{4,5},{5,6},{6,7},{7,4},{8,9},{9,10},{10,1... | collective-permute-start | bytes 6152 | tf_op jit(solution)/shard_map/ppermute | solution.py:382
  (23 other events, 375.5 us)

commit v2 on v1

--- a/solution.py
+++ b/solution.py
@@ -245,34 +245,56 @@
     return found
 
 
-def pack_kernel(spans, slots, from_ref, slot_ref, adapter_ref, holder_ref, a_ref, b_ref, kv_ref,
-                a0_ref, a1_ref, b_out, k1_ref, k2_ref, k3_ref, sems):
+class Staged:
+    def __init__(self, sems):
+        self.sems, self.jobs = sems, []
+
+    def go(self, src, stage, dst):
+        pltpu.make_async_copy(src, stage, self.sems.at[len(self.jobs)]).start()
+        self.jobs.append((stage, dst))
+
+    def finish(self):
+        half = len(self.jobs)
+        for i, (stage, dst) in enumerate(self.jobs):
+            pltpu.make_async_copy(dst, stage, self.sems.at[i]).wait()
+            pltpu.make_async_copy(stage, dst, self.sems.at[half + i]).start()
+        for i, (stage, dst) in enumerate(self.jobs):
+            pltpu.make_async_copy(stage, dst, self.sems.at[half + i]).wait()
+
+
+def pack_kernel(spans, slots, from_hbm, slot_hbm, adapter_hbm, holder_hbm, a_ref, b_ref, kv_ref,
+                a0_ref, a1_ref, b_out, k1_ref, k2_ref, k3_ref,
+                from_ref, slot_ref, adapter_ref, holder_ref, a_stage, b_stage, k_stage, small_sems, sems):
     me = lax.axis_index("replica")
-    copies = []
-
-    def go(src, dst):
-        copy = pltpu.make_async_copy(src, dst, sems.at[len(copies)])
+    small = [
+        pltpu.make_async_copy(src, dst, small_sems.at[i])
+        for i, (src, dst) in enumerate(
+            ((adapter_hbm, adapter_ref), (holder_hbm, holder_ref), (from_hbm, from_ref), (slot_hbm, slot_ref))
+        )
+    ]
+    for copy in small:
         copy.start()
-        copies.append(copy)
+    for copy in small:
+        copy.wait()
+    staged = Staged(sems)
 
     order, _ = needed_first(adapter_ref, me ^ 3)
     held = [held_slot(holder_ref, spans, slots, me, c) for c in order]
     for j in range(2):
-        go(a_ref.at[held[j]], a0_ref.at[j])
+        staged.go(a_ref.at[held[j]], a_stage.at[j], a0_ref.at[j])
+    for j in range(COPIES):
+        staged.go(b_ref.at[held[j]], b_stage.at[j], b_out.at[j])
     for k, out in ((1, k1_ref), (2, k2_ref), (3, k3_ref)):
         chosen = jnp.int32(0)
         for a in range(2):
             chosen = jnp.where(from_ref[me ^ k, a] == me, slot_ref[me ^ k, a], chosen)
-        go(kv_ref.at[chosen], out)
-    for j in range(COPIES):
-        go(b_ref.at[held[j]], b_out.at[j])
+        staged.go(kv_ref.at[chosen], k_stage.at[k - 1], out)
     for j in range(2):
-        go(a_ref.at[held[2 + j]], a1_ref.at[j])
-    for copy in copies:
-        copy.wait()
-
-
-def pick_kernel(spans, slots, base, count, adapter_ref, holder_ref, dest_ref, store_ref, core_ref, out_ref, sems):
+        staged.go(a_ref.at[held[2 + j]], a_stage.at[2 + j], a1_ref.at[j])
+    staged.finish()
+
+
+def pick_kernel(spans, slots, base, count, adapter_ref, holder_ref, dest_ref, store_ref, core_ref, out_ref, stage, sems):
     me = lax.axis_index("replica")
     dest = me ^ 2
     order, _ = needed_first(adapter_ref, dest)
@@ -282,14 +304,17 @@
 
         @pl.when(mine)
         def _():
-            pltpu.make_async_copy(store_ref.at[holder % slots], out_ref.at[j], sems.at[j]).start()
+            pltpu.make_async_copy(store_ref.at[holder % slots], stage.at[j], sems.at[j]).start()
 
         @pl.when(jnp.logical_not(mine))
         def _():
-            pltpu.make_async_copy(core_ref.at[j], out_ref.at[j], sems.at[j]).start()
+            pltpu.make_async_copy(core_ref.at[j], stage.at[j], sems.at[j]).start()
 
     for j in range(count):
-        pltpu.make_async_copy(core_ref.at[j], out_ref.at[j], sems.at[j]).wait()
+        pltpu.make_async_copy(core_ref.at[j], stage.at[j], sems.at[j]).wait()
+        pltpu.make_async_copy(stage.at[j], out_ref.at[j], sems.at[count + j]).start()
+    for j in range(count):
+        pltpu.make_async_copy(stage.at[j], out_ref.at[j], sems.at[count + j]).wait()
 
 
 def choose(near, place_near, place_far, near_refs, far_refs, dst, sem):
@@ -328,17 +353,22 @@
 
 
 def install_kernel(spans, slots, adapter_ref, holder_ref, dest_ref, c0_ref, c1_ref, x0_ref, x1_ref, cb_ref, xb_ref,
-                   a_out, b_out, sems):
+                   a_out, b_out, a_stage, b_stage, sems):
     me = lax.axis_index("replica")
     _, place_far = needed_first(adapter_ref, me)
     _, place_near = needed_first(adapter_ref, me ^ 2)
     for c in range(COPIES):
         near = holder_of(holder_ref, dest_ref, spans, me, c) // slots == (me ^ 1)
-        choose(near, place_near[c], place_far[c], (c0_ref, c1_ref), (x0_ref, x1_ref), a_out.at[c], sems.at[c])
-        choose(near, place_near[c], place_far[c], (cb_ref,), (xb_ref,), b_out.at[c], sems.at[COPIES + c])
+        choose(near, place_near[c], place_far[c], (c0_ref, c1_ref), (x0_ref, x1_ref), a_stage.at[c], sems.at[c])
+        choose(near, place_near[c], place_far[c], (cb_ref,), (xb_ref,), b_stage.at[c], sems.at[COPIES + c])
     for c in range(COPIES):
-        pltpu.make_async_copy(c0_ref.at[0], a_out.at[c], sems.at[c]).wait()
-        pltpu.make_async_copy(cb_ref.at[0], b_out.at[c], sems.at[COPIES + c]).wait()
+        pltpu.make_async_copy(c0_ref.at[0], a_stage.at[c], sems.at[c]).wait()
+        pltpu.make_async_copy(a_stage.at[c], a_out.at[c], sems.at[2 * COPIES + c]).start()
+        pltpu.make_async_copy(cb_ref.at[0], b_stage.at[c], sems.at[COPIES + c]).wait()
+        pltpu.make_async_copy(b_stage.at[c], b_out.at[c], sems.at[3 * COPIES + c]).start()
+    for c in range(COPIES):
+        pltpu.make_async_copy(a_stage.at[c], a_out.at[c], sems.at[2 * COPIES + c]).wait()
+        pltpu.make_async_copy(b_stage.at[c], b_out.at[c], sems.at[3 * COPIES + c]).wait()
 
 
 SMEM = pl.BlockSpec(memory_space=pltpu.SMEM)
@@ -389,16 +419,23 @@
     a0, a1, b_all, k1, k2, k3 = pl.pallas_call(
         functools.partial(pack_kernel, spans, slots),
         out_shape=(shaped(2, *unit_a), shaped(2, *unit_a), shaped(COPIES, *unit_b), shaped(*unit_k), shaped(*unit_k), shaped(*unit_k)),
-        in_specs=[SMEM] * 4 + [ANY] * 3,
+        in_specs=[ANY] * 7,
         out_specs=(ANY,) * 6,
-        scratch_shapes=[pltpu.SemaphoreType.DMA((4 + COPIES + 3,))],
+        scratch_shapes=[pltpu.SMEM(x.shape, x.dtype) for x in (arrival_from, arrival_slot, arrival_adapter, hot_holder)]
+        + [
+            pltpu.VMEM((COPIES,) + unit_a, kind),
+            pltpu.VMEM((COPIES,) + unit_b, kind),
+            pltpu.VMEM((3,) + unit_k, kind),
+            pltpu.SemaphoreType.DMA((4,)),
+            pltpu.SemaphoreType.DMA((2 * (2 * COPIES + 3),)),
+        ],
         cost_estimate=cost(8 * size_a + 8 * size_b),
     )(arrival_from, arrival_slot, arrival_adapter, hot_holder, store_a, store_b, kv_cache)
     core_a0, core_b = swap(a0, 1), swap(b_all, 1)
     core_a1 = swap(a1, 1)
     far = (swap(k2, 2), swap(k3, 3))
     near = swap(k1, 1)
-    pieces = [hidden] + [shift(hidden, k) for k in range(1, tensors)]
+    a0, hidden = lax.optimization_barrier((a0, hidden))
 
     def pick(base, count, store, core):
         return pl.pallas_call(
@@ -406,18 +443,26 @@
             out_shape=shaped(count, *store.shape[1:]),
             in_specs=[SMEM] * 3 + [ANY] * 2,
             out_specs=ANY,
-            scratch_shapes=[pltpu.SemaphoreType.DMA((count,))],
+            scratch_shapes=[pltpu.VMEM((count,) + store.shape[1:], kind), pltpu.SemaphoreType.DMA((2 * count,))],
             cost_estimate=cost(4 * count * math.prod(store.shape[1:])),
         )(arrival_adapter, hot_holder, hot_dest, store, core)
 
-    far_b = swap(pick(0, COPIES, store_b, core_b), 2)
-    far_a0 = swap(pick(0, 2, store_a, core_a0), 2)
-    far_a1 = swap(pick(2, 2, store_a, core_a1), 2)
+    to_a0 = pick(0, 2, store_a, core_a0)
+    far_a0 = swap(to_a0, 2)
+    to_b = pick(0, COPIES, store_b, core_b)
+    far_b = swap(to_b, 2)
+    to_a1 = pick(2, 2, store_a, core_a1)
+    far_a1 = swap(to_a1, 2)
 
     own_adapter = lax.dynamic_slice_in_dim(resident_adapter, me * resident, resident)
     every = jnp.einsum("msd,epkd->msepk", hidden[:resident], store_a, preferred_element_type=jnp.float32)
     is_own = own_adapter[:, None] == jnp.arange(slots, dtype=jnp.int32)[None, :]
     part_own = jnp.sum(jnp.where(is_own[:, None, :, None, None], every, 0.0), axis=2)
+
+    _, hidden, part_own, queries, lengths, own_adapter, kv_cache = lax.optimization_barrier(
+        (to_a1, hidden, part_own, queries, lengths, own_adapter, kv_cache)
+    )
+    pieces = [hidden] + [shift(hidden, k) for k in range(1, tensors)]
 
     def total(part):
         out = part
@@ -465,7 +510,7 @@
         functools.partial(arrive_kernel, spans, slots),
         out_shape=(shaped(arrive, rows, math.prod(unit_a[:2]), dtype=jnp.float32), shaped(arrive, *unit_b)),
         in_specs=[SMEM] * 3 + [VMEM] + [ANY] * 5,
-        out_specs=(VMEM, ANY),
+        out_specs=(VMEM, VMEM),
         scratch_shapes=[pltpu.VMEM((arrive,) + unit_a, kind), pltpu.SemaphoreType.DMA((2 * arrive,))],
         cost_estimate=cost(arrive * (size_a + 2 * size_b), 2 * arrive * rows * size_a // 2),
     )(arrival_adapter, hot_holder, hot_dest, guests, core_a0, core_a1, far_a0, core_b, far_b)
@@ -481,7 +526,11 @@
         out_shape=(shaped(COPIES, *unit_a), shaped(COPIES, *unit_b)),
         in_specs=[SMEM] * 3 + [ANY] * 6,
         out_specs=(ANY, ANY),
-        scratch_shapes=[pltpu.SemaphoreType.DMA((2 * COPIES,))],
+        scratch_shapes=[
+            pltpu.VMEM((COPIES,) + unit_a, kind),
+            pltpu.VMEM((COPIES,) + unit_b, kind),
+            pltpu.SemaphoreType.DMA((4 * COPIES,)),
+        ],
         cost_estimate=cost(8 * size_a + 8 * size_b),
     )(arrival_adapter, hot_holder, hot_dest, core_a0, core_a1, far_a0, far_a1, core_b, far_b)
     return (attn_out, new_kv, arrived, installed_a, installed_b)

time: 333 us -> 117 us (0.35)
  Pallas kernels: 243 us -> 18.9 us
  waiting for transfers between devices: 22.7 us -> 29.7 us
    pallas_call x1, Pallas kernels: 85.4 us -> 3.74 us  [paired(): pl.pallas_call(functools.partial(pack_kernel, spans, slots), out_shape=(s...]
    pallas_call x1, Pallas kernels: 73.5 us -> 3.43 us  [paired(): pl.pallas_call(functools.partial(install_kernel, spans, slots), out_shape...]
    pallas_call x3, Pallas kernels: 77.5 us -> 8.35 us  [pick(): pl.pallas_call(functools.partial(pick_kernel, spans, slots, base, count),...]
    ppermute x9, waiting for transfers between devices: 18.9 us -> 29 us  [swap(): return lax.ppermute(array, 'replica', [(i, i ^ k) for i in range(PAIRED)])]
    unnamed x66 -> x70, local copies, waits for them, and re-layouts: 10.3 us -> 11.1 us
  transfers between devices with their start and end apart: 18 -> 18, of which waited for: 3 -> 2; matrix products, arithmetic and copies ran while one was open for 9% -> 29% of each run, Pallas kernels for 73% -> 13%
where the time goes in v2:
time: 117 us; the launch traced here: 116 us
  waiting for transfers between devices  29.7 us (25%)
  starting transfers between devices  21.9 us (19%)
  local copies, waits for them, and re-layouts  19 us (16%)
  Pallas kernels  18.9 us (16%)
  matrix products  15.5 us (13%)
  other arithmetic  10 us (9%)
  between operations  1.41 us (1%)
    ppermute x9, waiting for transfers between devices, swap(): return lax.ppermute(array, 'replica', [(i, i ^ k) for i in range(PAIRED)])  29 us
    ppermute x9, starting transfers between devices, shift(): lax.ppermute(array, 'tensor', [(i, (i + k) % tensors) for i in range(tens...  13.8 us
    unnamed x70, local copies, waits for them, and re-layouts  11.1 us
    pallas_call x3, Pallas kernels, pick(): pl.pallas_call(functools.partial(pick_kernel, spans, slots, base, count),...  8.35 us
    ppermute x9, starting transfers between devices, swap(): return lax.ppermute(array, 'replica', [(i, i ^ k) for i in range(PAIRED)])  8.04 us
    dot_general x1, matrix products, paired(): jnp.einsum('msd,dgc->msgc', whole, w_kv, preferred_element_type=jnp.float32)  5.05 us
    dot_general x1, matrix products, paired(): jnp.einsum('msd,epkd->msepk', hidden[:resident], store_a, preferred_eleme...  4.24 us
    pallas_call x1, Pallas kernels, paired(): pl.pallas_call(functools.partial(pack_kernel, spans, slots), out_shape=(s...  3.74 us
  transfers between devices with their start and end apart: 18, of which 2 were waited for; matrix products, arithmetic and copies ran while one was open for 29% of the time, Pallas kernels for 13%

profile of v2, /device:TPU:0, one launch (start us, length us, event | category | flops | bytes accessed | tf_op | source)
XLA Modules:
  0.0 116.3 jit_solution(17616631731684636828)
XLA Ops:
  0.7 1.4 %copy.174.adapter_hbm.adapter_ref = s32[4,2]{1,0:T(4,128)} copy(s32[4,2]{0,1:T(2,128)} %param.23) | data formatting | bytes 64 | tf_op args[10]
  2.1 1.3 %copy.171.from_hbm = s32[4,2]{1,0:T(4,128)} copy(s32[4,2]{0,1:T(2,128)} %param.20) | data formatting | bytes 64 | tf_op args[7]
  4.7 3.7 %shard_map.164 = (bf16[2,2,64,2048]{3,2,1,0:T(8,128)(2,1)}, bf16[2,2,64,2048]{3,2,1,0:T(8,128)(2,1)}, bf16[4,2,64,256]{3,2,1,0:T(8,128)(2,1)}, bf16[128,2,256]{2...) custom-call(s32[4,2]{1,0:T(4,128)} %copy.171.from_hbm, s32[4,2]{1,0:T(4,128)} %copy.172.slot_hbm, ...), custom_call_target="tpu_custom_call" | custom-call | bytes 4718592 | tf_op jit(solution)/shard_map/pallas_call | solution.py:419
  9.8 2.4 %collective-permute-start.8 = (bf16[128,2,256]{2,1,0:T(2,128)(2,1)}, bf16[128,2,256]{2,1,0:T(2,128)(2,1)S(1)}, u32[]{:S(2)}, u32[]{:S(2)}) collective-permute-start(bf16[128,2,256]{2,1,0:T(2,128)(2,1)} %get-tuple-element.32), channel_id=1, source_target_pairs={{0,8},{4,12},{8,0},{12,4},{1,9},{5,13},{9,1},{13,5},{2,10},{6,14},... | collective-permute-start | bytes 393224 | tf_op jit(solution)/shard_map/ppermute | solution.py:409
  13.5 4.2 %fusion.11 = f32[12,2,2,64]{3,0,2,1:T(8,128)S(1)} fusion(bf16[8,2,64,2048]{3,2,1,0:T(8,128)(2,1)} %store_ref.4, bf16[14,2,2048]{2,0,1:T(8,128)(2,1)S(1)} %copy.176, pred[12,8]{0,1:T(8,128)(4,1)S(1)} %iota_compare_fusion.1), kind=kOutput, calls=%fused_computation.14 | convolution fusion | flops 100709376 | bytes 4321376 | tf_op jit(solution)/shard_map/msd,epkd->msepk/dot_general | solution.py:458
  21.4 2.5 %shard_map.167 = bf16[4,2,64,256]{3,2,1,0:T(8,128)(2,1)} custom-call(s32[4,2]{1,0:T(4,128)} %copy.174.adapter_hbm.adapter_ref, s32[16]{0:T(128)} %holder_ref.9, s32[16,1]{1,0:T(8,128)} %copy.175.dest_ref, bf16[8,2,64,256]{3,2,1,0:T(8,128)(2,1)} %store_ref.5, bf16[4,2,64,256]{3,2,1,0:T(8,128)(2,1)} %copy-done.5), custom_call_target="tpu_custom_call" | custom-call | bytes 524288 | tf_op jit(solution)/shard_map/pallas_call | solution.py:441
  23.9 2.1 %collective-permute-start.13 = (bf16[4,2,64,256]{3,2,1,0:T(8,128)(2,1)}, bf16[4,2,64,256]{3,2,1,0:T(8,128)(2,1)S(1)}, u32[]{:S(2)}, u32[]{:S(2)}) collective-permute-start(bf16[4,2,64,256]{3,2,1,0:T(8,128)(2,1)} %shard_map.167), channel_id=1, source_target_pairs={{0,8},{4,12},{8,0},{12,4},{1,9},{5,13},{9,1},{13,5},{2,10},{6,14},... | collective-permute-start | bytes 786440 | tf_op jit(solution)/shard_map/ppermute | solution.py:409
  27.0 2.9 %shard_map.165 = bf16[2,2,64,2048]{3,2,1,0:T(8,128)(2,1)} custom-call(s32[4,2]{1,0:T(4,128)} %copy.174.adapter_hbm.adapter_ref, s32[16]{0:T(128)} %holder_ref.9, s32[16,1]{1,0:T(8,128)} %copy.175.dest_ref, bf16[8,2,64,2048]{3,2,1,0:T(8,128)(2,1)} %store_ref.4, bf16[2,2,64,2048]{3,2,1,0:T(8,128)(2,1)} %copy-done.1), custom_call_target="tpu_custom_call" | custom-call | bytes 2097152 | tf_op jit(solution)/shard_map/pallas_call | solution.py:441
  30.1 1.6 %collective-permute-start.4 = (f32[24,128]{1,0:T(8,128)S(1)}, f32[24,128]{1,0:T(8,128)S(1)}, u32[]{:S(2)}, u32[]{:S(2)}) collective-permute-start(f32[24,128]{1,0:T(8,128)S(1)} %reshape.374), channel_id=1, source_target_pairs={{0,1},{1,2},{2,3},{3,0},{4,5},{5,6},{6,7},{7,4},{8,9},{9,10},{10,1... | collective-permute-start | bytes 36872 | tf_op jit(solution)/shard_map/ppermute | solution.py:412
  31.6 2.6 %collective-permute-start.5 = (f32[24,128]{1,0:T(8,128)S(1)}, f32[24,128]{1,0:T(8,128)S(1)}, u32[]{:S(2)}, u32[]{:S(2)}) collective-permute-start(f32[24,128]{1,0:T(8,128)S(1)} %reshape.374), channel_id=1, source_target_pairs={{0,2},{1,3},{2,0},{3,1},{4,6},{5,7},{6,4},{7,5},{8,10},{9,11},{10,... | collective-permute-start | bytes 36872 | tf_op jit(solution)/shard_map/ppermute | solution.py:412
  34.2 1.3 %collective-permute-start.6 = (f32[24,128]{1,0:T(8,128)S(1)}, f32[24,128]{1,0:T(8,128)}, u32[]{:S(2)}, u32[]{:S(2)}) collective-permute-start(f32[24,128]{1,0:T(8,128)S(1)} %reshape.374), channel_id=1, source_target_pairs={{0,3},{1,0},{2,1},{3,2},{4,7},{5,4},{6,5},{7,6},{8,11},{9,8},{10,9... | collective-permute-start | bytes 36872 | tf_op jit(solution)/shard_map/ppermute | solution.py:412
  38.4 1.7 %copy.177 = bf16[12,128,2,256]{3,1,2,0:T(8,128)(2,1)S(1)} copy(bf16[12,128,2,256]{3,2,1,0:T(2,128)(2,1)} %kv_ref.1) | data formatting | bytes 3145728 | tf_op jit(solution)/shard_map/optimization_barrier | solution.py:462
  40.3 1.5 %fusion.58 = (f32[2,2,2,8]{3,1,2,0:T(2,128)}, f32[2,2,2,8,128]{4,3,1,2,0:T(8,128)}) fusion(bf16[2,128,2,256]{3,1,2,0:T(8,128)(2,1)S(1)} %select_select_fusion, pred[2,128]{1,0:T(4,128)(4,1)S(1)} %iota_compare_fusion.2, bf16[14,2,16,128]{3,2,1,0:T(8,128)(2,1)S(1)} %copy-done.27), kind=kOutput, calls=%fused_computation.140 | convolution fusion | flops 2121664 | bytes 180992 | tf_op jit(solution)/shard_map/msgjd,mcgd->msgjc/dot_general | solution.py:45
  41.8 1.8 %fusion.60 = (f32[12,2,2,8]{3,1,2,0:T(2,128)}, f32[12,2,2,8,128]{4,3,1,2,0:T(8,128)}) fusion(bf16[12,128,2,256]{3,1,2,0:T(8,128)(2,1)S(1)} %copy.177, pred[12,128]{1,0:T(8,128)(4,1)S(1)} %iota_compare_fusion, bf16[14,2,16,128]{3,2,1,0:T(8,128)(2,1)S(1)} %copy-done.27), kind=kOutput, calls=%fused_computation.142 | convolution fusion | flops 12729984 | bytes 1084928 | tf_op jit(solution)/shard_map/msgjd,mcgd->msgjc/dot_general | solution.py:45
  46.8 2.9 %shard_map.166 = bf16[2,2,64,2048]{3,2,1,0:T(8,128)(2,1)} custom-call(s32[4,2]{1,0:T(4,128)} %copy.174.adapter_hbm.adapter_ref, s32[16]{0:T(128)} %holder_ref.9, s32[16,1]{1,0:T(8,128)} %copy.175.dest_ref, bf16[8,2,64,2048]{3,2,1,0:T(8,128)(2,1)} %store_ref.4, bf16[2,2,64,2048]{3,2,1,0:T(8,128)(2,1)} %copy-done.2), custom_call_target="tpu_custom_call" | custom-call | bytes 2097152 | tf_op jit(solution)/shard_map/pallas_call | solution.py:441
  50.2 2.7 %collective-permute-start.3 = (bf16[14,2,2048]{2,1,0:T(2,128)(2,1)S(1)}, bf16[14,2,2048]{2,1,0:T(2,128)(2,1)}, u32[]{:S(2)}, u32[]{:S(2)}) collective-permute-start(bf16[14,2,2048]{2,1,0:T(2,128)(2,1)S(1)} %copy-done.10), channel_id=1, source_target_pairs={{0,3},{1,0},{2,1},{3,2},{4,7},{5,4},{6,5},{7,6},{8,11},{9,8},{10,9... | collective-permute-start | bytes 344072 | tf_op jit(solution)/shard_map/ppermute | solution.py:412
  56.0 1.5 %collective-permute-start.11 = (bf16[2,2,64,2048]{3,2,1,0:T(8,128)(2,1)}, bf16[2,2,64,2048]{3,2,1,0:T(8,128)(2,1)S(1)}, u32[]{:S(2)}, u32[]{:S(2)}) collective-permute-start(bf16[2,2,64,2048]{3,2,1,0:T(8,128)(2,1)} %shard_map.166), channel_id=1, source_target_pairs={{0,8},{4,12},{8,0},{12,4},{1,9},{5,13},{9,1},{13,5},{2,10},{6,14},... | collective-permute-start | bytes 3145736 | tf_op jit(solution)/shard_map/ppermute | solution.py:409
  58.2 1.5 %pad_maximum_fusion = bf16[14,2,8192]{2,1,0:T(2,128)(2,1)S(1)} fusion(bf16[14,2,2048]{2,1,0:T(2,128)(2,1)} %collective-permute-done.3, bf16[14,2,2048]{2,1,0:T(2,128)(2,1)} %collective-permute-done.2, bf16[14,2,2048]{2,1,0:T(2,128)(2,1)} %collective-permute-done.1, bf16[14,2,2048]{2,1,0:T(2,128)(2,1)S(1)} %copy-done.10), kind=kLoop, calls=%fused_computation.38 | loop fusion | flops 1835008 | bytes 917504 | tf_op jit(solution)/shard_map/concatenate | solution.py:474
  59.7 1.6 %gather_fusion = bf16[4,14,2,2048]{3,2,1,0:T(2,128)(2,1)S(1)} fusion(bf16[14,2,4,2048]{3,1,2,0:T(2,128)(2,1)S(1)} %bitcast.115, s32[1024]{0:T(1024)} %pad_clamp_fusion.2), kind=kCustom, calls=%fused_computation | custom fusion | bytes 917520 | tf_op jit(solution)/shard_map/jit(_take)/gather | solution.py:477
  62.9 5.1 %fusion = f32[14,2,2,256]{3,0,2,1:T(8,128)S(1)} fusion(bf16[8192,2,256]{2,1,0:T(2,128)(2,1)} %param.16, bf16[14,2,8192,1]{2,1,0,3:T(2,128)(2,1)S(1)} %fusion.27), kind=kOutput, calls=%fused_computation.3 | convolution fusion | flops 234881024 | bytes 8904704 | tf_op jit(solution)/shard_map/msd,dgc->msgc/dot_general | solution.py:478
  70.2 29.0 %collective-permute-done.11.x0_ref = bf16[2,2,64,2048]{3,2,1,0:T(8,128)(2,1)S(1)} collective-permute-done((bf16[2,2,64,2048]{3,2,1,0:T(8,128)(2,1)}, bf16[2,2,64,2048]{3,2,1,0:T(8,128)(2,1)S(1)}, u32[]{:S(2)}, u32[]{:S(2)}) %collective-permute-start.11) | collective-permute-done | bytes 1048608 | tf_op jit(solution)/shard_map/ppermute | solution.py:409
  100.1 3.4 %shard_map.168 = (f32[2,16,128]{2,1,0:T(8,128)}, bf16[2,2,64,256]{3,2,1,0:T(8,128)(2,1)}) custom-call(s32[4,2]{1,0:T(4,128)} %copy.174.adapter_hbm.adapter_ref, s32[16]{0:T(128)} %holder_ref.9, s32[16,1]{1,0:T(8,128)} %copy.175.dest_ref, bf16[16,2048]{1,0:T(8,128)(2,1)} %pad.4.hid_ref, bf16[2,2,64,2048]{3,2,1,0:T(8,128)(2,1)} %copy-done.2, ...), custom_call_target="tpu_custom_call" | custom-call | flops 16777216 | bytes 1310720 | tf_op jit(solution)/shard_map/pallas_call | solution.py:509
  106.2 2.6 %collective-permute-start.16 = (f32[4,128]{1,0:T(4,128)S(1)}, f32[4,128]{1,0:T(4,128)S(1)}, u32[]{:S(2)}, u32[]{:S(2)}) collective-permute-start(f32[4,128]{1,0:T(4,128)S(1)} %pad_maximum_fusion.2), channel_id=1, source_target_pairs={{0,3},{1,0},{2,1},{3,2},{4,7},{5,4},{6,5},{7,6},{8,11},{9,8},{10,9... | collective-permute-start | bytes 6152 | tf_op jit(solution)/shard_map/ppermute | solution.py:412
  109.9 3.4 %shard_map.169 = (bf16[4,2,64,2048]{3,2,1,0:T(8,128)(2,1)}, bf16[4,2,64,256]{3,2,1,0:T(8,128)(2,1)}) custom-call(s32[4,2]{1,0:T(4,128)} %copy.174.adapter_hbm.adapter_ref, s32[16]{0:T(128)} %holder_ref.9, s32[16,1]{1,0:T(8,128)} %copy.175.dest_ref, bf16[2,2,64,2048]{3,2,1,0:T(8,128)(2,1)} %copy-done.2, bf16[2,2,64,2048]{3,2,1,0:T(8,128)(2,1)} %copy-done.1, ...), custom_call_target="tpu_custom_call" | custom-call | bytes 4718592 | tf_op jit(solution)/shard_map/pallas_call | solution.py:524
  (184 shorter events, 30.2 us)
Async XLA Ops:
  8.5 17.5 %collective-permute-start = (bf16[2,2,64,2048]{3,2,1,0:T(8,128)(2,1)}, bf16[2,2,64,2048]{3,2,1,0:T(8,128)(2,1)S(1)}, u32[]{:S(2)}, u32[]{:S(2)}) collective-permute-start(bf16[2,2,64,2048]{3,2,1,0:T(8,128)(2,1)} %get-tuple-element.22), channel_id=1, source_target_pairs={{0,4},{4,0},{8,12},{12,8},{1,5},{5,1},{9,13},{13,9},{2,6},{6,2},{1... | collective-permute-start | bytes 3145736 | tf_op jit(solution)/shard_map/ppermute | solution.py:409
  9.3 11.4 %collective-permute-start.12 = (bf16[4,2,64,256]{3,2,1,0:T(8,128)(2,1)}, bf16[4,2,64,256]{3,2,1,0:T(8,128)(2,1)S(1)}, u32[]{:S(2)}, u32[]{:S(2)}) collective-permute-start(bf16[4,2,64,256]{3,2,1,0:T(8,128)(2,1)} %get-tuple-element.34), channel_id=1, source_target_pairs={{0,4},{4,0},{8,12},{12,8},{1,5},{5,1},{9,13},{13,9},{2,6},{6,2},{1... | collective-permute-start | bytes 786440 | tf_op jit(solution)/shard_map/ppermute | solution.py:409
  9.4 11.0 %collective-permute-start.7 = (bf16[128,2,256]{2,1,0:T(2,128)(2,1)}, bf16[128,2,256]{2,1,0:T(2,128)(2,1)S(1)}, u32[]{:S(2)}, u32[]{:S(2)}) collective-permute-start(bf16[128,2,256]{2,1,0:T(2,128)(2,1)} %get-tuple-element.31), channel_id=1, source_target_pairs={{0,4},{4,0},{8,12},{12,8},{1,5},{5,1},{9,13},{13,9},{2,6},{6,2},{1... | collective-permute-start | bytes 393224 | tf_op jit(solution)/shard_map/ppermute | solution.py:409
  9.8 10.8 %collective-permute-start.8 = (bf16[128,2,256]{2,1,0:T(2,128)(2,1)}, bf16[128,2,256]{2,1,0:T(2,128)(2,1)S(1)}, u32[]{:S(2)}, u32[]{:S(2)}) collective-permute-start(bf16[128,2,256]{2,1,0:T(2,128)(2,1)} %get-tuple-element.32), channel_id=1, source_target_pairs={{0,8},{4,12},{8,0},{12,4},{1,9},{5,13},{9,1},{13,5},{2,10},{6,14},... | collective-permute-start | bytes 393224 | tf_op jit(solution)/shard_map/ppermute | solution.py:409
  12.2 8.5 %collective-permute-start.9 = (bf16[128,2,256]{2,1,0:T(2,128)(2,1)}, bf16[128,2,256]{2,1,0:T(2,128)(2,1)S(1)}, u32[]{:S(2)}, u32[]{:S(2)}) collective-permute-start(bf16[128,2,256]{2,1,0:T(2,128)(2,1)} %get-tuple-element.33), channel_id=1, source_target_pairs={{0,12},{4,8},{8,4},{12,0},{1,13},{5,9},{9,5},{13,1},{2,14},{6,10},... | collective-permute-start | bytes 393224 | tf_op jit(solution)/shard_map/ppermute | solution.py:409
  20.4 25.5 %collective-permute-start.10 = (bf16[2,2,64,2048]{3,2,1,0:T(8,128)(2,1)}, bf16[2,2,64,2048]{3,2,1,0:T(8,128)(2,1)S(1)}, u32[]{:S(2)}, u32[]{:S(2)}) collective-permute-start(bf16[2,2,64,2048]{3,2,1,0:T(8,128)(2,1)} %get-tuple-element.23), channel_id=1, source_target_pairs={{0,4},{4,0},{8,12},{12,8},{1,5},{5,1},{9,13},{13,9},{2,6},{6,2},{1... | collective-permute-start | bytes 3145736 | tf_op jit(solution)/shard_map/ppermute | solution.py:409
  23.9 46.2 %collective-permute-start.13 = (bf16[4,2,64,256]{3,2,1,0:T(8,128)(2,1)}, bf16[4,2,64,256]{3,2,1,0:T(8,128)(2,1)S(1)}, u32[]{:S(2)}, u32[]{:S(2)}) collective-permute-start(bf16[4,2,64,256]{3,2,1,0:T(8,128)(2,1)} %shard_map.167), channel_id=1, source_target_pairs={{0,8},{4,12},{8,0},{12,4},{1,9},{5,13},{9,1},{13,5},{2,10},{6,14},... | collective-permute-start | bytes 786440 | tf_op jit(solution)/shard_map/ppermute | solution.py:409
  30.1 19.7 %copy-start.15 = (f32[24,128]{1,0:T(8,128)}, f32[24,128]{1,0:T(8,128)S(1)}, u32[]{:S(2)}) copy-start(f32[24,128]{1,0:T(8,128)S(1)} %reshape.374) | copy-start | bytes 36868
  30.1 19.7 %collective-permute-start.4 = (f32[24,128]{1,0:T(8,128)S(1)}, f32[24,128]{1,0:T(8,128)S(1)}, u32[]{:S(2)}, u32[]{:S(2)}) collective-permute-start(f32[24,128]{1,0:T(8,128)S(1)} %reshape.374), channel_id=1, source_target_pairs={{0,1},{1,2},{2,3},{3,0},{4,5},{5,6},{6,7},{7,4},{8,9},{9,10},{10,1... | collective-permute-start | bytes 36872 | tf_op jit(solution)/shard_map/ppermute | solution.py:412
  31.6 18.6 %collective-permute-start.5 = (f32[24,128]{1,0:T(8,128)S(1)}, f32[24,128]{1,0:T(8,128)S(1)}, u32[]{:S(2)}, u32[]{:S(2)}) collective-permute-start(f32[24,128]{1,0:T(8,128)S(1)} %reshape.374), channel_id=1, source_target_pairs={{0,2},{1,3},{2,0},{3,1},{4,6},{5,7},{6,4},{7,5},{8,10},{9,11},{10,... | collective-permute-start | bytes 36872 | tf_op jit(solution)/shard_map/ppermute | solution.py:412
  34.2 18.7 %collective-permute-start.6 = (f32[24,128]{1,0:T(8,128)S(1)}, f32[24,128]{1,0:T(8,128)}, u32[]{:S(2)}, u32[]{:S(2)}) collective-permute-start(f32[24,128]{1,0:T(8,128)S(1)} %reshape.374), channel_id=1, source_target_pairs={{0,3},{1,0},{2,1},{3,2},{4,7},{5,4},{6,5},{7,6},{8,11},{9,8},{10,9... | collective-permute-start | bytes 36872 | tf_op jit(solution)/shard_map/ppermute | solution.py:412
  45.9 10.2 %collective-permute-start.1 = (bf16[14,2,2048]{2,1,0:T(2,128)(2,1)S(1)}, bf16[14,2,2048]{2,1,0:T(2,128)(2,1)}, u32[]{:S(2)}, u32[]{:S(2)}) collective-permute-start(bf16[14,2,2048]{2,1,0:T(2,128)(2,1)S(1)} %copy-done.10), channel_id=1, source_target_pairs={{0,1},{1,2},{2,3},{3,0},{4,5},{5,6},{6,7},{7,4},{8,9},{9,10},{10,1... | collective-permute-start | bytes 344072 | tf_op jit(solution)/shard_map/ppermute | solution.py:412
  49.8 8.4 %collective-permute-start.2 = (bf16[14,2,2048]{2,1,0:T(2,128)(2,1)S(1)}, bf16[14,2,2048]{2,1,0:T(2,128)(2,1)}, u32[]{:S(2)}, u32[]{:S(2)}) collective-permute-start(bf16[14,2,2048]{2,1,0:T(2,128)(2,1)S(1)} %copy-done.10), channel_id=1, source_target_pairs={{0,2},{1,3},{2,0},{3,1},{4,6},{5,7},{6,4},{7,5},{8,10},{9,11},{10,... | collective-permute-start | bytes 344072 | tf_op jit(solution)/shard_map/ppermute | solution.py:412
  50.2 8.0 %collective-permute-start.3 = (bf16[14,2,2048]{2,1,0:T(2,128)(2,1)S(1)}, bf16[14,2,2048]{2,1,0:T(2,128)(2,1)}, u32[]{:S(2)}, u32[]{:S(2)}) collective-permute-start(bf16[14,2,2048]{2,1,0:T(2,128)(2,1)S(1)} %copy-done.10), channel_id=1, source_target_pairs={{0,3},{1,0},{2,1},{3,2},{4,7},{5,4},{6,5},{7,6},{8,11},{9,8},{10,9... | collective-permute-start | bytes 344072 | tf_op jit(solution)/shard_map/ppermute | solution.py:412
  52.9 56.0 %collective-permute-start.17 = (bf16[2,2,64,2048]{3,2,1,0:T(8,128)(2,1)}, bf16[2,2,64,2048]{3,2,1,0:T(8,128)(2,1)S(1)}, u32[]{:S(2)}, u32[]{:S(2)}) collective-permute-start(bf16[2,2,64,2048]{3,2,1,0:T(8,128)(2,1)} %shard_map.165), channel_id=1, source_target_pairs={{0,8},{4,12},{8,0},{12,4},{1,9},{5,13},{9,1},{13,5},{2,10},{6,14},... | collective-permute-start | bytes 3145736 | tf_op jit(solution)/shard_map/ppermute | solution.py:409
  56.0 43.1 %collective-permute-start.11 = (bf16[2,2,64,2048]{3,2,1,0:T(8,128)(2,1)}, bf16[2,2,64,2048]{3,2,1,0:T(8,128)(2,1)S(1)}, u32[]{:S(2)}, u32[]{:S(2)}) collective-permute-start(bf16[2,2,64,2048]{3,2,1,0:T(8,128)(2,1)} %shard_map.166), channel_id=1, source_target_pairs={{0,8},{4,12},{8,0},{12,4},{1,9},{5,13},{9,1},{13,5},{2,10},{6,14},... | collective-permute-start | bytes 3145736 | tf_op jit(solution)/shard_map/ppermute | solution.py:409
  70.1 43.6 %copy-start.22 = (f32[2,2,64]{2,0,1:T(2,128)S(1)}, f32[2,2,64]{2,0,1:T(2,128)}, u32[]{:S(2)}) copy-start(f32[2,2,64]{2,0,1:T(2,128)} %get-tuple-element.74) | copy-start | bytes 3076
  70.1 43.6 %copy-start.23 = (f32[2,2,64]{2,0,1:T(2,128)S(1)}, f32[2,2,64]{2,0,1:T(2,128)}, u32[]{:S(2)}) copy-start(f32[2,2,64]{2,0,1:T(2,128)} %get-tuple-element.75) | copy-start | bytes 3076
  70.1 44.6 %copy-start.24 = (f32[2,2,2,8]{3,1,2,0:T(2,128)S(1)}, f32[2,2,2,8]{3,1,2,0:T(2,128)}, u32[]{:S(2)}) copy-start(f32[2,2,2,8]{3,1,2,0:T(2,128)} %get-tuple-element.76) | copy-start | bytes 772
  70.1 44.7 %copy-start.16 = (f32[2,2,2,8,128]{4,3,1,2,0:T(8,128)S(1)}, f32[2,2,2,8,128]{4,3,1,2,0:T(8,128)}, u32[]{:S(2)}) copy-start(f32[2,2,2,8,128]{4,3,1,2,0:T(8,128)} %get-tuple-element.77) | copy-start | bytes 98308
  70.1 29.0 %copy-start.8 = (bf16[4,2,64,256]{3,2,1,0:T(8,128)(2,1)}, bf16[4,2,64,256]{3,2,1,0:T(8,128)(2,1)S(1)}, u32[]{:S(2)}) copy-start(bf16[4,2,64,256]{3,2,1,0:T(8,128)(2,1)S(1)} %collective-permute-done.13.xb_ref) | copy-start | bytes 786436
  104.3 9.0 %collective-permute-start.14 = (f32[4,128]{1,0:T(4,128)S(1)}, f32[4,128]{1,0:T(4,128)S(1)}, u32[]{:S(2)}, u32[]{:S(2)}) collective-permute-start(f32[4,128]{1,0:T(4,128)S(1)} %pad_maximum_fusion.2), channel_id=1, source_target_pairs={{0,1},{1,2},{2,3},{3,0},{4,5},{5,6},{6,7},{7,4},{8,9},{9,10},{10,1... | collective-permute-start | bytes 6152 | tf_op jit(solution)/shard_map/ppermute | solution.py:412
  105.2 8.1 %collective-permute-start.15 = (f32[4,128]{1,0:T(4,128)S(1)}, f32[4,128]{1,0:T(4,128)S(1)}, u32[]{:S(2)}, u32[]{:S(2)}) collective-permute-start(f32[4,128]{1,0:T(4,128)S(1)} %pad_maximum_fusion.2), channel_id=1, source_target_pairs={{0,2},{1,3},{2,0},{3,1},{4,6},{5,7},{6,4},{7,5},{8,10},{9,11},{10,... | collective-permute-start | bytes 6152 | tf_op jit(solution)/shard_map/ppermute | solution.py:412
  106.2 7.1 %collective-permute-start.16 = (f32[4,128]{1,0:T(4,128)S(1)}, f32[4,128]{1,0:T(4,128)S(1)}, u32[]{:S(2)}, u32[]{:S(2)}) collective-permute-start(f32[4,128]{1,0:T(4,128)S(1)} %pad_maximum_fusion.2), channel_id=1, source_target_pairs={{0,3},{1,0},{2,1},{3,2},{4,7},{5,4},{6,5},{7,6},{8,11},{9,8},{10,9... | collective-permute-start | bytes 6152 | tf_op jit(solution)/shard_map/ppermute | solution.py:412
  (26 other events, 188.7 us)

commit v3 on v2

--- a/solution.py
+++ b/solution.py
@@ -211,21 +211,11 @@
 
 
 def needed_first(adapter_ref, dest):
-    first = adapter_ref[dest, 0]
-    second = adapter_ref[dest, 1]
-    other = jnp.where(first == 0, 1, 0)
-    second = jnp.where(second == first, other, second)
-    place, seen = [], jnp.int32(2)
-    for c in range(COPIES):
-        early = jnp.logical_or(first == c, second == c)
-        place.append(jnp.where(first == c, 0, jnp.where(second == c, 1, seen)))
-        seen = seen + jnp.where(early, 0, 1)
-    order = []
-    for j in range(COPIES):
-        at = jnp.int32(0)
-        for c in range(1, COPIES):
-            at = at + jnp.where(place[c] == j, c, 0)
-        order.append(at)
+    first, second = adapter_ref[0, dest], adapter_ref[1, dest]
+    ids = range(1, COPIES)
+    keys = [jnp.where(first == c, 0, jnp.where(second == c, 1, 2 + c)) for c in ids]
+    place = [sum(jnp.where(other < key, 1, 0) for other in keys) for key in keys]
+    order = [sum(jnp.where(place[c - 1] == j, c, 0) for c in ids) for j in range(COPIES - 1)]
     return order, place
 
 
@@ -241,7 +231,7 @@
     found = jnp.int32(0)
     for s in range(spans):
         row = copy_id * spans + s
-        found = jnp.where(dest_ref[row, 0] == dest, holder_ref[row], found)
+        found = jnp.where(dest_ref[0, row] == dest, holder_ref[row], found)
     return found
 
 
@@ -249,21 +239,34 @@
     def __init__(self, sems):
         self.sems, self.jobs = sems, []
 
-    def go(self, src, stage, dst):
-        pltpu.make_async_copy(src, stage, self.sems.at[len(self.jobs)]).start()
+    def go(self, options, stage, dst):
+        sem = self.sems.at[len(self.jobs)]
+        for condition, src in options:
+            if condition is None:
+                pltpu.make_async_copy(src, stage, sem).start()
+            else:
+
+                @pl.when(condition)
+                def _():
+                    pltpu.make_async_copy(src, stage, sem).start()
+
         self.jobs.append((stage, dst))
+
+    def arrived(self, i):
+        stage, _ = self.jobs[i]
+        pltpu.make_async_copy(stage, stage, self.sems.at[i]).wait()
 
     def finish(self):
         half = len(self.jobs)
         for i, (stage, dst) in enumerate(self.jobs):
-            pltpu.make_async_copy(dst, stage, self.sems.at[i]).wait()
+            self.arrived(i)
             pltpu.make_async_copy(stage, dst, self.sems.at[half + i]).start()
         for i, (stage, dst) in enumerate(self.jobs):
             pltpu.make_async_copy(stage, dst, self.sems.at[half + i]).wait()
 
 
 def pack_kernel(spans, slots, from_hbm, slot_hbm, adapter_hbm, holder_hbm, a_ref, b_ref, kv_ref,
-                a0_ref, a1_ref, b_out, k1_ref, k2_ref, k3_ref,
+                z_out, u0_out, u12_out, b_out, k1_out, k2_out, k3_out,
                 from_ref, slot_ref, adapter_ref, holder_ref, a_stage, b_stage, k_stage, small_sems, sems):
     me = lax.axis_index("replica")
     small = [
@@ -277,98 +280,94 @@
     for copy in small:
         copy.wait()
     staged = Staged(sems)
-
     order, _ = needed_first(adapter_ref, me ^ 3)
-    held = [held_slot(holder_ref, spans, slots, me, c) for c in order]
-    for j in range(2):
-        staged.go(a_ref.at[held[j]], a_stage.at[j], a0_ref.at[j])
-    for j in range(COPIES):
-        staged.go(b_ref.at[held[j]], b_stage.at[j], b_out.at[j])
-    for k, out in ((1, k1_ref), (2, k2_ref), (3, k3_ref)):
-        chosen = jnp.int32(0)
-        for a in range(2):
-            chosen = jnp.where(from_ref[me ^ k, a] == me, slot_ref[me ^ k, a], chosen)
-        staged.go(kv_ref.at[chosen], k_stage.at[k - 1], out)
-    for j in range(2):
-        staged.go(a_ref.at[held[2 + j]], a_stage.at[2 + j], a1_ref.at[j])
+    outs = (z_out, u0_out, u12_out.at[0], u12_out.at[1])
+    for j, c in enumerate([0] + order):
+        staged.go([(None, a_ref.at[held_slot(holder_ref, spans, slots, me, c)])], a_stage.at[j], outs[j])
+        if j == 0:
+            for c in range(COPIES):
+                staged.go([(None, b_ref.at[held_slot(holder_ref, spans, slots, me, c)])], b_stage.at[c], b_out.at[c])
+            for k, out in ((1, k1_out), (2, k2_out), (3, k3_out)):
+                chosen = jnp.int32(0)
+                for a in range(2):
+                    chosen = jnp.where(from_ref[a, me ^ k] == me, slot_ref[a, me ^ k], chosen)
+                staged.go([(None, kv_ref.at[chosen])], k_stage.at[k - 1], out)
     staged.finish()
 
 
-def pick_kernel(spans, slots, base, count, adapter_ref, holder_ref, dest_ref, store_ref, core_ref, out_ref, stage, sems):
+def pick_kernel(spans, slots, places, copies, adapter_ref, holder_ref, dest_ref, a_ref, b_ref, core_a, core_b, *rest):
+    outs, (a_stage, b_stage, sems) = rest[:-3], rest[-3:]
     me = lax.axis_index("replica")
-    dest = me ^ 2
-    order, _ = needed_first(adapter_ref, dest)
-    for j in range(count):
-        holder = holder_of(holder_ref, dest_ref, spans, dest, order[base + j])
+    order, _ = needed_first(adapter_ref, me ^ 2)
+    staged = Staged(sems)
+
+    def options(c, store, core):
+        holder = holder_of(holder_ref, dest_ref, spans, me ^ 2, c)
         mine = holder // slots == me
-
-        @pl.when(mine)
-        def _():
-            pltpu.make_async_copy(store_ref.at[holder % slots], stage.at[j], sems.at[j]).start()
-
-        @pl.when(jnp.logical_not(mine))
-        def _():
-            pltpu.make_async_copy(core_ref.at[j], stage.at[j], sems.at[j]).start()
-
-    for j in range(count):
-        pltpu.make_async_copy(core_ref.at[j], stage.at[j], sems.at[j]).wait()
-        pltpu.make_async_copy(stage.at[j], out_ref.at[j], sems.at[count + j]).start()
-    for j in range(count):
-        pltpu.make_async_copy(stage.at[j], out_ref.at[j], sems.at[count + j]).wait()
-
-
-def choose(near, place_near, place_far, near_refs, far_refs, dst, sem):
-    for wanted, place, refs in ((near, place_near, near_refs), (jnp.logical_not(near), place_far, far_refs)):
-        each = COPIES // 2 if len(refs) == 2 else COPIES
-        for r, ref in enumerate(refs):
-            inside = jnp.logical_and(place >= r * each, place < (r + 1) * each)
-
-            @pl.when(jnp.logical_and(wanted, inside))
-            def _():
-                pltpu.make_async_copy(ref.at[place - r * each], dst, sem).start()
-
-
-def arrive_kernel(spans, slots, adapter_ref, holder_ref, dest_ref, hid_ref, c0_ref, c1_ref, x0_ref, cb_ref, xb_ref,
-                  out_ref, b_out, units, sems):
+        return [(mine, store.at[holder % slots]), (jnp.logical_not(mine), core)]
+
+    for i, j in enumerate(places):
+        core = core_a if len(core_a.shape) == 3 else core_a.at[i]
+        staged.go(options(order[j], a_ref, core), a_stage.at[i], outs[i])
+    for c in range(copies):
+        staged.go(options(c, b_ref, core_b.at[c]), b_stage.at[c], outs[-1].at[c])
+    staged.finish()
+
+
+def sources(spans, slots, adapter_ref, holder_ref, dest_ref, z_refs, near_refs, far_refs, near_b, far_b):
     me = lax.axis_index("replica")
     _, place_far = needed_first(adapter_ref, me)
     _, place_near = needed_first(adapter_ref, me ^ 2)
 
     def at(places, c):
-        found = places[0]
-        for i in range(1, COPIES):
-            found = jnp.where(c == i, places[i], found)
-        return found
-
+        return sum(jnp.where(c == i + 1, place, 0) for i, place in enumerate(places))
+
+    def options(c):
+        holder = holder_of(holder_ref, dest_ref, spans, me, c) // slots
+        near = holder == (me ^ 1)
+        far = jnp.logical_not(near)
+        of_a = []
+        zero = c == 0
+        for k, ref in enumerate(z_refs):
+            of_a.append((jnp.logical_and(zero, holder == (me ^ (k + 1))), ref))
+        for side, places, refs in ((near, place_near, near_refs), (far, place_far, far_refs)):
+            for j, ref in enumerate(refs):
+                here = jnp.logical_and(side, at(places, c) == j)
+                of_a.append((jnp.logical_and(c != 0, here), ref))
+        return of_a, [(near, near_b.at[c]), (far, far_b.at[c])]
+
+    return options
+
+
+def arrive_kernel(spans, slots, adapter_ref, holder_ref, dest_ref, hid_ref, z1, z2, z3, u0, u12, f0, f1, cb, xb,
+                  out_ref, b_out, units, sems):
+    me = lax.axis_index("replica")
+    options = sources(
+        spans, slots, adapter_ref, holder_ref, dest_ref, (z1, z2, z3), (u0, u12.at[0], u12.at[1]), (f0, f1), cb, xb
+    )
+    staged = Staged(sems)
     for a in range(2):
-        c = adapter_ref[me, a]
-        near = holder_of(holder_ref, dest_ref, spans, me, c) // slots == (me ^ 1)
-        choose(near, at(place_near, c), at(place_far, c), (c0_ref, c1_ref), (x0_ref, x0_ref), units.at[a], sems.at[a])
-        choose(near, at(place_near, c), at(place_far, c), (cb_ref,), (xb_ref,), b_out.at[a], sems.at[2 + a])
+        of_a, of_b = options(adapter_ref[a, me])
+        staged.go(of_a, units.at[a], None)
+        staged.go(of_b, b_out.at[a], None)
     for a in range(2):
-        pltpu.make_async_copy(c0_ref.at[0], units.at[a], sems.at[a]).wait()
+        staged.arrived(2 * a)
         unit = units[a].reshape(units.shape[1] * units.shape[2], units.shape[3])
         out_ref[a] = lax.dot_general(hid_ref[...], unit, (((1,), (1,)), ((), ())), preferred_element_type=jnp.float32)
-        pltpu.make_async_copy(cb_ref.at[0], b_out.at[a], sems.at[2 + a]).wait()
-
-
-def install_kernel(spans, slots, adapter_ref, holder_ref, dest_ref, c0_ref, c1_ref, x0_ref, x1_ref, cb_ref, xb_ref,
+        staged.arrived(2 * a + 1)
+
+
+def install_kernel(spans, slots, adapter_ref, holder_ref, dest_ref, z1, z2, z3, u0, u12, f0, f1, f2, cb, xb,
                    a_out, b_out, a_stage, b_stage, sems):
-    me = lax.axis_index("replica")
-    _, place_far = needed_first(adapter_ref, me)
-    _, place_near = needed_first(adapter_ref, me ^ 2)
+    options = sources(
+        spans, slots, adapter_ref, holder_ref, dest_ref, (z1, z2, z3), (u0, u12.at[0], u12.at[1]), (f0, f1, f2), cb, xb
+    )
+    staged = Staged(sems)
     for c in range(COPIES):
-        near = holder_of(holder_ref, dest_ref, spans, me, c) // slots == (me ^ 1)
-        choose(near, place_near[c], place_far[c], (c0_ref, c1_ref), (x0_ref, x1_ref), a_stage.at[c], sems.at[c])
-        choose(near, place_near[c], place_far[c], (cb_ref,), (xb_ref,), b_stage.at[c], sems.at[COPIES + c])
-    for c in range(COPIES):
-        pltpu.make_async_copy(c0_ref.at[0], a_stage.at[c], sems.at[c]).wait()
-        pltpu.make_async_copy(a_stage.at[c], a_out.at[c], sems.at[2 * COPIES + c]).start()
-        pltpu.make_async_copy(cb_ref.at[0], b_stage.at[c], sems.at[COPIES + c]).wait()
-        pltpu.make_async_copy(b_stage.at[c], b_out.at[c], sems.at[3 * COPIES + c]).start()
-    for c in range(COPIES):
-        pltpu.make_async_copy(a_stage.at[c], a_out.at[c], sems.at[2 * COPIES + c]).wait()
-        pltpu.make_async_copy(b_stage.at[c], b_out.at[c], sems.at[3 * COPIES + c]).wait()
+        of_a, of_b = options(jnp.int32(c))
+        staged.go(of_a, a_stage.at[c], a_out.at[c])
+        staged.go(of_b, b_stage.at[c], b_out.at[c])
+    staged.finish()
 
 
 SMEM = pl.BlockSpec(memory_space=pltpu.SMEM)
@@ -416,12 +415,18 @@
 
     size_a, size_b = 2 * math.prod(unit_a), 2 * math.prod(unit_b)
 
-    a0, a1, b_all, k1, k2, k3 = pl.pallas_call(
+    plan = (arrival_adapter.T, hot_holder, hot_dest.T)
+    leave = (arrival_from.T, arrival_slot.T)
+
+    z, u0, u12, b_all, k1, k2, k3 = pl.pallas_call(
         functools.partial(pack_kernel, spans, slots),
-        out_shape=(shaped(2, *unit_a), shaped(2, *unit_a), shaped(COPIES, *unit_b), shaped(*unit_k), shaped(*unit_k), shaped(*unit_k)),
+        out_shape=(
+            shaped(*unit_a), shaped(*unit_a), shaped(2, *unit_a), shaped(COPIES, *unit_b),
+            shaped(*unit_k), shaped(*unit_k), shaped(*unit_k),
+        ),
         in_specs=[ANY] * 7,
-        out_specs=(ANY,) * 6,
-        scratch_shapes=[pltpu.SMEM(x.shape, x.dtype) for x in (arrival_from, arrival_slot, arrival_adapter, hot_holder)]
+        out_specs=(ANY,) * 7,
+        scratch_shapes=[pltpu.SMEM(x.shape, x.dtype) for x in leave + plan[:2]]
         + [
             pltpu.VMEM((COPIES,) + unit_a, kind),
             pltpu.VMEM((COPIES,) + unit_b, kind),
@@ -430,39 +435,45 @@
             pltpu.SemaphoreType.DMA((2 * (2 * COPIES + 3),)),
         ],
         cost_estimate=cost(8 * size_a + 8 * size_b),
-    )(arrival_from, arrival_slot, arrival_adapter, hot_holder, store_a, store_b, kv_cache)
-    core_a0, core_b = swap(a0, 1), swap(b_all, 1)
-    core_a1 = swap(a1, 1)
+    )(*leave, *plan[:2], store_a, store_b, kv_cache)
+    z2 = swap(z, 2)
+    core_u0, core_b = swap(u0, 1), swap(b_all, 1)
+    core_u12 = swap(u12, 1)
+    u0, hidden = lax.optimization_barrier((u0, hidden))
+
+    def pick(places, copies, core):
+        out = pl.pallas_call(
+            functools.partial(pick_kernel, spans, slots, places, copies),
+            out_shape=tuple(shaped(*unit_a) for _ in places) + (shaped(COPIES, *unit_b),) * (copies > 0),
+            in_specs=[SMEM] * 3 + [ANY] * 4,
+            out_specs=(ANY,) * (len(places) + (copies > 0)),
+            scratch_shapes=[
+                pltpu.VMEM((len(places),) + unit_a, kind),
+                pltpu.VMEM((COPIES,) + unit_b, kind),
+                pltpu.SemaphoreType.DMA((2 * (len(places) + copies),)),
+            ],
+            cost_estimate=cost(2 * len(places) * size_a + 2 * copies * size_b),
+        )(*plan, store_a, store_b, core, core_b)
+        return out
+
+    to0, to_b = pick((0,), COPIES, core_u0)
+    f0 = swap(to0, 2)
+    to1, to2 = pick((1, 2), 0, core_u12)
+
+    z2, to1 = lax.optimization_barrier((z2, to1))
+    f1 = swap(to1, 2)
+    f0, to_b, k2, k3 = lax.optimization_barrier((f0, to_b, k2, k3))
+    far_b = swap(to_b, 2)
     far = (swap(k2, 2), swap(k3, 3))
-    near = swap(k1, 1)
-    a0, hidden = lax.optimization_barrier((a0, hidden))
-
-    def pick(base, count, store, core):
-        return pl.pallas_call(
-            functools.partial(pick_kernel, spans, slots, base, count),
-            out_shape=shaped(count, *store.shape[1:]),
-            in_specs=[SMEM] * 3 + [ANY] * 2,
-            out_specs=ANY,
-            scratch_shapes=[pltpu.VMEM((count,) + store.shape[1:], kind), pltpu.SemaphoreType.DMA((2 * count,))],
-            cost_estimate=cost(4 * count * math.prod(store.shape[1:])),
-        )(arrival_adapter, hot_holder, hot_dest, store, core)
-
-    to_a0 = pick(0, 2, store_a, core_a0)
-    far_a0 = swap(to_a0, 2)
-    to_b = pick(0, COPIES, store_b, core_b)
-    far_b = swap(to_b, 2)
-    to_a1 = pick(2, 2, store_a, core_a1)
-    far_a1 = swap(to_a1, 2)
+    far_b, to2 = lax.optimization_barrier((far_b, to2))
+    f2 = swap(to2, 2)
 
     own_adapter = lax.dynamic_slice_in_dim(resident_adapter, me * resident, resident)
     every = jnp.einsum("msd,epkd->msepk", hidden[:resident], store_a, preferred_element_type=jnp.float32)
     is_own = own_adapter[:, None] == jnp.arange(slots, dtype=jnp.int32)[None, :]
     part_own = jnp.sum(jnp.where(is_own[:, None, :, None, None], every, 0.0), axis=2)
 
-    _, hidden, part_own, queries, lengths, own_adapter, kv_cache = lax.optimization_barrier(
-        (to_a1, hidden, part_own, queries, lengths, own_adapter, kv_cache)
-    )
-    pieces = [hidden] + [shift(hidden, k) for k in range(1, tensors)]
+    _, part_own = lax.optimization_barrier((to0, part_own))
 
     def total(part):
         out = part
@@ -471,6 +482,12 @@
         return out.astype(jnp.bfloat16)
 
     shrink_own = total(part_own.reshape(resident * steps, -1)).reshape(resident, steps, 2, -1)
+    _, _, _, shrink_own, hidden, lengths, kv_cache, queries = lax.optimization_barrier(
+        (to1, to2, z2, shrink_own, hidden, lengths, kv_cache, queries)
+    )
+    pieces = [hidden] + [shift(hidden, k) for k in range(1, tensors)]
+    pieces, z, k1 = lax.optimization_barrier((pieces, z, k1))
+    z1, z3, near = swap(z, 1), swap(z2, 1), swap(k1, 1)
     whole = jnp.concatenate(pieces, axis=2)
     whole = whole.reshape(requests, steps, tensors, width)
     turn = (tensor_index - jnp.arange(tensors, dtype=jnp.int32)) % tensors
@@ -509,11 +526,11 @@
     part_new, up_new = pl.pallas_call(
         functools.partial(arrive_kernel, spans, slots),
         out_shape=(shaped(arrive, rows, math.prod(unit_a[:2]), dtype=jnp.float32), shaped(arrive, *unit_b)),
-        in_specs=[SMEM] * 3 + [VMEM] + [ANY] * 5,
+        in_specs=[SMEM] * 3 + [VMEM] + [ANY] * 9,
         out_specs=(VMEM, VMEM),
         scratch_shapes=[pltpu.VMEM((arrive,) + unit_a, kind), pltpu.SemaphoreType.DMA((2 * arrive,))],
         cost_estimate=cost(arrive * (size_a + 2 * size_b), 2 * arrive * rows * size_a // 2),
-    )(arrival_adapter, hot_holder, hot_dest, guests, core_a0, core_a1, far_a0, core_b, far_b)
+    )(*plan, guests, z1, z2, z3, core_u0, core_u12, f0, f1, core_b, far_b)
     part_new = jnp.concatenate([part_new[a, a * steps : (a + 1) * steps] for a in range(arrive)], axis=0)
     shrink_new = total(part_new).reshape(arrive, steps, 2, -1)
     fresh_new = fresh_rows(base[resident:], shrink_new, up_new, arrival_len)
@@ -524,7 +541,7 @@
     installed_a, installed_b = pl.pallas_call(
         functools.partial(install_kernel, spans, slots),
         out_shape=(shaped(COPIES, *unit_a), shaped(COPIES, *unit_b)),
-        in_specs=[SMEM] * 3 + [ANY] * 6,
+        in_specs=[SMEM] * 3 + [ANY] * 10,
         out_specs=(ANY, ANY),
         scratch_shapes=[
             pltpu.VMEM((COPIES,) + unit_a, kind),
@@ -532,7 +549,7 @@
             pltpu.SemaphoreType.DMA((4 * COPIES,)),
         ],
         cost_estimate=cost(8 * size_a + 8 * size_b),
-    )(arrival_adapter, hot_holder, hot_dest, core_a0, core_a1, far_a0, far_a1, core_b, far_b)
+    )(*plan, z1, z2, z3, core_u0, core_u12, f0, f1, f2, core_b, far_b)
     return (attn_out, new_kv, arrived, installed_a, installed_b)
 
 

time: 117 us -> 91.3 us (0.78)
  waiting for transfers between devices: 29.7 us -> 9.35 us
  local copies, waits for them, and re-layouts: 19 us -> 14.9 us
  Pallas kernels: 18.9 us -> 16.1 us
  starting transfers between devices: 21.9 us -> 24.1 us
    ppermute x9 -> x13, waiting for transfers between devices: 29 us -> 9.33 us  [swap(): return lax.ppermute(array, 'replica', [(i, i ^ k) for i in range(PAIRED)])]
    unnamed x70, local copies, waits for them, and re-layouts: 11.1 us -> 6.18 us
    pallas_call x3 -> x2, Pallas kernels: 8.35 us -> 5.66 us  [pick(): pl.pallas_call(functools.partial(pick_kernel, spans, slots, places, copie...]
    ppermute x9 -> x13, starting transfers between devices: 8.04 us -> 10.7 us  [swap(): return lax.ppermute(array, 'replica', [(i, i ^ k) for i in range(PAIRED)])]
    optimization_barrier x3, local copies, waits for them, and re-layouts: 1.73 us -> 0.33 us  [the longest x1 0.27 us: paired(): lax.optimization_barrier((to1, to2, z2, shrink_own, hidden, lengths, kv_c...]
    ppermute x3, local copies, waits for them, and re-layouts: 0.05 us -> 1.35 us  [swap(): return lax.ppermute(array, 'replica', [(i, i ^ k) for i in range(PAIRED)])]
  transfers between devices with their start and end apart: 18 -> 22, of which waited for: 2 -> 3; matrix products, arithmetic and copies ran while one was open for 29% -> 36% of each run, Pallas kernels for 13% -> 14%
where the time goes in v3:
time: 91.3 us; the launch traced here: 90.7 us
  starting transfers between devices  24.1 us (26%)
  Pallas kernels  16.1 us (18%)
  matrix products  15.6 us (17%)
  local copies, waits for them, and re-layouts  14.9 us (16%)
  waiting for transfers between devices  9.35 us (10%)
  other arithmetic  9.26 us (10%)
  between operations  1.41 us (2%)
    ppermute x9, starting transfers between devices, shift(): lax.ppermute(array, 'tensor', [(i, (i + k) % tensors) for i in range(tens...  13.5 us
    ppermute x13, starting transfers between devices, swap(): return lax.ppermute(array, 'replica', [(i, i ^ k) for i in range(PAIRED)])  10.7 us
    ppermute x13, waiting for transfers between devices, swap(): return lax.ppermute(array, 'replica', [(i, i ^ k) for i in range(PAIRED)])  9.33 us
    unnamed x70, local copies, waits for them, and re-layouts  6.18 us
    pallas_call x2, Pallas kernels, pick(): pl.pallas_call(functools.partial(pick_kernel, spans, slots, places, copie...  5.66 us
    dot_general x1, matrix products, paired(): jnp.einsum('msd,dgc->msgc', whole, w_kv, preferred_element_type=jnp.float32)  5.06 us
    dot_general x1, matrix products, paired(): jnp.einsum('msd,epkd->msepk', hidden[:resident], store_a, preferred_eleme...  4.24 us
    pallas_call x1, Pallas kernels, paired(): pl.pallas_call(functools.partial(pack_kernel, spans, slots), out_shape=(s...  3.7 us
  transfers between devices with their start and end apart: 22, of which 3 were waited for; matrix products, arithmetic and copies ran while one was open for 36% of the time, Pallas kernels for 14%

profile of v3, /device:TPU:0, one launch (start us, length us, event | category | flops | bytes accessed | tf_op | source)
XLA Modules:
  0.0 90.7 jit_solution(13604444392719791611)
XLA Ops:
  0.7 3.7 %shard_map.164 = (bf16[2,64,2048]{2,1,0:T(8,128)(2,1)}, bf16[2,64,2048]{2,1,0:T(8,128)(2,1)}, bf16[2,2,64,2048]{3,2,1,0:T(8,128)(2,1)}, bf16[4,2,64,256]{3,2,1,0...) custom-call(s32[2,4]{1,0:T(2,128)} %bitcast.130, ...), custom_call_target="tpu_custom_call" | custom-call | bytes 4718592 | tf_op jit(solution)/shard_map/pallas_call | solution.py:421
  4.4 3.2 %collective-permute-start = (bf16[2,64,2048]{2,1,0:T(8,128)(2,1)}, bf16[2,64,2048]{2,1,0:T(8,128)(2,1)}, u32[]{:S(2)}, u32[]{:S(2)}) collective-permute-start(bf16[2,64,2048]{2,1,0:T(8,128)(2,1)} %get-tuple-element.70), channel_id=1, source_target_pairs={{0,8},{4,12},{8,0},{12,4},{1,9},{5,13},{9,1},{13,5},{2,10},{6,14},... | collective-permute-start | bytes 1572872 | tf_op jit(solution)/shard_map/ppermute | solution.py:408
  9.5 1.4 %collective-permute-done.2.core_b.cb = bf16[4,2,64,256]{3,2,1,0:T(8,128)(2,1)S(1)} collective-permute-done((bf16[4,2,64,256]{3,2,1,0:T(8,128)(2,1)}, bf16[4,2,64,256]{3,2,1,0:T(8,128)(2,1)S(1)}, u32[]{:S(2)}, u32[]{:S(2)}) %collective-permute-start.2) | collective-permute-done | bytes 262176 | tf_op jit(solution)/shard_map/ppermute | solution.py:408
  12.4 2.9 %shard_map.166 = (bf16[2,64,2048]{2,1,0:T(8,128)(2,1)}, bf16[4,2,64,256]{3,2,1,0:T(8,128)(2,1)}) custom-call(s32[2,4]{1,0:T(2,128)} %bitcast.126, s32[16]{0:T(128)} %holder_ref.7, s32[1,16]{1,0:T(1,128)} %bitcast.132, bf16[8,2,64,2048]{3,2,1,0:T(8,128)(2,1)} %a_ref.5, bf16[8,2,64,256]{3,2,1,0:T(8,128)(2,1)} %b_ref.5, bf16[2,64,2048]{2,1,0:T(8,128)(2,1)} %copy-done.4, ...), custom_call_target="tpu_custom_call" | custom-call | bytes 1572864 | tf_op jit(solution)/shard_map/pallas_call | solution.py:445
  15.5 4.2 %fusion.11 = f32[12,2,2,64]{3,0,2,1:T(8,128)S(1)} fusion(bf16[8,2,64,2048]{3,2,1,0:T(8,128)(2,1)} %a_ref.5, bf16[14,2,2048]{2,0,1:T(8,128)(2,1)S(1)} %copy.119, pred[12,8]{0,1:T(8,128)(4,1)S(1)} %iota_compare_fusion.1), kind=kOutput, calls=%fused_computation.14 | convolution fusion | flops 100709376 | bytes 4321376 | tf_op jit(solution)/shard_map/msd,epkd->msepk/dot_general | solution.py:472
  19.8 3.8 %collective-permute-start.8 = (f32[24,128]{1,0:T(8,128)S(1)}, f32[24,128]{1,0:T(8,128)S(1)}, u32[]{:S(2)}, u32[]{:S(2)}) collective-permute-start(f32[24,128]{1,0:T(8,128)S(1)} %reshape.372), channel_id=1, source_target_pairs={{0,3},{1,0},{2,1},{3,2},{4,7},{5,4},{6,5},{7,6},{8,11},{9,8},{10,9... | collective-permute-start | bytes 36872 | tf_op jit(solution)/shard_map/ppermute | solution.py:411
  23.7 7.2 %collective-permute-done.4.f0 = bf16[2,64,2048]{2,1,0:T(8,128)(2,1)S(1)} collective-permute-done((bf16[2,64,2048]{2,1,0:T(8,128)(2,1)}, bf16[2,64,2048]{2,1,0:T(8,128)(2,1)S(1)}, u32[]{:S(2)}, u32[]{:S(2)}) %collective-permute-start.4) | collective-permute-done | bytes 524320 | tf_op jit(solution)/shard_map/ppermute | solution.py:408
  30.9 1.7 %collective-permute-start.6 = (f32[24,128]{1,0:T(8,128)S(1)}, f32[24,128]{1,0:T(8,128)S(1)}, u32[]{:S(2)}, u32[]{:S(2)}) collective-permute-start(f32[24,128]{1,0:T(8,128)S(1)} %reshape.372), channel_id=1, source_target_pairs={{0,1},{1,2},{2,3},{3,0},{4,5},{5,6},{6,7},{7,4},{8,9},{9,10},{10,1... | collective-permute-start | bytes 36872 | tf_op jit(solution)/shard_map/ppermute | solution.py:411
  32.6 1.6 %collective-permute-start.5 = (bf16[4,2,64,256]{3,2,1,0:T(8,128)(2,1)}, bf16[4,2,64,256]{3,2,1,0:T(8,128)(2,1)S(1)}, u32[]{:S(2)}, u32[]{:S(2)}) collective-permute-start(bf16[4,2,64,256]{3,2,1,0:T(8,128)(2,1)} %get-tuple-element.51), channel_id=1, source_target_pairs={{0,8},{4,12},{8,0},{12,4},{1,9},{5,13},{9,1},{13,5},{2,10},{6,14},... | collective-permute-start | bytes 786440 | tf_op jit(solution)/shard_map/ppermute | solution.py:408
  34.8 1.5 %gather_fusion.1 = bf16[12,2,64,256]{3,2,1,0:T(8,128)(2,1)} fusion(bf16[8,2,64,256]{3,2,1,0:T(8,128)(2,1)S(1)} %copy-done.1, s32[1024]{0:T(1024)S(1)} %pad_clamp_fusion.1), kind=kCustom, calls=%fused_computation.1 | custom fusion | bytes 1572912 | tf_op jit(solution)/shard_map/jit(_take)/gather | solution.py:514
  39.2 2.8 %shard_map.165 = (bf16[2,64,2048]{2,1,0:T(8,128)(2,1)}, bf16[2,64,2048]{2,1,0:T(8,128)(2,1)}) custom-call(s32[2,4]{1,0:T(2,128)} %bitcast.127, s32[16]{0:T(128)} %holder_ref.7, s32[1,16]{1,0:T(1,128)} %bitcast.133, bf16[8,2,64,2048]{3,2,1,0:T(8,128)(2,1)} %a_ref.5, bf16[8,2,64,256]{3,2,1,0:T(8,128)(2,1)} %b_ref.5, bf16[2,2,64,2048]{3,2,1,0:T(8,128)(2,1)} %copy-done.2, ...), custom_call_target="tpu_custom_call" | custom-call | bytes 2097152 | tf_op jit(solution)/shard_map/pallas_call | solution.py:445
  42.0 1.4 %collective-permute-start.16 = (bf16[2,64,2048]{2,1,0:T(8,128)(2,1)}, bf16[2,64,2048]{2,1,0:T(8,128)(2,1)S(1)}, u32[]{:S(2)}, u32[]{:S(2)}) collective-permute-start(bf16[2,64,2048]{2,1,0:T(8,128)(2,1)} %collective-permute-done.z2), channel_id=1, source_target_pairs={{0,4},{4,0},{8,12},{12,8},{1,5},{5,1},{9,13},{13,9},{2,6},{6,2},{1... | collective-permute-start | bytes 1572872 | tf_op jit(solution)/shard_map/ppermute | solution.py:408
  45.2 1.6 %collective-permute-start.9 = (bf16[14,2,2048]{2,1,0:T(2,128)(2,1)S(1)}, bf16[14,2,2048]{2,1,0:T(2,128)(2,1)}, u32[]{:S(2)}, u32[]{:S(2)}) collective-permute-start(bf16[14,2,2048]{2,1,0:T(2,128)(2,1)S(1)} %copy-done.13), channel_id=1, source_target_pairs={{0,1},{1,2},{2,3},{3,0},{4,5},{5,6},{6,7},{7,4},{8,9},{9,10},{10,1... | collective-permute-start | bytes 344072 | tf_op jit(solution)/shard_map/ppermute | solution.py:411
  46.8 1.1 %collective-permute-start.10 = (bf16[14,2,2048]{2,1,0:T(2,128)(2,1)S(1)}, bf16[14,2,2048]{2,1,0:T(2,128)(2,1)}, u32[]{:S(2)}, u32[]{:S(2)}) collective-permute-start(bf16[14,2,2048]{2,1,0:T(2,128)(2,1)S(1)} %copy-done.13), channel_id=1, source_target_pairs={{0,2},{1,3},{2,0},{3,1},{4,6},{5,7},{6,4},{7,5},{8,10},{9,11},{10,... | collective-permute-start | bytes 344072 | tf_op jit(solution)/shard_map/ppermute | solution.py:411
  47.9 2.8 %collective-permute-start.11 = (bf16[14,2,2048]{2,1,0:T(2,128)(2,1)S(1)}, bf16[14,2,2048]{2,1,0:T(2,128)(2,1)}, u32[]{:S(2)}, u32[]{:S(2)}) collective-permute-start(bf16[14,2,2048]{2,1,0:T(2,128)(2,1)S(1)} %copy-done.13), channel_id=1, source_target_pairs={{0,3},{1,0},{2,1},{3,2},{4,7},{5,4},{6,5},{7,6},{8,11},{9,8},{10,9... | collective-permute-start | bytes 344072 | tf_op jit(solution)/shard_map/ppermute | solution.py:411
  51.6 1.4 %fusion.16 = f32[12,2,2,256]{3,1,2,0:T(2,128)S(1)} fusion(bf16[12,2,64,256]{3,2,1,0:T(8,128)(2,1)} %gather_fusion.1, pred[12]{0:T(512)(128)(4,1)S(1)} %get-tuple-element.104, bf16[12,2,2,64]{3,2,1,0:T(2,128)(2,1)S(1)} %reshape.373), kind=kOutput, calls=%fused_computation.19 | convolution fusion | flops 1978368 | bytes 841740 | tf_op jit(solution)/shard_map/gnot,gote->gnoe/dot_general | solution.py:507
  56.2 2.7 %fusion.60 = (f32[12,2,2,8]{3,1,2,0:T(2,128)}, f32[12,2,2,8,128]{4,3,1,2,0:T(8,128)}) fusion(bf16[12,128,2,256]{3,1,2,0:T(8,128)(2,1)S(1)} %copy.121, pred[12,128]{1,0:T(8,128)(4,1)S(1)} %iota_compare_fusion, bf16[14,2,16,128]{3,2,1,0:T(8,128)(2,1)} %param.14), kind=kOutput, calls=%fused_computation.142 | convolution fusion | flops 12729984 | bytes 1084928 | tf_op jit(solution)/shard_map/msgjd,mcgd->msgjc/dot_general | solution.py:45
  59.6 2.3 %collective-permute-start.21 = (bf16[2,64,2048]{2,1,0:T(8,128)(2,1)}, bf16[2,64,2048]{2,1,0:T(8,128)(2,1)S(1)}, u32[]{:S(2)}, u32[]{:S(2)}) collective-permute-start(bf16[2,64,2048]{2,1,0:T(8,128)(2,1)} %get-tuple-element.53), channel_id=1, source_target_pairs={{0,8},{4,12},{8,0},{12,4},{1,9},{5,13},{9,1},{13,5},{2,10},{6,14},... | collective-permute-start | bytes 1572872 | tf_op jit(solution)/shard_map/ppermute | solution.py:408
  62.4 1.5 %pad_maximum_fusion = bf16[14,2,8192]{2,1,0:T(2,128)(2,1)S(1)} fusion(bf16[14,2,2048]{2,1,0:T(2,128)(2,1)} %collective-permute-done.11, bf16[14,2,2048]{2,1,0:T(2,128)(2,1)} %collective-permute-done.10, bf16[14,2,2048]{2,1,0:T(2,128)(2,1)} %collective-permute-done.9, bf16[14,2,2048]{2,1,0:T(2,128)(2,1)S(1)} %copy-done.13), kind=kLoop, calls=%fused_computation.38 | loop fusion | flops 1835008 | bytes 917504 | tf_op jit(solution)/shard_map/concatenate | solution.py:491
  63.9 1.6 %gather_fusion = bf16[4,14,2,2048]{3,2,1,0:T(2,128)(2,1)S(1)} fusion(bf16[14,2,4,2048]{3,1,2,0:T(2,128)(2,1)S(1)} %bitcast.119, s32[1024]{0:T(1024)} %pad_clamp_fusion.2), kind=kCustom, calls=%fused_computation | custom fusion | bytes 917520 | tf_op jit(solution)/shard_map/jit(_take)/gather | solution.py:494
  66.5 5.1 %fusion = f32[14,2,2,256]{3,0,2,1:T(8,128)S(1)} fusion(bf16[8192,2,256]{2,1,0:T(2,128)(2,1)} %param.16, bf16[14,2,8192,1]{2,1,0,3:T(2,128)(2,1)S(1)} %fusion.27), kind=kOutput, calls=%fused_computation.3 | convolution fusion | flops 234881024 | bytes 8904704 | tf_op jit(solution)/shard_map/msd,dgc->msgc/dot_general | solution.py:495
  75.8 3.4 %shard_map.167 = (f32[2,16,128]{2,1,0:T(8,128)}, bf16[2,2,64,256]{3,2,1,0:T(8,128)(2,1)}) custom-call(s32[2,4]{1,0:T(2,128)} %bitcast.128, s32[16]{0:T(128)} %holder_ref.7, s32[1,16]{1,0:T(1,128)} %bitcast.134, bf16[16,2048]{1,0:T(8,128)(2,1)} %pad.4.hid_ref, bf16[2,64,2048]{2,1,0:T(8,128)(2,1)} %copy-done.9, bf16[2,64,2048]{2,1,0:T(8,128)(2,1)} %collective-permute-done.z2, ...), custom_call_target="tpu_custom_call" | custom-call | flops 16777216 | bytes 1310720 | tf_op jit(solution)/shard_map/pallas_call | solution.py:526
  80.9 1.5 %collective-permute-start.18 = (f32[4,128]{1,0:T(4,128)S(1)}, f32[4,128]{1,0:T(4,128)S(1)}, u32[]{:S(2)}, u32[]{:S(2)}) collective-permute-start(f32[4,128]{1,0:T(4,128)S(1)} %pad_maximum_fusion.2), channel_id=1, source_target_pairs={{0,1},{1,2},{2,3},{3,0},{4,5},{5,6},{6,7},{7,4},{8,9},{9,10},{10,1... | collective-permute-start | bytes 6152 | tf_op jit(solution)/shard_map/ppermute | solution.py:411
  84.5 3.3 %shard_map.168 = (bf16[4,2,64,2048]{3,2,1,0:T(8,128)(2,1)}, bf16[4,2,64,256]{3,2,1,0:T(8,128)(2,1)}) custom-call(s32[2,4]{1,0:T(2,128)} %bitcast.129, s32[16]{0:T(128)} %holder_ref.7, s32[1,16]{1,0:T(1,128)} %bitcast.135, bf16[2,64,2048]{2,1,0:T(8,128)(2,1)} %copy-done.9, bf16[2,64,2048]{2,1,0:T(8,128)(2,1)} %collective-permute-done.z2, ...), custom_call_target="tpu_custom_call" | custom-call | bytes 4718592 | tf_op jit(solution)/shard_map/pallas_call | solution.py:541
  (189 shorter events, 25.5 us)
Async XLA Ops:
  4.4 37.6 %collective-permute-start = (bf16[2,64,2048]{2,1,0:T(8,128)(2,1)}, bf16[2,64,2048]{2,1,0:T(8,128)(2,1)}, u32[]{:S(2)}, u32[]{:S(2)}) collective-permute-start(bf16[2,64,2048]{2,1,0:T(8,128)(2,1)} %get-tuple-element.70), channel_id=1, source_target_pairs={{0,8},{4,12},{8,0},{12,4},{1,9},{5,13},{9,1},{13,5},{2,10},{6,14},... | collective-permute-start | bytes 1572872 | tf_op jit(solution)/shard_map/ppermute | solution.py:408
  7.6 30.6 %collective-permute-start.1 = (bf16[2,2,64,2048]{3,2,1,0:T(8,128)(2,1)}, bf16[2,2,64,2048]{3,2,1,0:T(8,128)(2,1)S(1)}, u32[]{:S(2)}, u32[]{:S(2)}) collective-permute-start(bf16[2,2,64,2048]{3,2,1,0:T(8,128)(2,1)} %get-tuple-element.42), channel_id=1, source_target_pairs={{0,4},{4,0},{8,12},{12,8},{1,5},{5,1},{9,13},{13,9},{2,6},{6,2},{1... | collective-permute-start | bytes 3145736 | tf_op jit(solution)/shard_map/ppermute | solution.py:408
  7.6 3.2 %collective-permute-start.2 = (bf16[4,2,64,256]{3,2,1,0:T(8,128)(2,1)}, bf16[4,2,64,256]{3,2,1,0:T(8,128)(2,1)S(1)}, u32[]{:S(2)}, u32[]{:S(2)}) collective-permute-start(bf16[4,2,64,256]{3,2,1,0:T(8,128)(2,1)} %get-tuple-element.43), channel_id=1, source_target_pairs={{0,4},{4,0},{8,12},{12,8},{1,5},{5,1},{9,13},{13,9},{2,6},{6,2},{1... | collective-permute-start | bytes 786440 | tf_op jit(solution)/shard_map/ppermute | solution.py:408
  8.1 3.5 %collective-permute-start.3 = (bf16[2,64,2048]{2,1,0:T(8,128)(2,1)}, bf16[2,64,2048]{2,1,0:T(8,128)(2,1)S(1)}, u32[]{:S(2)}, u32[]{:S(2)}) collective-permute-start(bf16[2,64,2048]{2,1,0:T(8,128)(2,1)} %get-tuple-element.46), channel_id=1, source_target_pairs={{0,4},{4,0},{8,12},{12,8},{1,5},{5,1},{9,13},{13,9},{2,6},{6,2},{1... | collective-permute-start | bytes 1572872 | tf_op jit(solution)/shard_map/ppermute | solution.py:408
  15.3 22.3 %copy-start.30 = (bf16[128,2,256]{2,1,0:T(2,128)(2,1)S(1)}, bf16[128,2,256]{2,1,0:T(2,128)(2,1)}, u32[]{:S(2)}) copy-start(bf16[128,2,256]{2,1,0:T(2,128)(2,1)} %get-tuple-element.68) | copy-start | bytes 393220
  15.3 15.6 %collective-permute-start.4 = (bf16[2,64,2048]{2,1,0:T(8,128)(2,1)}, bf16[2,64,2048]{2,1,0:T(8,128)(2,1)S(1)}, u32[]{:S(2)}, u32[]{:S(2)}) collective-permute-start(bf16[2,64,2048]{2,1,0:T(8,128)(2,1)} %get-tuple-element.47), channel_id=1, source_target_pairs={{0,8},{4,12},{8,0},{12,4},{1,9},{5,13},{9,1},{13,5},{2,10},{6,14},... | collective-permute-start | bytes 1572872 | tf_op jit(solution)/shard_map/ppermute | solution.py:408
  19.7 31.0 %copy-start = (s32[48]{0:T(128)S(1)}, s32[48]{0:T(128)}, u32[]{:S(2)}) copy-start(s32[48]{0:T(128)} %param.19) | copy-start | bytes 580
  19.8 12.7 %collective-permute-start.8 = (f32[24,128]{1,0:T(8,128)S(1)}, f32[24,128]{1,0:T(8,128)S(1)}, u32[]{:S(2)}, u32[]{:S(2)}) collective-permute-start(f32[24,128]{1,0:T(8,128)S(1)} %reshape.372), channel_id=1, source_target_pairs={{0,3},{1,0},{2,1},{3,2},{4,7},{5,4},{6,5},{7,6},{8,11},{9,8},{10,9... | collective-permute-start | bytes 36872 | tf_op jit(solution)/shard_map/ppermute | solution.py:411
  23.7 14.0 %collective-permute-start.7 = (f32[24,128]{1,0:T(8,128)S(1)}, f32[24,128]{1,0:T(8,128)S(1)}, u32[]{:S(2)}, u32[]{:S(2)}) collective-permute-start(f32[24,128]{1,0:T(8,128)S(1)} %reshape.372), channel_id=1, source_target_pairs={{0,2},{1,3},{2,0},{3,1},{4,6},{5,7},{6,4},{7,5},{8,10},{9,11},{10,... | collective-permute-start | bytes 36872 | tf_op jit(solution)/shard_map/ppermute | solution.py:411
  30.9 6.8 %collective-permute-start.6 = (f32[24,128]{1,0:T(8,128)S(1)}, f32[24,128]{1,0:T(8,128)S(1)}, u32[]{:S(2)}, u32[]{:S(2)}) collective-permute-start(f32[24,128]{1,0:T(8,128)S(1)} %reshape.372), channel_id=1, source_target_pairs={{0,1},{1,2},{2,3},{3,0},{4,5},{5,6},{6,7},{7,4},{8,9},{9,10},{10,1... | collective-permute-start | bytes 36872 | tf_op jit(solution)/shard_map/ppermute | solution.py:411
  32.6 12.6 %collective-permute-start.5 = (bf16[4,2,64,256]{3,2,1,0:T(8,128)(2,1)}, bf16[4,2,64,256]{3,2,1,0:T(8,128)(2,1)S(1)}, u32[]{:S(2)}, u32[]{:S(2)}) collective-permute-start(bf16[4,2,64,256]{3,2,1,0:T(8,128)(2,1)} %get-tuple-element.51), channel_id=1, source_target_pairs={{0,8},{4,12},{8,0},{12,4},{1,9},{5,13},{9,1},{13,5},{2,10},{6,14},... | collective-permute-start | bytes 786440 | tf_op jit(solution)/shard_map/ppermute | solution.py:408
  37.6 6.2 %collective-permute-start.14 = (bf16[128,2,256]{2,1,0:T(2,128)(2,1)}, bf16[128,2,256]{2,1,0:T(2,128)(2,1)S(1)}, u32[]{:S(2)}, u32[]{:S(2)}) collective-permute-start(bf16[128,2,256]{2,1,0:T(2,128)(2,1)} %get-tuple-element.69), channel_id=1, source_target_pairs={{0,12},{4,8},{8,4},{12,0},{1,13},{5,9},{9,5},{13,1},{2,14},{6,10},... | collective-permute-start | bytes 393224 | tf_op jit(solution)/shard_map/ppermute | solution.py:408
  37.6 6.9 %collective-permute-start.13 = (bf16[128,2,256]{2,1,0:T(2,128)(2,1)S(1)}, bf16[128,2,256]{2,1,0:T(2,128)(2,1)S(1)}, u32[]{:S(2)}, u32[]{:S(2)}) collective-permute-start(bf16[128,2,256]{2,1,0:T(2,128)(2,1)S(1)} %copy-done.30), channel_id=1, source_target_pairs={{0,8},{4,12},{8,0},{12,4},{1,9},{5,13},{9,1},{13,5},{2,10},{6,14},... | collective-permute-start | bytes 393224 | tf_op jit(solution)/shard_map/ppermute | solution.py:408
  42.0 32.0 %collective-permute-start.16 = (bf16[2,64,2048]{2,1,0:T(8,128)(2,1)}, bf16[2,64,2048]{2,1,0:T(8,128)(2,1)S(1)}, u32[]{:S(2)}, u32[]{:S(2)}) collective-permute-start(bf16[2,64,2048]{2,1,0:T(8,128)(2,1)} %collective-permute-done.z2), channel_id=1, source_target_pairs={{0,4},{4,0},{8,12},{12,8},{1,5},{5,1},{9,13},{13,9},{2,6},{6,2},{1... | collective-permute-start | bytes 1572872 | tf_op jit(solution)/shard_map/ppermute | solution.py:408
  43.5 30.6 %collective-permute-start.17 = (bf16[2,64,2048]{2,1,0:T(8,128)(2,1)}, bf16[2,64,2048]{2,1,0:T(8,128)(2,1)S(1)}, u32[]{:S(2)}, u32[]{:S(2)}) collective-permute-start(bf16[2,64,2048]{2,1,0:T(8,128)(2,1)} %get-tuple-element.45), channel_id=1, source_target_pairs={{0,8},{4,12},{8,0},{12,4},{1,9},{5,13},{9,1},{13,5},{2,10},{6,14},... | collective-permute-start | bytes 1572872 | tf_op jit(solution)/shard_map/ppermute | solution.py:408
  45.2 14.3 %collective-permute-start.9 = (bf16[14,2,2048]{2,1,0:T(2,128)(2,1)S(1)}, bf16[14,2,2048]{2,1,0:T(2,128)(2,1)}, u32[]{:S(2)}, u32[]{:S(2)}) collective-permute-start(bf16[14,2,2048]{2,1,0:T(2,128)(2,1)S(1)} %copy-done.13), channel_id=1, source_target_pairs={{0,1},{1,2},{2,3},{3,0},{4,5},{5,6},{6,7},{7,4},{8,9},{9,10},{10,1... | collective-permute-start | bytes 344072 | tf_op jit(solution)/shard_map/ppermute | solution.py:411
  46.8 15.1 %collective-permute-start.10 = (bf16[14,2,2048]{2,1,0:T(2,128)(2,1)S(1)}, bf16[14,2,2048]{2,1,0:T(2,128)(2,1)}, u32[]{:S(2)}, u32[]{:S(2)}) collective-permute-start(bf16[14,2,2048]{2,1,0:T(2,128)(2,1)S(1)} %copy-done.13), channel_id=1, source_target_pairs={{0,2},{1,3},{2,0},{3,1},{4,6},{5,7},{6,4},{7,5},{8,10},{9,11},{10,... | collective-permute-start | bytes 344072 | tf_op jit(solution)/shard_map/ppermute | solution.py:411
  47.9 13.9 %collective-permute-start.11 = (bf16[14,2,2048]{2,1,0:T(2,128)(2,1)S(1)}, bf16[14,2,2048]{2,1,0:T(2,128)(2,1)}, u32[]{:S(2)}, u32[]{:S(2)}) collective-permute-start(bf16[14,2,2048]{2,1,0:T(2,128)(2,1)S(1)} %copy-done.13), channel_id=1, source_target_pairs={{0,3},{1,0},{2,1},{3,2},{4,7},{5,4},{6,5},{7,6},{8,11},{9,8},{10,9... | collective-permute-start | bytes 344072 | tf_op jit(solution)/shard_map/ppermute | solution.py:411
  59.6 24.1 %collective-permute-start.21 = (bf16[2,64,2048]{2,1,0:T(8,128)(2,1)}, bf16[2,64,2048]{2,1,0:T(8,128)(2,1)S(1)}, u32[]{:S(2)}, u32[]{:S(2)}) collective-permute-start(bf16[2,64,2048]{2,1,0:T(8,128)(2,1)} %get-tuple-element.53), channel_id=1, source_target_pairs={{0,8},{4,12},{8,0},{12,4},{1,9},{5,13},{9,1},{13,5},{2,10},{6,14},... | collective-permute-start | bytes 1572872 | tf_op jit(solution)/shard_map/ppermute | solution.py:408
  61.9 11.9 %collective-permute-start.12 = (bf16[128,2,256]{2,1,0:T(2,128)(2,1)}, bf16[128,2,256]{2,1,0:T(2,128)(2,1)S(1)}, u32[]{:S(2)}, u32[]{:S(2)}) collective-permute-start(bf16[128,2,256]{2,1,0:T(2,128)(2,1)} %get-tuple-element.67), channel_id=1, source_target_pairs={{0,4},{4,0},{8,12},{12,8},{1,5},{5,1},{9,13},{13,9},{2,6},{6,2},{1... | collective-permute-start | bytes 393224 | tf_op jit(solution)/shard_map/ppermute | solution.py:408
  61.9 12.1 %collective-permute-start.15 = (bf16[2,64,2048]{2,1,0:T(8,128)(2,1)}, bf16[2,64,2048]{2,1,0:T(8,128)(2,1)S(1)}, u32[]{:S(2)}, u32[]{:S(2)}) collective-permute-start(bf16[2,64,2048]{2,1,0:T(8,128)(2,1)} %get-tuple-element.70), channel_id=1, source_target_pairs={{0,4},{4,0},{8,12},{12,8},{1,5},{5,1},{9,13},{13,9},{2,6},{6,2},{1... | collective-permute-start | bytes 1572872 | tf_op jit(solution)/shard_map/ppermute | solution.py:408
  80.0 7.8 %collective-permute-start.20 = (f32[4,128]{1,0:T(4,128)S(1)}, f32[4,128]{1,0:T(4,128)S(1)}, u32[]{:S(2)}, u32[]{:S(2)}) collective-permute-start(f32[4,128]{1,0:T(4,128)S(1)} %pad_maximum_fusion.2), channel_id=1, source_target_pairs={{0,3},{1,0},{2,1},{3,2},{4,7},{5,4},{6,5},{7,6},{8,11},{9,8},{10,9... | collective-permute-start | bytes 6152 | tf_op jit(solution)/shard_map/ppermute | solution.py:411
  80.5 7.3 %collective-permute-start.19 = (f32[4,128]{1,0:T(4,128)S(1)}, f32[4,128]{1,0:T(4,128)S(1)}, u32[]{:S(2)}, u32[]{:S(2)}) collective-permute-start(f32[4,128]{1,0:T(4,128)S(1)} %pad_maximum_fusion.2), channel_id=1, source_target_pairs={{0,2},{1,3},{2,0},{3,1},{4,6},{5,7},{6,4},{7,5},{8,10},{9,11},{10,... | collective-permute-start | bytes 6152 | tf_op jit(solution)/shard_map/ppermute | solution.py:411
  80.9 6.9 %collective-permute-start.18 = (f32[4,128]{1,0:T(4,128)S(1)}, f32[4,128]{1,0:T(4,128)S(1)}, u32[]{:S(2)}, u32[]{:S(2)}) collective-permute-start(f32[4,128]{1,0:T(4,128)S(1)} %pad_maximum_fusion.2), channel_id=1, source_target_pairs={{0,1},{1,2},{2,3},{3,0},{4,5},{5,6},{6,7},{7,4},{8,9},{9,10},{10,1... | collective-permute-start | bytes 6152 | tf_op jit(solution)/shard_map/ppermute | solution.py:411
  (31 other events, 182.9 us)

commit v4 on v3

--- a/solution.py
+++ b/solution.py
@@ -208,6 +208,7 @@
 
 
 PAIRED = 4
+TENSORS = 4
 
 
 def needed_first(adapter_ref, dest):
@@ -266,7 +267,7 @@
 
 
 def pack_kernel(spans, slots, from_hbm, slot_hbm, adapter_hbm, holder_hbm, a_ref, b_ref, kv_ref,
-                z_out, u0_out, u12_out, b_out, k1_out, k2_out, k3_out,
+                z_out, u_out, b_out, k1_out, k2_out, k3_out,
                 from_ref, slot_ref, adapter_ref, holder_ref, a_stage, b_stage, k_stage, small_sems, sems):
     me = lax.axis_index("replica")
     small = [
@@ -281,7 +282,7 @@
         copy.wait()
     staged = Staged(sems)
     order, _ = needed_first(adapter_ref, me ^ 3)
-    outs = (z_out, u0_out, u12_out.at[0], u12_out.at[1])
+    outs = [z_out] + [u_out.at[j] for j in range(COPIES - 1)]
     for j, c in enumerate([0] + order):
         staged.go([(None, a_ref.at[held_slot(holder_ref, spans, slots, me, c)])], a_stage.at[j], outs[j])
         if j == 0:
@@ -307,8 +308,7 @@
         return [(mine, store.at[holder % slots]), (jnp.logical_not(mine), core)]
 
     for i, j in enumerate(places):
-        core = core_a if len(core_a.shape) == 3 else core_a.at[i]
-        staged.go(options(order[j], a_ref, core), a_stage.at[i], outs[i])
+        staged.go(options(order[j], a_ref, core_a.at[j]), a_stage.at[i], outs[i])
     for c in range(copies):
         staged.go(options(c, b_ref, core_b.at[c]), b_stage.at[c], outs[-1].at[c])
     staged.finish()
@@ -339,11 +339,11 @@
     return options
 
 
-def arrive_kernel(spans, slots, adapter_ref, holder_ref, dest_ref, hid_ref, z1, z2, z3, u0, u12, f0, f1, cb, xb,
+def arrive_kernel(spans, slots, adapter_ref, holder_ref, dest_ref, hid_ref, z1, z2, z3, u, f0, f1, cb, xb,
                   out_ref, b_out, units, sems):
     me = lax.axis_index("replica")
     options = sources(
-        spans, slots, adapter_ref, holder_ref, dest_ref, (z1, z2, z3), (u0, u12.at[0], u12.at[1]), (f0, f1), cb, xb
+        spans, slots, adapter_ref, holder_ref, dest_ref, (z1, z2, z3), [u.at[j] for j in range(COPIES - 1)], (f0, f1), cb, xb
     )
     staged = Staged(sems)
     for a in range(2):
@@ -357,10 +357,10 @@
         staged.arrived(2 * a + 1)
 
 
-def install_kernel(spans, slots, adapter_ref, holder_ref, dest_ref, z1, z2, z3, u0, u12, f0, f1, f2, cb, xb,
+def install_kernel(spans, slots, adapter_ref, holder_ref, dest_ref, z1, z2, z3, u, f0, f1, f2, cb, xb,
                    a_out, b_out, a_stage, b_stage, sems):
     options = sources(
-        spans, slots, adapter_ref, holder_ref, dest_ref, (z1, z2, z3), (u0, u12.at[0], u12.at[1]), (f0, f1, f2), cb, xb
+        spans, slots, adapter_ref, holder_ref, dest_ref, (z1, z2, z3), [u.at[j] for j in range(COPIES - 1)], (f0, f1, f2), cb, xb
     )
     staged = Staged(sems)
     for c in range(COPIES):
@@ -391,7 +391,6 @@
     hot_dest,
 ):
     me = lax.axis_index("replica")
-    tensors = lax.axis_size("tensor")
     tensor_index = lax.axis_index("tensor")
     resident, arrive = kv_cache.shape[0], arrival_from.shape[1]
     requests, steps, width = hidden.shape
@@ -407,8 +406,8 @@
     def swap(array, k):
         return lax.ppermute(array, "replica", [(i, i ^ k) for i in range(PAIRED)])
 
-    def shift(array, k):
-        return lax.ppermute(array, "tensor", [(i, (i + k) % tensors) for i in range(tensors)])
+    def mirror(array, k):
+        return lax.ppermute(array, "tensor", [(i, i ^ k) for i in range(TENSORS)])
 
     def cost(bytes_accessed, flops=0):
         return pl.CostEstimate(flops=flops, bytes_accessed=bytes_accessed, transcendentals=0)
@@ -418,14 +417,14 @@
     plan = (arrival_adapter.T, hot_holder, hot_dest.T)
     leave = (arrival_from.T, arrival_slot.T)
 
-    z, u0, u12, b_all, k1, k2, k3 = pl.pallas_call(
+    z, u, b_all, k1, k2, k3 = pl.pallas_call(
         functools.partial(pack_kernel, spans, slots),
         out_shape=(
-            shaped(*unit_a), shaped(*unit_a), shaped(2, *unit_a), shaped(COPIES, *unit_b),
+            shaped(*unit_a), shaped(COPIES - 1, *unit_a), shaped(COPIES, *unit_b),
             shaped(*unit_k), shaped(*unit_k), shaped(*unit_k),
         ),
         in_specs=[ANY] * 7,
-        out_specs=(ANY,) * 7,
+        out_specs=(ANY,) * 6,
         scratch_shapes=[pltpu.SMEM(x.shape, x.dtype) for x in leave + plan[:2]]
         + [
             pltpu.VMEM((COPIES,) + unit_a, kind),
@@ -437,9 +436,15 @@
         cost_estimate=cost(8 * size_a + 8 * size_b),
     )(*leave, *plan[:2], store_a, store_b, kv_cache)
     z2 = swap(z, 2)
-    core_u0, core_b = swap(u0, 1), swap(b_all, 1)
-    core_u12 = swap(u12, 1)
-    u0, hidden = lax.optimization_barrier((u0, hidden))
+    core_u, core_b = swap(u, 1), swap(b_all, 1)
+    far = (swap(k2, 2), swap(k3, 3))
+
+    u, hidden = lax.optimization_barrier((u, hidden))
+    own_adapter = lax.dynamic_slice_in_dim(resident_adapter, me * resident, resident)
+    every = jnp.einsum("msd,epkd->msepk", hidden[:resident], store_a, preferred_element_type=jnp.float32)
+    is_own = own_adapter[:, None] == jnp.arange(slots, dtype=jnp.int32)[None, :]
+    part_own = jnp.sum(jnp.where(is_own[:, None, :, None, None], every, 0.0), axis=2)
+    part_own, core_u = lax.optimization_barrier((part_own, core_u))
 
     def pick(places, copies, core):
         out = pl.pallas_call(
@@ -456,42 +461,32 @@
         )(*plan, store_a, store_b, core, core_b)
         return out
 
-    to0, to_b = pick((0,), COPIES, core_u0)
+    to0, to1, to2, to_b = pick((0, 1, 2), COPIES, core_u)
     f0 = swap(to0, 2)
-    to1, to2 = pick((1, 2), 0, core_u12)
-
-    z2, to1 = lax.optimization_barrier((z2, to1))
-    f1 = swap(to1, 2)
-    f0, to_b, k2, k3 = lax.optimization_barrier((f0, to_b, k2, k3))
-    far_b = swap(to_b, 2)
-    far = (swap(k2, 2), swap(k3, 3))
-    far_b, to2 = lax.optimization_barrier((far_b, to2))
-    f2 = swap(to2, 2)
-
-    own_adapter = lax.dynamic_slice_in_dim(resident_adapter, me * resident, resident)
-    every = jnp.einsum("msd,epkd->msepk", hidden[:resident], store_a, preferred_element_type=jnp.float32)
-    is_own = own_adapter[:, None] == jnp.arange(slots, dtype=jnp.int32)[None, :]
-    part_own = jnp.sum(jnp.where(is_own[:, None, :, None, None], every, 0.0), axis=2)
-
-    _, part_own = lax.optimization_barrier((to0, part_own))
+
+    z2, far, to1, to_b = lax.optimization_barrier((z2, far, to1, to_b))
+    f1, far_b = swap(to1, 2), swap(to_b, 2)
+
+    _, part_own, hidden, lengths, kv_cache, queries = lax.optimization_barrier(
+        (to0, part_own, hidden, lengths, kv_cache, queries)
+    )
 
     def total(part):
         out = part
-        for k in range(1, tensors):
-            out = out + shift(part, k)
+        for k in (2, 1):
+            out = out + mirror(out, k)
         return out.astype(jnp.bfloat16)
 
     shrink_own = total(part_own.reshape(resident * steps, -1)).reshape(resident, steps, 2, -1)
-    _, _, _, shrink_own, hidden, lengths, kv_cache, queries = lax.optimization_barrier(
-        (to1, to2, z2, shrink_own, hidden, lengths, kv_cache, queries)
-    )
-    pieces = [hidden] + [shift(hidden, k) for k in range(1, tensors)]
-    pieces, z, k1 = lax.optimization_barrier((pieces, z, k1))
+    high, low = tensor_index >= 2, tensor_index % 2 == 1
+    other = mirror(hidden, 2)
+    halves = jnp.concatenate([jnp.where(high, other, hidden), jnp.where(high, hidden, other)], axis=2)
+    other = mirror(halves, 1)
+    even, odd = jnp.where(low, other, halves), jnp.where(low, halves, other)
+    whole = jnp.concatenate([even[..., :width], odd[..., :width], even[..., width:], odd[..., width:]], axis=2)
+    f0, whole, to2, z, k1 = lax.optimization_barrier((f0, whole, to2, z, k1))
+    f2 = swap(to2, 2)
     z1, z3, near = swap(z, 1), swap(z2, 1), swap(k1, 1)
-    whole = jnp.concatenate(pieces, axis=2)
-    whole = whole.reshape(requests, steps, tensors, width)
-    turn = (tensor_index - jnp.arange(tensors, dtype=jnp.int32)) % tensors
-    whole = jnp.take(whole, turn, axis=2).reshape(requests, steps, tensors * width)
     base = jnp.einsum("msd,dgc->msgc", whole, w_kv, preferred_element_type=jnp.float32)
 
     my_from = lax.dynamic_index_in_dim(arrival_from, me, 0, keepdims=False)
@@ -526,11 +521,11 @@
     part_new, up_new = pl.pallas_call(
         functools.partial(arrive_kernel, spans, slots),
         out_shape=(shaped(arrive, rows, math.prod(unit_a[:2]), dtype=jnp.float32), shaped(arrive, *unit_b)),
-        in_specs=[SMEM] * 3 + [VMEM] + [ANY] * 9,
+        in_specs=[SMEM] * 3 + [VMEM] + [ANY] * 8,
         out_specs=(VMEM, VMEM),
         scratch_shapes=[pltpu.VMEM((arrive,) + unit_a, kind), pltpu.SemaphoreType.DMA((2 * arrive,))],
         cost_estimate=cost(arrive * (size_a + 2 * size_b), 2 * arrive * rows * size_a // 2),
-    )(*plan, guests, z1, z2, z3, core_u0, core_u12, f0, f1, core_b, far_b)
+    )(*plan, guests, z1, z2, z3, core_u, f0, f1, core_b, far_b)
     part_new = jnp.concatenate([part_new[a, a * steps : (a + 1) * steps] for a in range(arrive)], axis=0)
     shrink_new = total(part_new).reshape(arrive, steps, 2, -1)
     fresh_new = fresh_rows(base[resident:], shrink_new, up_new, arrival_len)
@@ -541,7 +536,7 @@
     installed_a, installed_b = pl.pallas_call(
         functools.partial(install_kernel, spans, slots),
         out_shape=(shaped(COPIES, *unit_a), shaped(COPIES, *unit_b)),
-        in_specs=[SMEM] * 3 + [ANY] * 10,
+        in_specs=[SMEM] * 3 + [ANY] * 9,
         out_specs=(ANY, ANY),
         scratch_shapes=[
             pltpu.VMEM((COPIES,) + unit_a, kind),
@@ -549,7 +544,7 @@
             pltpu.SemaphoreType.DMA((4 * COPIES,)),
         ],
         cost_estimate=cost(8 * size_a + 8 * size_b),
-    )(*plan, z1, z2, z3, core_u0, core_u12, f0, f1, f2, core_b, far_b)
+    )(*plan, z1, z2, z3, core_u, f0, f1, f2, core_b, far_b)
     return (attn_out, new_kv, arrived, installed_a, installed_b)
 
 
@@ -576,5 +571,5 @@
         P(("parts", "replica"), None, None, "tensor"),
         P(("parts", "replica"), None, None, "tensor"),
     )
-    local = paired if mesh.shape["replica"] == PAIRED else general
+    local = paired if mesh.shape["replica"] == PAIRED and mesh.shape["tensor"] == TENSORS else general
     return jax.shard_map(local, mesh=mesh, in_specs=in_specs, out_specs=out_specs, check_vma=False)

time: 91.3 us -> 83.1 us (0.910)
  starting transfers between devices: 24.1 us -> 19.3 us
  Pallas kernels: 16.1 us -> 13.5 us
    ppermute x13 -> x12, waiting for transfers between devices: 9.33 us -> 0.03 us  [swap(): return lax.ppermute(array, 'replica', [(i, i ^ k) for i in range(PAIRED)])]
    ppermute x9 -> x6, waiting for transfers between devices: 0.02 us -> 8.78 us  [mirror(): return lax.ppermute(array, 'tensor', [(i, i ^ k) for i in range(TENSORS)])]
    ppermute x9 -> x6, starting transfers between devices: 13.5 us -> 9.45 us  [mirror(): return lax.ppermute(array, 'tensor', [(i, i ^ k) for i in range(TENSORS)])]
    optimization_barrier x3 -> x5, local copies, waits for them, and re-layouts: 0.33 us -> 4.26 us  [the longest x2 3.18 us: paired(): z2, far, to1, to_b = lax.optimization_barrier((z2, far, to1, to_b))]
    pallas_call x2 -> x1, Pallas kernels: 5.66 us -> 3.11 us  [pick(): pl.pallas_call(functools.partial(pick_kernel, spans, slots, places, copie...]
    gather x2 -> x0, local copies, waits for them, and re-layouts: 2 us -> none  [paired(): jnp.take(whole, turn, axis=2).reshape(requests, steps, tensors * width)]
    dot_general x2, matrix products: 2.96 us -> 1.57 us  [attend(): jnp.einsum('msgjd,mcgd->msgjc', grouped, stored[..., :head_length], prefe...]
    ppermute x3 -> x1, local copies, waits for them, and re-layouts: 1.35 us -> 0.02 us  [swap(): return lax.ppermute(array, 'replica', [(i, i ^ k) for i in range(PAIRED)])]
  transfers between devices with their start and end apart: 22 -> 18, of which waited for: 3 -> 3; matrix products, arithmetic and copies ran while one was open for 36% -> 39% of each run, Pallas kernels for 14% -> 12%
where the time goes in v4:
time: 83.1 us; the launch traced here: 82.3 us
  starting transfers between devices  19.3 us (23%)
  matrix products  15.7 us (19%)
  local copies, waits for them, and re-layouts  14.5 us (17%)
  Pallas kernels  13.5 us (16%)
  other arithmetic  9.16 us (11%)
  waiting for transfers between devices  8.81 us (11%)
  between operations  1.31 us (2%)
    ppermute x12, starting transfers between devices, swap(): return lax.ppermute(array, 'replica', [(i, i ^ k) for i in range(PAIRED)])  9.82 us
    ppermute x6, starting transfers between devices, mirror(): return lax.ppermute(array, 'tensor', [(i, i ^ k) for i in range(TENSORS)])  9.45 us
    ppermute x6, waiting for transfers between devices, mirror(): return lax.ppermute(array, 'tensor', [(i, i ^ k) for i in range(TENSORS)])  8.78 us
    unnamed x60, local copies, waits for them, and re-layouts  5.54 us
    dot_general x1, matrix products, paired(): jnp.einsum('msd,dgc->msgc', whole, w_kv, preferred_element_type=jnp.float32)  5.2 us
    dot_general x1, matrix products, paired(): jnp.einsum('msd,epkd->msepk', hidden[:resident], store_a, preferred_eleme...  4.86 us
    pallas_call x1, Pallas kernels, paired(): pl.pallas_call(functools.partial(pack_kernel, spans, slots), out_shape=(s...  3.72 us
    pallas_call x1, Pallas kernels, paired(): pl.pallas_call(functools.partial(arrive_kernel, spans, slots), out_shape=...  3.43 us
  transfers between devices with their start and end apart: 18, of which 3 were waited for; matrix products, arithmetic and copies ran while one was open for 39% of the time, Pallas kernels for 12%

profile of v4, /device:TPU:0, one launch (start us, length us, event | category | flops | bytes accessed | tf_op | source)
XLA Modules:
  0.0 82.3 jit_solution(384453564750382848)
XLA Ops:
  0.7 3.7 %shard_map.164 = (bf16[2,64,2048]{2,1,0:T(8,128)(2,1)}, bf16[3,2,64,2048]{3,2,1,0:T(8,128)(2,1)}, bf16[4,2,64,256]{3,2,1,0:T(8,128)(2,1)}, bf16[128,2,256]{2,1,0...) custom-call(s32[2,4]{1,0:T(2,128)} %bitcast.116, s32[2,4]{1,0:T(2,128)} %bitcast.117, ...), custom_call_target="tpu_custom_call" | custom-call | bytes 4718592 | tf_op jit(solution)/shard_map/pallas_call | solution.py:420
  4.4 3.0 %collective-permute-start.9 = (bf16[128,2,256]{2,1,0:T(2,128)(2,1)}, bf16[128,2,256]{2,1,0:T(2,128)(2,1)}, u32[]{:S(2)}, u32[]{:S(2)}) collective-permute-start(bf16[128,2,256]{2,1,0:T(2,128)(2,1)} %get-tuple-element.53), channel_id=1, source_target_pairs={{0,8},{4,12},{8,0},{12,4},{1,9},{5,13},{9,1},{13,5},{2,10},{6,14},... | collective-permute-start | bytes 393224 | tf_op jit(solution)/shard_map/ppermute | solution.py:407
  7.6 1.9 %collective-permute-start.8 = (bf16[2,64,2048]{2,1,0:T(8,128)(2,1)}, bf16[2,64,2048]{2,1,0:T(8,128)(2,1)}, u32[]{:S(2)}, u32[]{:S(2)}) collective-permute-start(bf16[2,64,2048]{2,1,0:T(8,128)(2,1)} %get-tuple-element.59), channel_id=1, source_target_pairs={{0,8},{4,12},{8,0},{12,4},{1,9},{5,13},{9,1},{13,5},{2,10},{6,14},... | collective-permute-start | bytes 1572872 | tf_op jit(solution)/shard_map/ppermute | solution.py:407
  10.5 1.5 %gather_fusion = bf16[12,2,64,256]{3,2,1,0:T(8,128)(2,1)} fusion(bf16[8,2,64,256]{3,2,1,0:T(8,128)(2,1)S(1)} %copy-done.2, s32[1024]{0:T(1024)S(1)} %pad_clamp_fusion.1), kind=kCustom, calls=%fused_computation | custom fusion | bytes 1572912 | tf_op jit(solution)/shard_map/jit(_take)/gather | solution.py:509
  13.6 4.9 %fusion.11 = f32[12,2,2,64]{3,0,2,1:T(8,128)} fusion(bf16[8,2,64,2048]{3,2,1,0:T(8,128)(2,1)} %a_ref.3, bf16[14,2,2048]{2,0,1:T(8,128)(2,1)S(1)} %copy.116, pred[12,8]{0,1:T(8,128)(4,1)S(1)} %iota_compare_fusion.1), kind=kOutput, calls=%fused_computation.13 | convolution fusion | flops 100709376 | bytes 4321376 | tf_op jit(solution)/shard_map/msd,epkd->msepk/dot_general | solution.py:444
  18.5 1.2 %copy-done.1 = bf16[3,2,64,2048]{3,2,1,0:T(8,128)(2,1)} copy-done((bf16[3,2,64,2048]{3,2,1,0:T(8,128)(2,1)}, bf16[3,2,64,2048]{3,2,1,0:T(8,128)(2,1)S(1)}, u32[]{:S(2)}) %copy-start.1) | copy-done | bytes 1572888
  19.7 3.1 %shard_map.165 = (bf16[2,64,2048]{2,1,0:T(8,128)(2,1)}, bf16[2,64,2048]{2,1,0:T(8,128)(2,1)}, bf16[2,64,2048]{2,1,0:T(8,128)(2,1)}, bf16[4,2,64,256]{3,2,1,0:T(8,128)(2,1)}) custom-call(s32[2,4]{1,0:T(2,128)} %bitcast.113, s32[16]{0:T(128)} %holder_ref.5, s32[1,16]{1,0:T(1,128)} %bitcast.118, bf16[8,2,64,2048]{3,2,1,0:T(8,128)(2,1)} %a_ref.3, ...), custom_call_target="tpu_custom_call" | custom-call | bytes 3670016 | tf_op jit(solution)/shard_map/pallas_call | solution.py:450
  24.5 2.6 %collective-permute-start.5 = (f32[24,128]{1,0:T(8,128)S(1)}, f32[24,128]{1,0:T(8,128)S(1)}, u32[]{:S(2)}, u32[]{:S(2)}) collective-permute-start(f32[24,128]{1,0:T(8,128)S(1)} %reshape.313), channel_id=1, source_target_pairs={{0,2},{1,3},{2,0},{3,1},{4,6},{5,7},{6,4},{7,5},{8,10},{9,11},{10,... | collective-permute-start | bytes 36872 | tf_op jit(solution)/shard_map/ppermute | solution.py:410
  27.3 1.4 %multiply_cosine_fusion = (f32[12,2,64]{2,0,1:T(8,128)S(1)}, f32[12,2,64]{2,0,1:T(8,128)}) fusion(f32[64]{0:T(128)} %copy-done.20, f32[12,2]{0,1:T(2,128)S(1)} %add_convert_fusion.5), kind=kLoop, calls=%fused_computation.74 | loop fusion | flops 1536 | bytes 12640 | tf_op jit(solution)/shard_map/cos | solution.py:23
  29.9 1.6 %copy.131 = bf16[128,2,256]{2,0,1:T(8,128)(2,1)} copy(bf16[128,2,256]{2,1,0:T(2,128)(2,1)} %collective-permute-done.9) | data formatting | bytes 262144 | tf_op jit(solution)/shard_map/optimization_barrier | solution.py:467
  31.5 1.6 %copy.132 = bf16[128,2,256]{2,0,1:T(8,128)(2,1)} copy(bf16[128,2,256]{2,1,0:T(2,128)(2,1)} %collective-permute-done.10) | data formatting | bytes 262144 | tf_op jit(solution)/shard_map/optimization_barrier | solution.py:467
  33.1 1.8 %collective-permute-start.14 = (bf16[4,2,64,256]{3,2,1,0:T(8,128)(2,1)}, bf16[4,2,64,256]{3,2,1,0:T(8,128)(2,1)S(1)}, u32[]{:S(2)}, u32[]{:S(2)}) collective-permute-start(bf16[4,2,64,256]{3,2,1,0:T(8,128)(2,1)} %get-tuple-element.63), channel_id=1, source_target_pairs={{0,8},{4,12},{8,0},{12,4},{1,9},{5,13},{9,1},{13,5},{2,10},{6,14},... | collective-permute-start | bytes 786440 | tf_op jit(solution)/shard_map/ppermute | solution.py:407
  35.5 2.0 %collective-permute-start.6 = (f32[24,128]{1,0:T(8,128)S(1)}, f32[24,128]{1,0:T(8,128)S(1)}, u32[]{:S(2)}, u32[]{:S(2)}) collective-permute-start(f32[24,128]{1,0:T(8,128)S(1)} %add.159), channel_id=1, source_target_pairs={{0,1},{1,0},{2,3},{3,2},{4,5},{5,4},{6,7},{7,6},{8,9},{9,8},{10,11... | collective-permute-start | bytes 36872 | tf_op jit(solution)/shard_map/ppermute | solution.py:410
  38.7 1.3 %collective-permute-done.6 = f32[24,128]{1,0:T(8,128)S(1)} collective-permute-done((f32[24,128]{1,0:T(8,128)S(1)}, f32[24,128]{1,0:T(8,128)S(1)}, u32[]{:S(2)}, u32[]{:S(2)}) %collective-permute-start.6) | collective-permute-done | bytes 12320 | tf_op jit(solution)/shard_map/ppermute | solution.py:410
  41.4 1.2 %collective-permute-start.4 = (bf16[14,2,4096]{2,1,0:T(2,128)(2,1)S(1)}, bf16[14,2,4096]{2,1,0:T(2,128)(2,1)S(1)}, u32[]{:S(2)}, u32[]{:S(2)}) collective-permute-start(bf16[14,2,4096]{2,1,0:T(2,128)(2,1)S(1)} %pad_maximum_fusion.1), channel_id=1, source_target_pairs={{0,1},{1,0},{2,3},{3,2},{4,5},{5,4},{6,7},{7,6},{8,9},{9,8},{10,11... | collective-permute-start | bytes 688136 | tf_op jit(solution)/shard_map/ppermute | solution.py:410
  42.6 1.4 %fusion.16 = f32[12,2,2,256]{3,1,2,0:T(2,128)S(1)} fusion(bf16[12,2,64,256]{3,2,1,0:T(8,128)(2,1)} %gather_fusion, pred[12]{0:T(512)(128)(4,1)} %get-tuple-element.96, bf16[12,2,2,64]{3,2,1,0:T(2,128)(2,1)S(1)} %reshape.314), kind=kOutput, calls=%fused_computation.18 | convolution fusion | flops 1978368 | bytes 841740 | tf_op jit(solution)/shard_map/gnot,gote->gnoe/dot_general | solution.py:502
  44.2 5.3 %collective-permute-done.4 = bf16[14,2,4096]{2,1,0:T(2,128)(2,1)S(1)} collective-permute-done((bf16[14,2,4096]{2,1,0:T(2,128)(2,1)S(1)}, bf16[14,2,4096]{2,1,0:T(2,128)(2,1)S(1)}, u32[]{:S(2)}, u32[]{:S(2)}) %collective-permute-start.4) | collective-permute-done | bytes 229408 | tf_op jit(solution)/shard_map/ppermute | solution.py:410
  51.0 5.2 %fusion = f32[14,2,2,256]{3,0,2,1:T(8,128)S(1)} fusion(bf16[8192,2,256]{2,1,0:T(2,128)(2,1)} %param.16, bf16[14,2,8192,1]{2,1,0,3:T(2,128)(2,1)S(1)} %bitcast.109), kind=kOutput, calls=%fused_computation.2 | convolution fusion | flops 234881024 | bytes 8904704 | tf_op jit(solution)/shard_map/msd,dgc->msgc/dot_general | solution.py:490
  59.0 1.5 %collective-permute-start.17 = (bf16[2,64,2048]{2,1,0:T(8,128)(2,1)}, bf16[2,64,2048]{2,1,0:T(8,128)(2,1)S(1)}, u32[]{:S(2)}, u32[]{:S(2)}) collective-permute-start(bf16[2,64,2048]{2,1,0:T(8,128)(2,1)} %get-tuple-element.66), channel_id=1, source_target_pairs={{0,8},{4,12},{8,0},{12,4},{1,9},{5,13},{9,1},{13,5},{2,10},{6,14},... | collective-permute-start | bytes 1572872 | tf_op jit(solution)/shard_map/ppermute | solution.py:407
  62.4 3.4 %shard_map.166 = (f32[2,16,128]{2,1,0:T(8,128)}, bf16[2,2,64,256]{3,2,1,0:T(8,128)(2,1)}) custom-call(s32[2,4]{1,0:T(2,128)} %bitcast.114, s32[16]{0:T(128)} %holder_ref.5, s32[1,16]{1,0:T(1,128)} %bitcast.119, bf16[16,2048]{1,0:T(8,128)(2,1)} %pad.4.hid_ref, bf16[2,64,2048]{2,1,0:T(8,128)(2,1)} %copy-done.8, ...), custom_call_target="tpu_custom_call" | custom-call | flops 16777216 | bytes 1310720 | tf_op jit(solution)/shard_map/pallas_call | solution.py:521
  66.6 2.2 %collective-permute-start.15 = (f32[4,128]{1,0:T(4,128)S(1)}, f32[4,128]{1,0:T(4,128)S(1)}, u32[]{:S(2)}, u32[]{:S(2)}) collective-permute-start(f32[4,128]{1,0:T(4,128)S(1)} %pad_maximum_fusion.3), channel_id=1, source_target_pairs={{0,2},{1,3},{2,0},{3,1},{4,6},{5,7},{6,4},{7,5},{8,10},{9,11},{10,... | collective-permute-start | bytes 6152 | tf_op jit(solution)/shard_map/ppermute | solution.py:410
  69.0 2.2 %collective-permute-done.15 = f32[4,128]{1,0:T(4,128)S(1)} collective-permute-done((f32[4,128]{1,0:T(4,128)S(1)}, f32[4,128]{1,0:T(4,128)S(1)}, u32[]{:S(2)}, u32[]{:S(2)}) %collective-permute-start.15) | collective-permute-done | bytes 2080 | tf_op jit(solution)/shard_map/ppermute | solution.py:410
  71.2 1.5 %collective-permute-start.16 = (f32[4,128]{1,0:T(4,128)S(1)}, f32[4,128]{1,0:T(4,128)S(1)}, u32[]{:S(2)}, u32[]{:S(2)}) collective-permute-start(f32[4,128]{1,0:T(4,128)S(1)} %fusion.54), channel_id=1, source_target_pairs={{0,1},{1,0},{2,3},{3,2},{4,5},{5,4},{6,7},{7,6},{8,9},{9,8},{10,11... | collective-permute-start | bytes 6152 | tf_op jit(solution)/shard_map/ppermute | solution.py:410
  75.4 3.3 %shard_map.167 = (bf16[4,2,64,2048]{3,2,1,0:T(8,128)(2,1)}, bf16[4,2,64,256]{3,2,1,0:T(8,128)(2,1)}) custom-call(s32[2,4]{1,0:T(2,128)} %bitcast.115, s32[16]{0:T(128)} %holder_ref.5, s32[1,16]{1,0:T(1,128)} %bitcast.120, bf16[2,64,2048]{2,1,0:T(8,128)(2,1)} %copy-done.8, bf16[2,64,2048]{2,1,0:T(8,128)(2,1)} %collective-permute-done.8.z2, ...), custom_call_target="tpu_custom_call" | custom-call | bytes 4718592 | tf_op jit(solution)/shard_map/pallas_call | solution.py:536
  (170 shorter events, 22.2 us)
Async XLA Ops:
  0.7 11.3 %copy-start.12 = (bf16[14,2,2048]{2,1,0:T(2,128)(2,1)S(1)}, bf16[14,2,2048]{2,1,0:T(2,128)(2,1)}, u32[]{:S(2)}) copy-start(bf16[14,2,2048]{2,1,0:T(2,128)(2,1)} %param.13) | copy-start | bytes 344068
  4.4 25.5 %collective-permute-start.9 = (bf16[128,2,256]{2,1,0:T(2,128)(2,1)}, bf16[128,2,256]{2,1,0:T(2,128)(2,1)}, u32[]{:S(2)}, u32[]{:S(2)}) collective-permute-start(bf16[128,2,256]{2,1,0:T(2,128)(2,1)} %get-tuple-element.53), channel_id=1, source_target_pairs={{0,8},{4,12},{8,0},{12,4},{1,9},{5,13},{9,1},{13,5},{2,10},{6,14},... | collective-permute-start | bytes 393224 | tf_op jit(solution)/shard_map/ppermute | solution.py:407
  7.4 22.5 %collective-permute-start.10 = (bf16[128,2,256]{2,1,0:T(2,128)(2,1)}, bf16[128,2,256]{2,1,0:T(2,128)(2,1)}, u32[]{:S(2)}, u32[]{:S(2)}) collective-permute-start(bf16[128,2,256]{2,1,0:T(2,128)(2,1)} %get-tuple-element.54), channel_id=1, source_target_pairs={{0,12},{4,8},{8,4},{12,0},{1,13},{5,9},{9,5},{13,1},{2,14},{6,10},... | collective-permute-start | bytes 393224 | tf_op jit(solution)/shard_map/ppermute | solution.py:407
  7.4 11.1 %collective-permute-start.1 = (bf16[4,2,64,256]{3,2,1,0:T(8,128)(2,1)}, bf16[4,2,64,256]{3,2,1,0:T(8,128)(2,1)S(1)}, u32[]{:S(2)}, u32[]{:S(2)}) collective-permute-start(bf16[4,2,64,256]{3,2,1,0:T(8,128)(2,1)} %get-tuple-element.40), channel_id=1, source_target_pairs={{0,4},{4,0},{8,12},{12,8},{1,5},{5,1},{9,13},{13,9},{2,6},{6,2},{1... | collective-permute-start | bytes 786440 | tf_op jit(solution)/shard_map/ppermute | solution.py:407
  7.6 22.3 %collective-permute-start.8 = (bf16[2,64,2048]{2,1,0:T(8,128)(2,1)}, bf16[2,64,2048]{2,1,0:T(8,128)(2,1)}, u32[]{:S(2)}, u32[]{:S(2)}) collective-permute-start(bf16[2,64,2048]{2,1,0:T(8,128)(2,1)} %get-tuple-element.59), channel_id=1, source_target_pairs={{0,8},{4,12},{8,0},{12,4},{1,9},{5,13},{9,1},{13,5},{2,10},{6,14},... | collective-permute-start | bytes 1572872 | tf_op jit(solution)/shard_map/ppermute | solution.py:407
  9.5 9.0 %collective-permute-start = (bf16[3,2,64,2048]{3,2,1,0:T(8,128)(2,1)}, bf16[3,2,64,2048]{3,2,1,0:T(8,128)(2,1)S(1)}, u32[]{:S(2)}, u32[]{:S(2)}) collective-permute-start(bf16[3,2,64,2048]{3,2,1,0:T(8,128)(2,1)} %get-tuple-element.37), channel_id=1, source_target_pairs={{0,4},{4,0},{8,12},{12,8},{1,5},{5,1},{9,13},{13,9},{2,6},{6,2},{1... | collective-permute-start | bytes 4718600 | tf_op jit(solution)/shard_map/ppermute | solution.py:407
  13.0 14.2 %copy-start.20 = (f32[64]{0:T(128)}, f32[64]{0:T(128)S(1)}, u32[]{:S(2)}) copy-start(f32[64]{0:T(128)S(1)} %negate_power_fusion) | copy-start | bytes 772
  18.5 16.6 %copy-start.3 = (bf16[12,128,2,256]{3,2,1,0:T(2,128)(2,1)S(1)}, bf16[12,128,2,256]{3,2,1,0:T(2,128)(2,1)}, u32[]{:S(2)}) copy-start(bf16[12,128,2,256]{3,2,1,0:T(2,128)(2,1)} %kv_ref.1) | copy-start | bytes 4718596
  22.9 14.6 %copy-start.26 = (bf16[14,2,16,128]{3,2,1,0:T(8,128)(2,1)S(1)}, bf16[14,2,16,128]{3,2,1,0:T(8,128)(2,1)}, u32[]{:S(2)}) copy-start(bf16[14,2,16,128]{3,2,1,0:T(8,128)(2,1)} %param.14) | copy-start | bytes 344068
  24.5 10.9 %collective-permute-start.5 = (f32[24,128]{1,0:T(8,128)S(1)}, f32[24,128]{1,0:T(8,128)S(1)}, u32[]{:S(2)}, u32[]{:S(2)}) collective-permute-start(f32[24,128]{1,0:T(8,128)S(1)} %reshape.313), channel_id=1, source_target_pairs={{0,2},{1,3},{2,0},{3,1},{4,6},{5,7},{6,4},{7,5},{8,10},{9,11},{10,... | collective-permute-start | bytes 36872 | tf_op jit(solution)/shard_map/ppermute | solution.py:410
  29.4 21.6 %collective-permute-start.2 = (bf16[2,64,2048]{2,1,0:T(8,128)(2,1)}, bf16[2,64,2048]{2,1,0:T(8,128)(2,1)S(1)}, u32[]{:S(2)}, u32[]{:S(2)}) collective-permute-start(bf16[2,64,2048]{2,1,0:T(8,128)(2,1)} %get-tuple-element.41), channel_id=1, source_target_pairs={{0,8},{4,12},{8,0},{12,4},{1,9},{5,13},{9,1},{13,5},{2,10},{6,14},... | collective-permute-start | bytes 1572872 | tf_op jit(solution)/shard_map/ppermute | solution.py:407
  31.5 8.6 %collective-permute-start.3 = (bf16[14,2,2048]{2,1,0:T(2,128)(2,1)S(1)}, bf16[14,2,2048]{2,1,0:T(2,128)(2,1)}, u32[]{:S(2)}, u32[]{:S(2)}) collective-permute-start(bf16[14,2,2048]{2,1,0:T(2,128)(2,1)S(1)} %copy-done.12), channel_id=1, source_target_pairs={{0,2},{1,3},{2,0},{3,1},{4,6},{5,7},{6,4},{7,5},{8,10},{9,11},{10,... | collective-permute-start | bytes 344072 | tf_op jit(solution)/shard_map/ppermute | solution.py:410
  33.1 27.4 %collective-permute-start.14 = (bf16[4,2,64,256]{3,2,1,0:T(8,128)(2,1)}, bf16[4,2,64,256]{3,2,1,0:T(8,128)(2,1)S(1)}, u32[]{:S(2)}, u32[]{:S(2)}) collective-permute-start(bf16[4,2,64,256]{3,2,1,0:T(8,128)(2,1)} %get-tuple-element.63), channel_id=1, source_target_pairs={{0,8},{4,12},{8,0},{12,4},{1,9},{5,13},{9,1},{13,5},{2,10},{6,14},... | collective-permute-start | bytes 786440 | tf_op jit(solution)/shard_map/ppermute | solution.py:407
  34.9 25.7 %collective-permute-start.13 = (bf16[2,64,2048]{2,1,0:T(8,128)(2,1)}, bf16[2,64,2048]{2,1,0:T(8,128)(2,1)S(1)}, u32[]{:S(2)}, u32[]{:S(2)}) collective-permute-start(bf16[2,64,2048]{2,1,0:T(8,128)(2,1)} %get-tuple-element.62), channel_id=1, source_target_pairs={{0,8},{4,12},{8,0},{12,4},{1,9},{5,13},{9,1},{13,5},{2,10},{6,14},... | collective-permute-start | bytes 1572872 | tf_op jit(solution)/shard_map/ppermute | solution.py:407
  35.5 4.5 %collective-permute-start.6 = (f32[24,128]{1,0:T(8,128)S(1)}, f32[24,128]{1,0:T(8,128)S(1)}, u32[]{:S(2)}, u32[]{:S(2)}) collective-permute-start(f32[24,128]{1,0:T(8,128)S(1)} %add.159), channel_id=1, source_target_pairs={{0,1},{1,0},{2,3},{3,2},{4,5},{5,4},{6,7},{7,6},{8,9},{9,8},{10,11... | collective-permute-start | bytes 36872 | tf_op jit(solution)/shard_map/ppermute | solution.py:410
  40.0 20.6 %collective-permute-start.12 = (bf16[2,64,2048]{2,1,0:T(8,128)(2,1)}, bf16[2,64,2048]{2,1,0:T(8,128)(2,1)S(1)}, u32[]{:S(2)}, u32[]{:S(2)}) collective-permute-start(bf16[2,64,2048]{2,1,0:T(8,128)(2,1)} %collective-permute-done.8.z2), channel_id=1, source_target_pairs={{0,4},{4,0},{8,12},{12,8},{1,5},{5,1},{9,13},{13,9},{2,6},{6,2},{1... | collective-permute-start | bytes 1572872 | tf_op jit(solution)/shard_map/ppermute | solution.py:407
  41.4 8.1 %collective-permute-start.4 = (bf16[14,2,4096]{2,1,0:T(2,128)(2,1)S(1)}, bf16[14,2,4096]{2,1,0:T(2,128)(2,1)S(1)}, u32[]{:S(2)}, u32[]{:S(2)}) collective-permute-start(bf16[14,2,4096]{2,1,0:T(2,128)(2,1)S(1)} %pad_maximum_fusion.1), channel_id=1, source_target_pairs={{0,1},{1,0},{2,3},{3,2},{4,5},{5,4},{6,7},{7,6},{8,9},{9,8},{10,11... | collective-permute-start | bytes 688136 | tf_op jit(solution)/shard_map/ppermute | solution.py:410
  56.2 2.7 %collective-permute-start.7 = (bf16[128,2,256]{2,1,0:T(2,128)(2,1)S(1)}, bf16[128,2,256]{2,1,0:T(2,128)(2,1)S(1)}, u32[]{:S(2)}, u32[]{:S(2)}) collective-permute-start(bf16[128,2,256]{2,1,0:T(2,128)(2,1)S(1)} %copy-done.25), channel_id=1, source_target_pairs={{0,4},{4,0},{8,12},{12,8},{1,5},{5,1},{9,13},{13,9},{2,6},{6,2},{1... | collective-permute-start | bytes 393224 | tf_op jit(solution)/shard_map/ppermute | solution.py:407
  56.3 4.3 %collective-permute-start.11 = (bf16[2,64,2048]{2,1,0:T(8,128)(2,1)}, bf16[2,64,2048]{2,1,0:T(8,128)(2,1)S(1)}, u32[]{:S(2)}, u32[]{:S(2)}) collective-permute-start(bf16[2,64,2048]{2,1,0:T(8,128)(2,1)} %get-tuple-element.59), channel_id=1, source_target_pairs={{0,4},{4,0},{8,12},{12,8},{1,5},{5,1},{9,13},{13,9},{2,6},{6,2},{1... | collective-permute-start | bytes 1572872 | tf_op jit(solution)/shard_map/ppermute | solution.py:407
  58.2 10.6 %copy-start.14 = (bf16[128,2,256]{2,0,1:T(8,128)(2,1)S(1)}, bf16[128,2,256]{2,0,1:T(8,128)(2,1)}, u32[]{:S(2)}) copy-start(bf16[128,2,256]{2,0,1:T(8,128)(2,1)} %copy.131) | copy-start | bytes 393220
  59.0 15.6 %collective-permute-start.17 = (bf16[2,64,2048]{2,1,0:T(8,128)(2,1)}, bf16[2,64,2048]{2,1,0:T(8,128)(2,1)S(1)}, u32[]{:S(2)}, u32[]{:S(2)}) collective-permute-start(bf16[2,64,2048]{2,1,0:T(8,128)(2,1)} %get-tuple-element.66), channel_id=1, source_target_pairs={{0,8},{4,12},{8,0},{12,4},{1,9},{5,13},{9,1},{13,5},{2,10},{6,14},... | collective-permute-start | bytes 1572872 | tf_op jit(solution)/shard_map/ppermute | solution.py:407
  65.8 12.9 %copy-start.16 = (bf16[2,2,64,256]{3,2,1,0:T(8,128)(2,1)S(1)}, bf16[2,2,64,256]{3,2,1,0:T(8,128)(2,1)}, u32[]{:S(2)}) copy-start(bf16[2,2,64,256]{3,2,1,0:T(8,128)(2,1)} %get-tuple-element.64) | copy-start | bytes 393220
  66.6 4.5 %collective-permute-start.15 = (f32[4,128]{1,0:T(4,128)S(1)}, f32[4,128]{1,0:T(4,128)S(1)}, u32[]{:S(2)}, u32[]{:S(2)}) collective-permute-start(f32[4,128]{1,0:T(4,128)S(1)} %pad_maximum_fusion.3), channel_id=1, source_target_pairs={{0,2},{1,3},{2,0},{3,1},{4,6},{5,7},{6,4},{7,5},{8,10},{9,11},{10,... | collective-permute-start | bytes 6152 | tf_op jit(solution)/shard_map/ppermute | solution.py:410
  71.2 7.5 %collective-permute-start.16 = (f32[4,128]{1,0:T(4,128)S(1)}, f32[4,128]{1,0:T(4,128)S(1)}, u32[]{:S(2)}, u32[]{:S(2)}) collective-permute-start(f32[4,128]{1,0:T(4,128)S(1)} %fusion.54), channel_id=1, source_target_pairs={{0,1},{1,0},{2,3},{3,2},{4,5},{5,4},{6,7},{7,6},{8,9},{9,8},{10,11... | collective-permute-start | bytes 6152 | tf_op jit(solution)/shard_map/ppermute | solution.py:410
  (23 other events, 127.9 us)

commit v5 on v4

--- a/solution.py
+++ b/solution.py
@@ -445,6 +445,8 @@
     is_own = own_adapter[:, None] == jnp.arange(slots, dtype=jnp.int32)[None, :]
     part_own = jnp.sum(jnp.where(is_own[:, None, :, None, None], every, 0.0), axis=2)
     part_own, core_u = lax.optimization_barrier((part_own, core_u))
+    _, sent = lax.optimization_barrier((core_b, hidden))
+    other = mirror(sent, 2)
 
     def pick(places, copies, core):
         out = pl.pallas_call(
@@ -467,9 +469,8 @@
     z2, far, to1, to_b = lax.optimization_barrier((z2, far, to1, to_b))
     f1, far_b = swap(to1, 2), swap(to_b, 2)
 
-    _, part_own, hidden, lengths, kv_cache, queries = lax.optimization_barrier(
-        (to0, part_own, hidden, lengths, kv_cache, queries)
-    )
+    _, other, lengths, queries, k1 = lax.optimization_barrier((to0, other, lengths, queries, k1))
+    near = swap(k1, 1)
 
     def total(part):
         out = part
@@ -477,17 +478,15 @@
             out = out + mirror(out, k)
         return out.astype(jnp.bfloat16)
 
-    shrink_own = total(part_own.reshape(resident * steps, -1)).reshape(resident, steps, 2, -1)
     high, low = tensor_index >= 2, tensor_index % 2 == 1
-    other = mirror(hidden, 2)
-    halves = jnp.concatenate([jnp.where(high, other, hidden), jnp.where(high, hidden, other)], axis=2)
+    halves = jnp.concatenate([jnp.where(high, other, sent), jnp.where(high, sent, other)], axis=2)
     other = mirror(halves, 1)
     even, odd = jnp.where(low, other, halves), jnp.where(low, halves, other)
     whole = jnp.concatenate([even[..., :width], odd[..., :width], even[..., width:], odd[..., width:]], axis=2)
-    f0, whole, to2, z, k1 = lax.optimization_barrier((f0, whole, to2, z, k1))
+    base = jnp.einsum("msd,dgc->msgc", whole, w_kv, preferred_element_type=jnp.float32)
+    f0, base, to2, z, z2 = lax.optimization_barrier((f0, base, to2, z, z2))
     f2 = swap(to2, 2)
-    z1, z3, near = swap(z, 1), swap(z2, 1), swap(k1, 1)
-    base = jnp.einsum("msd,dgc->msgc", whole, w_kv, preferred_element_type=jnp.float32)
+    z1, z3 = swap(z, 1), swap(z2, 1)
 
     my_from = lax.dynamic_index_in_dim(arrival_from, me, 0, keepdims=False)
     my_slot = lax.dynamic_index_in_dim(arrival_slot, me, 0, keepdims=False)
@@ -507,10 +506,6 @@
         return jnp.concatenate([turned, raw[..., head_length:]], axis=-1).astype(jnp.bfloat16)
 
     up_own = jnp.take(store_b, own_adapter, axis=0)
-    fresh_own = fresh_rows(base[:resident], shrink_own, up_own, own_len)
-    stay_out = attend(queries[:resident], kv_cache, own_len, fresh_own)
-    stay_out = jnp.where(staying[:, None, None], stay_out, 0.0).astype(jnp.bfloat16)
-    stay_kv = jnp.where(staying[:, None, None, None], fresh_own, jnp.zeros((), jnp.bfloat16))
 
     way = (my_from ^ me)[:, None, None, None]
     arrived = jnp.where(way == 1, near[None], jnp.where(way == 2, far[0][None], far[1][None]))
@@ -526,13 +521,19 @@
         scratch_shapes=[pltpu.VMEM((arrive,) + unit_a, kind), pltpu.SemaphoreType.DMA((2 * arrive,))],
         cost_estimate=cost(arrive * (size_a + 2 * size_b), 2 * arrive * rows * size_a // 2),
     )(*plan, guests, z1, z2, z3, core_u, f0, f1, core_b, far_b)
-    part_new = jnp.concatenate([part_new[a, a * steps : (a + 1) * steps] for a in range(arrive)], axis=0)
-    shrink_new = total(part_new).reshape(arrive, steps, 2, -1)
-    fresh_new = fresh_rows(base[resident:], shrink_new, up_new, arrival_len)
-    move_out = attend(queries[resident:], arrived, arrival_len, fresh_new).astype(jnp.bfloat16)
-
-    attn_out = jnp.concatenate([stay_out, move_out], axis=0)
-    new_kv = jnp.concatenate([stay_kv, fresh_new], axis=0)
+    part = jnp.concatenate(
+        [part_own.reshape(resident * steps, -1)]
+        + [part_new[a, a * steps : (a + 1) * steps] for a in range(arrive)],
+        axis=0,
+    )
+    shrink = total(part).reshape(requests, steps, 2, -1)
+
+    seen = jnp.concatenate([own_len, arrival_len])
+    live = jnp.concatenate([staying, jnp.ones((arrive,), bool)])
+    fresh = fresh_rows(base, shrink, jnp.concatenate([up_own, up_new]), seen)
+    mixed = attend(queries, jnp.concatenate([kv_cache, arrived]), seen, fresh)
+    attn_out = jnp.where(live[:, None, None], mixed, 0.0).astype(jnp.bfloat16)
+    new_kv = jnp.where(live[:, None, None, None], fresh, jnp.zeros((), jnp.bfloat16))
     installed_a, installed_b = pl.pallas_call(
         functools.partial(install_kernel, spans, slots),
         out_shape=(shaped(COPIES, *unit_a), shaped(COPIES, *unit_b)),

time: 83.1 us -> 84.9 us (1.022)
  starting transfers between devices: 19.3 us -> 16.1 us
  matrix products: 15.7 us -> 12.7 us
  local copies, waits for them, and re-layouts: 14.5 us -> 17.5 us
  waiting for transfers between devices: 8.81 us -> 11.8 us
  other arithmetic: 9.16 us -> 10.9 us
    ppermute x12, waiting for transfers between devices: 0.03 us -> 5.32 us  [swap(): return lax.ppermute(array, 'replica', [(i, i ^ k) for i in range(PAIRED)])]
    ppermute x6 -> x4, starting transfers between devices: 9.45 us -> 6.38 us  [mirror(): return lax.ppermute(array, 'tensor', [(i, i ^ k) for i in range(TENSORS)])]
    ppermute x6 -> x4, waiting for transfers between devices: 8.78 us -> 6.47 us  [mirror(): return lax.ppermute(array, 'tensor', [(i, i ^ k) for i in range(TENSORS)])]
    concatenate x5 -> x3, other arithmetic: 1.63 us -> 0.11 us  [the longest x1 0.07 us: paired(): seen = jnp.concatenate([own_len, arrival_len])]
    dot_general x2 -> x1, matrix products: 1.55 us -> 0.25 us  [fresh_rows(): jnp.einsum('gnot,gote->gnoe', shrink, up, preferred_element_type=jnp.floa...]
    select_n x1, other arithmetic: 0.11 us -> 1.15 us  [paired(): jnp.where((row_ids[None, :] < arrival_len[:, None])[:, :, None, None], ar...]
    select_n x1 -> x2, other arithmetic: 0.01 us -> 1.02 us  [paired(): up_own = jnp.take(store_b, own_adapter, axis=0)]
    gather x1, local copies, waits for them, and re-layouts: 1.51 us -> 0.6 us  [paired(): up_own = jnp.take(store_b, own_adapter, axis=0)]
  transfers between devices with their start and end apart: 18 -> 16, of which waited for: 3 -> 4; matrix products, arithmetic and copies ran while one was open for 39% -> 41% of each run, Pallas kernels for 12% -> 12%
where the time goes in v5:
time: 84.9 us; the launch traced here: 83.9 us
  local copies, waits for them, and re-layouts  17.5 us (21%)
  starting transfers between devices  16.1 us (19%)
  Pallas kernels  13.8 us (16%)
  matrix products  12.7 us (15%)
  waiting for transfers between devices  11.8 us (14%)
  other arithmetic  10.9 us (13%)
  between operations  1.07 us (1%)
    ppermute x12, starting transfers between devices, swap(): return lax.ppermute(array, 'replica', [(i, i ^ k) for i in range(PAIRED)])  9.75 us
    ppermute x4, waiting for transfers between devices, mirror(): return lax.ppermute(array, 'tensor', [(i, i ^ k) for i in range(TENSORS)])  6.47 us
    unnamed x45, local copies, waits for them, and re-layouts  6.4 us
    ppermute x4, starting transfers between devices, mirror(): return lax.ppermute(array, 'tensor', [(i, i ^ k) for i in range(TENSORS)])  6.38 us
    dot_general x1, matrix products, paired(): jnp.einsum('msd,dgc->msgc', whole, w_kv, preferred_element_type=jnp.float32)  5.57 us
    ppermute x12, waiting for transfers between devices, swap(): return lax.ppermute(array, 'replica', [(i, i ^ k) for i in range(PAIRED)])  5.32 us
    dot_general x1, matrix products, paired(): jnp.einsum('msd,epkd->msepk', hidden[:resident], store_a, preferred_eleme...  4.85 us
    pallas_call x1, Pallas kernels, paired(): pl.pallas_call(functools.partial(pack_kernel, spans, slots), out_shape=(s...  3.74 us
  transfers between devices with their start and end apart: 16, of which 4 were waited for; matrix products, arithmetic and copies ran while one was open for 41% of the time, Pallas kernels for 12%

profile of v5, /device:TPU:0, one launch (start us, length us, event | category | flops | bytes accessed | tf_op | source)
XLA Modules:
  0.0 83.9 jit_solution(14923941172666230727)
XLA Ops:
  0.7 3.7 %shard_map.164 = (bf16[2,64,2048]{2,1,0:T(8,128)(2,1)}, bf16[3,2,64,2048]{3,2,1,0:T(8,128)(2,1)}, bf16[4,2,64,256]{3,2,1,0:T(8,128)(2,1)}, bf16[128,2,256]{2,1,0...) custom-call(s32[2,4]{1,0:T(2,128)} %bitcast.77, s32[2,4]{1,0:T(2,128)} %bitcast.78, ...), custom_call_target="tpu_custom_call" | custom-call | bytes 4718592 | tf_op jit(solution)/shard_map/pallas_call | solution.py:420
  5.0 2.9 %collective-permute-start.4 = (bf16[2,64,2048]{2,1,0:T(8,128)(2,1)}, bf16[2,64,2048]{2,1,0:T(8,128)(2,1)}, u32[]{:S(2)}, u32[]{:S(2)}) collective-permute-start(bf16[2,64,2048]{2,1,0:T(8,128)(2,1)} %get-tuple-element.58), channel_id=1, source_target_pairs={{0,8},{4,12},{8,0},{12,4},{1,9},{5,13},{9,1},{13,5},{2,10},{6,14},... | collective-permute-start | bytes 1572872 | tf_op jit(solution)/shard_map/ppermute | solution.py:407
  8.0 1.1 %collective-permute-start.6 = (bf16[128,2,256]{2,1,0:T(2,128)(2,1)}, bf16[128,2,256]{2,1,0:T(2,128)(2,1)}, u32[]{:S(2)}, u32[]{:S(2)}) collective-permute-start(bf16[128,2,256]{2,1,0:T(2,128)(2,1)} %get-tuple-element.48), channel_id=1, source_target_pairs={{0,12},{4,8},{8,4},{12,0},{1,13},{5,9},{9,5},{13,1},{2,14},{6,10},... | collective-permute-start | bytes 393224 | tf_op jit(solution)/shard_map/ppermute | solution.py:407
  10.9 4.8 %fusion.11 = f32[12,2,2,64]{3,0,2,1:T(8,128)} fusion(bf16[8,2,64,2048]{3,2,1,0:T(8,128)(2,1)} %a_ref.3, bf16[14,2,2048]{2,0,1:T(8,128)(2,1)S(1)} %copy.97, pred[12,8]{0,1:T(8,128)(4,1)S(1)} %iota_compare_fusion.1), kind=kOutput, calls=%fused_computation.15 | convolution fusion | flops 100709376 | bytes 4321376 | tf_op jit(solution)/shard_map/msd,epkd->msepk/dot_general | solution.py:444
  17.5 2.6 %collective-permute-start.2 = (bf16[14,2,2048]{2,0,1:T(8,128)(2,1)}, bf16[14,2,2048]{2,0,1:T(8,128)(2,1)}, u32[]{:S(2)}, u32[]{:S(2)}) collective-permute-start(bf16[14,2,2048]{2,0,1:T(8,128)(2,1)} %copy.98), channel_id=1, source_target_pairs={{0,2},{1,3},{2,0},{3,1},{4,6},{5,7},{6,4},{7,5},{8,10},{9,11},{10,... | collective-permute-start | bytes 344072 | tf_op jit(solution)/shard_map/ppermute | solution.py:410
  20.7 1.7 %copy.102 = bf16[12,128,2,256]{3,1,2,0:T(8,128)(2,1)S(1)} copy(bf16[12,128,2,256]{3,2,1,0:T(2,128)(2,1)} %kv_ref.1) | data formatting | bytes 3145728 | tf_op args[2]
  23.7 1.4 %pad.5.hid_ref = bf16[16,2048]{1,0:T(8,128)(2,1)} pad(bf16[4,2048]{1,0:T(4,128)(2,1)} %reshape.236, bf16[]{:T(256)} %constant.80.clone.1), padding=0_12x0_0 | pad | bytes 81922 | tf_op jit(solution)/shard_map/jit(_pad)/pad | solution.py:515
  26.4 1.2 %copy-done.2 = bf16[3,2,64,2048]{3,2,1,0:T(8,128)(2,1)} copy-done((bf16[3,2,64,2048]{3,2,1,0:T(8,128)(2,1)}, bf16[3,2,64,2048]{3,2,1,0:T(8,128)(2,1)S(1)}, u32[]{:S(2)}) %copy-start.2) | copy-done | bytes 1572888
  27.5 3.2 %shard_map.165 = (bf16[2,64,2048]{2,1,0:T(8,128)(2,1)}, bf16[2,64,2048]{2,1,0:T(8,128)(2,1)}, bf16[2,64,2048]{2,1,0:T(8,128)(2,1)}, bf16[4,2,64,256]{3,2,1,0:T(8,128)(2,1)}) custom-call(s32[2,4]{1,0:T(2,128)} %bitcast.74, s32[16]{0:T(128)} %holder_ref.5, s32[1,16]{1,0:T(1,128)} %bitcast.79, bf16[8,2,64,2048]{3,2,1,0:T(8,128)(2,1)} %a_ref.3, ...), custom_call_target="tpu_custom_call" | custom-call | bytes 3670016 | tf_op jit(solution)/shard_map/pallas_call | solution.py:452
  32.8 1.6 %collective-permute-start.8 = (bf16[14,2,4096]{2,0,1:T(8,128)(2,1)S(1)}, bf16[14,2,4096]{2,0,1:T(8,128)(2,1)}, u32[]{:S(2)}, u32[]{:S(2)}) collective-permute-start(bf16[14,2,4096]{2,0,1:T(8,128)(2,1)S(1)} %pad_maximum_fusion.1), channel_id=1, source_target_pairs={{0,1},{1,0},{2,3},{3,2},{4,5},{5,4},{6,7},{7,6},{8,9},{9,8},{10,11... | collective-permute-start | bytes 688136 | tf_op jit(solution)/shard_map/ppermute | solution.py:410
  34.5 1.2 %collective-permute-start.11 = (bf16[2,64,2048]{2,1,0:T(8,128)(2,1)}, bf16[2,64,2048]{2,1,0:T(8,128)(2,1)S(1)}, u32[]{:S(2)}, u32[]{:S(2)}) collective-permute-start(bf16[2,64,2048]{2,1,0:T(8,128)(2,1)} %get-tuple-element.61), channel_id=1, source_target_pairs={{0,8},{4,12},{8,0},{12,4},{1,9},{5,13},{9,1},{13,5},{2,10},{6,14},... | collective-permute-start | bytes 1572872 | tf_op jit(solution)/shard_map/ppermute | solution.py:407
  38.0 3.3 %collective-permute-done.8 = bf16[14,2,4096]{2,0,1:T(8,128)(2,1)} collective-permute-done((bf16[14,2,4096]{2,0,1:T(8,128)(2,1)S(1)}, bf16[14,2,4096]{2,0,1:T(8,128)(2,1)}, u32[]{:S(2)}, u32[]{:S(2)}) %collective-permute-start.8) | collective-permute-done | bytes 229408 | tf_op jit(solution)/shard_map/ppermute | solution.py:410
  41.3 1.0 %broadcast_select_fusion.2 = (bf16[14,2,4096]{2,0,1:T(8,128)(2,1)S(1)}, bf16[14,2,4096]{2,0,1:T(8,128)(2,1)S(1)}) fusion(bf16[14,2,4096]{2,0,1:T(8,128)(2,1)} %collective-permute-done.8, pred[]{:T(512)S(6)} %eq.70, bf16[14,2,2048]{2,0,1:T(8,128)(2,1)S(1)} %get-tuple-element.105, bf16[14,2,2048]{2,0,1:T(8,128)(2,1)S(1)} %get-tuple-element.104), kind=kLoop, calls=%fused_computation.41 | loop fusion | flops 688128 | bytes 917505 | tf_op jit(solution)/shard_map/jit(_where)/select_n | solution.py:484
  42.4 5.6 %fusion = f32[14,2,2,256]{3,0,2,1:T(8,128)} fusion(bf16[8192,2,256]{2,1,0:T(2,128)(2,1)} %param.16, bf16[14,2,2048]{2,0,1:T(8,128)(2,1)S(1)} %get-tuple-element.116, bf16[14,2,2048]{2,0,1:T(8,128)(2,1)S(1)} %get-tuple-element.101, bf16[14,2,2048]{2,0,1:T(8,128)(2,1)S(1)} %get-tuple-element.117, bf16[14,2,2048]{2,0,1:T(8,128)(2,1)S(1)} %get-tuple-element.100), kind=kOutput, calls=%fused_computation.2 | convolution fusion | flops 236716032 | bytes 8904704 | tf_op jit(solution)/shard_map/msd,dgc->msgc/dot_general | solution.py:486
  50.7 1.6 %copy.100 = bf16[128,2,256]{2,0,1:T(8,128)(2,1)} copy(bf16[128,2,256]{2,1,0:T(2,128)(2,1)} %collective-permute-done.5) | data formatting | bytes 262144 | tf_op jit(solution)/shard_map/optimization_barrier | solution.py:469
  52.3 1.6 %copy.101 = bf16[128,2,256]{2,0,1:T(8,128)(2,1)} copy(bf16[128,2,256]{2,1,0:T(2,128)(2,1)} %collective-permute-done.6) | data formatting | bytes 262144 | tf_op jit(solution)/shard_map/optimization_barrier | solution.py:469
  53.9 1.3 %iota_compare_fusion.3 = pred[2,128]{1,0:T(4,128)(4,1)} fusion(s32[2]{0:T(128)} %copy-done.19), kind=kLoop, calls=%fused_computation.89 | loop fusion | flops 256 | bytes 264 | tf_op jit(solution)/shard_map/lt | solution.py:513
  56.1 1.5 %collective-permute-start.15 = (bf16[2,64,2048]{2,1,0:T(8,128)(2,1)}, bf16[2,64,2048]{2,1,0:T(8,128)(2,1)}, u32[]{:S(2)}, u32[]{:S(2)}) collective-permute-start(bf16[2,64,2048]{2,1,0:T(8,128)(2,1)} %get-tuple-element.66), channel_id=1, source_target_pairs={{0,8},{4,12},{8,0},{12,4},{1,9},{5,13},{9,1},{13,5},{2,10},{6,14},... | collective-permute-start | bytes 1572872 | tf_op jit(solution)/shard_map/ppermute | solution.py:407
  57.6 5.1 %collective-permute-done.12.xb = bf16[4,2,64,256]{3,2,1,0:T(8,128)(2,1)S(1)} collective-permute-done((bf16[4,2,64,256]{3,2,1,0:T(8,128)(2,1)}, bf16[4,2,64,256]{3,2,1,0:T(8,128)(2,1)S(1)}, u32[]{:S(2)}, u32[]{:S(2)}) %collective-permute-start.12) | collective-permute-done | bytes 262176 | tf_op jit(solution)/shard_map/ppermute | solution.py:407
  63.8 3.4 %shard_map.166 = (f32[2,16,128]{2,1,0:T(8,128)}, bf16[2,2,64,256]{3,2,1,0:T(8,128)(2,1)}) custom-call(s32[2,4]{1,0:T(2,128)} %bitcast.75, s32[16]{0:T(128)} %holder_ref.5, s32[1,16]{1,0:T(1,128)} %bitcast.80, bf16[16,2048]{1,0:T(8,128)(2,1)} %pad.5.hid_ref, bf16[2,64,2048]{2,1,0:T(8,128)(2,1)} %collective-permute-done.9.z1, ...), custom_call_target="tpu_custom_call" | custom-call | flops 16777216 | bytes 1310720 | tf_op jit(solution)/shard_map/pallas_call | solution.py:516
  68.3 1.2 %select_select_fusion = bf16[2,128,2,256]{3,1,2,0:T(8,128)(2,1)S(1)} fusion(pred[2]{0:T(512)(128)(4,1)} %get-tuple-element.95, pred[2]{0:T(512)(128)(4,1)} %get-tuple-element.94, pred[2,128]{1,0:T(4,128)(4,1)} %iota_compare_fusion.3, bf16[128,2,256]{2,0,1:T(8,128)(2,1)} %copy.101, bf16[128,2,256]{2,0,1:T(8,128)(2,1)} %copy.100, bf16[128,2,256]{2,0,1:T(8,128)(2,1)} %copy.99), kind=kLoop, calls=%fused_computation.39 | loop fusion | flops 393216 | bytes 655620 | tf_op jit(solution)/shard_map/jit(_where)/select_n | solution.py:513
  69.5 3.1 %collective-permute-done.13 = f32[28,128]{1,0:T(8,128)S(1)} collective-permute-done((f32[28,128]{1,0:T(8,128)S(1)}, f32[28,128]{1,0:T(8,128)S(1)}, u32[]{:S(2)}, u32[]{:S(2)}) %collective-permute-start.13) | collective-permute-done | bytes 14368 | tf_op jit(solution)/shard_map/ppermute | solution.py:410
  72.7 1.8 %collective-permute-start.14 = (f32[28,128]{1,0:T(8,128)S(1)}, f32[28,128]{1,0:T(8,128)S(1)}, u32[]{:S(2)}, u32[]{:S(2)}) collective-permute-start(f32[28,128]{1,0:T(8,128)S(1)} %fusion.49), channel_id=1, source_target_pairs={{0,1},{1,0},{2,3},{3,2},{4,5},{5,4},{6,7},{7,6},{8,9},{9,8},{10,11... | collective-permute-start | bytes 43016 | tf_op jit(solution)/shard_map/ppermute | solution.py:410
  76.1 3.4 %shard_map.167 = (bf16[4,2,64,2048]{3,2,1,0:T(8,128)(2,1)}, bf16[4,2,64,256]{3,2,1,0:T(8,128)(2,1)}) custom-call(s32[2,4]{1,0:T(2,128)} %bitcast.76, s32[16]{0:T(128)} %holder_ref.5, s32[1,16]{1,0:T(1,128)} %bitcast.81, bf16[2,64,2048]{2,1,0:T(8,128)(2,1)} %collective-permute-done.9.z1, bf16[2,64,2048]{2,1,0:T(8,128)(2,1)} %collective-permute-done.4.z2, ...), custom_call_target="tpu_custom_call" | custom-call | bytes 4718592 | tf_op jit(solution)/shard_map/pallas_call | solution.py:537
  (128 shorter events, 23.5 us)
Async XLA Ops:
  0.6 73.8 %copy-start = (bf16[14,2,16,128]{3,2,1,0:T(8,128)(2,1)S(1)}, bf16[14,2,16,128]{3,2,1,0:T(8,128)(2,1)}, u32[]{:S(2)}) copy-start(bf16[14,2,16,128]{3,2,1,0:T(8,128)(2,1)} %param.14) | copy-start | bytes 344068
  0.6 8.4 %copy-start.14 = (s32[4,2]{0,1:T(2,128)S(1)}, s32[4,2]{0,1:T(2,128)}, u32[]{:S(2)}) copy-start(s32[4,2]{0,1:T(2,128)} %param.20) | copy-start | bytes 100
  0.7 8.4 %copy-start.8 = (bf16[14,2,2048]{2,1,0:T(2,128)(2,1)S(1)}, bf16[14,2,2048]{2,1,0:T(2,128)(2,1)}, u32[]{:S(2)}) copy-start(bf16[14,2,2048]{2,1,0:T(2,128)(2,1)} %param.13) | copy-start | bytes 344068
  0.7 8.5 %copy-start.17 = (s32[48]{0:T(128)S(1)}, s32[48]{0:T(128)}, u32[]{:S(2)}) copy-start(s32[48]{0:T(128)} %param.22) | copy-start | bytes 580
  0.7 8.6 %copy-start.3 = (bf16[8,2,64,256]{3,2,1,0:T(8,128)(2,1)S(1)}, bf16[8,2,64,256]{3,2,1,0:T(8,128)(2,1)}, u32[]{:S(2)}) copy-start(bf16[8,2,64,256]{3,2,1,0:T(8,128)(2,1)} %b_ref.3) | copy-start | bytes 1572868
  4.4 21.9 %collective-permute-start = (bf16[3,2,64,2048]{3,2,1,0:T(8,128)(2,1)}, bf16[3,2,64,2048]{3,2,1,0:T(8,128)(2,1)S(1)}, u32[]{:S(2)}, u32[]{:S(2)}) collective-permute-start(bf16[3,2,64,2048]{3,2,1,0:T(8,128)(2,1)} %get-tuple-element.37), channel_id=1, source_target_pairs={{0,4},{4,0},{8,12},{12,8},{1,5},{5,1},{9,13},{13,9},{2,6},{6,2},{1... | collective-permute-start | bytes 4718600 | tf_op jit(solution)/shard_map/ppermute | solution.py:407
  4.9 11.8 %collective-permute-start.1 = (bf16[4,2,64,256]{3,2,1,0:T(8,128)(2,1)}, bf16[4,2,64,256]{3,2,1,0:T(8,128)(2,1)S(1)}, u32[]{:S(2)}, u32[]{:S(2)}) collective-permute-start(bf16[4,2,64,256]{3,2,1,0:T(8,128)(2,1)} %get-tuple-element.40), channel_id=1, source_target_pairs={{0,4},{4,0},{8,12},{12,8},{1,5},{5,1},{9,13},{13,9},{2,6},{6,2},{1... | collective-permute-start | bytes 786440 | tf_op jit(solution)/shard_map/ppermute | solution.py:407
  5.0 29.4 %collective-permute-start.4 = (bf16[2,64,2048]{2,1,0:T(8,128)(2,1)}, bf16[2,64,2048]{2,1,0:T(8,128)(2,1)}, u32[]{:S(2)}, u32[]{:S(2)}) collective-permute-start(bf16[2,64,2048]{2,1,0:T(8,128)(2,1)} %get-tuple-element.58), channel_id=1, source_target_pairs={{0,8},{4,12},{8,0},{12,4},{1,9},{5,13},{9,1},{13,5},{2,10},{6,14},... | collective-permute-start | bytes 1572872 | tf_op jit(solution)/shard_map/ppermute | solution.py:407
  7.9 26.5 %collective-permute-start.5 = (bf16[128,2,256]{2,1,0:T(2,128)(2,1)}, bf16[128,2,256]{2,1,0:T(2,128)(2,1)}, u32[]{:S(2)}, u32[]{:S(2)}) collective-permute-start(bf16[128,2,256]{2,1,0:T(2,128)(2,1)} %get-tuple-element.47), channel_id=1, source_target_pairs={{0,8},{4,12},{8,0},{12,4},{1,9},{5,13},{9,1},{13,5},{2,10},{6,14},... | collective-permute-start | bytes 393224 | tf_op jit(solution)/shard_map/ppermute | solution.py:407
  8.0 26.5 %collective-permute-start.6 = (bf16[128,2,256]{2,1,0:T(2,128)(2,1)}, bf16[128,2,256]{2,1,0:T(2,128)(2,1)}, u32[]{:S(2)}, u32[]{:S(2)}) collective-permute-start(bf16[128,2,256]{2,1,0:T(2,128)(2,1)} %get-tuple-element.48), channel_id=1, source_target_pairs={{0,12},{4,8},{8,4},{12,0},{1,13},{5,9},{9,5},{13,1},{2,14},{6,10},... | collective-permute-start | bytes 393224 | tf_op jit(solution)/shard_map/ppermute | solution.py:407
  16.7 9.6 %copy-start.4 = (bf16[4,2,64,256]{3,2,1,0:T(8,128)(2,1)}, bf16[4,2,64,256]{3,2,1,0:T(8,128)(2,1)S(1)}, u32[]{:S(2)}) copy-start(bf16[4,2,64,256]{3,2,1,0:T(8,128)(2,1)S(1)} %collective-permute-done.1.core_b.cb) | copy-start | bytes 786436
  17.5 14.3 %collective-permute-start.2 = (bf16[14,2,2048]{2,0,1:T(8,128)(2,1)}, bf16[14,2,2048]{2,0,1:T(8,128)(2,1)}, u32[]{:S(2)}, u32[]{:S(2)}) collective-permute-start(bf16[14,2,2048]{2,0,1:T(8,128)(2,1)} %copy.98), channel_id=1, source_target_pairs={{0,2},{1,3},{2,0},{3,1},{4,6},{5,7},{6,4},{7,5},{8,10},{9,11},{10,... | collective-permute-start | bytes 344072 | tf_op jit(solution)/shard_map/ppermute | solution.py:410
  27.5 9.0 %copy-start.1 = (s32[48]{0:T(128)S(1)}, s32[48]{0:T(128)}, u32[]{:S(2)}) copy-start(s32[48]{0:T(128)} %param.19) | copy-start | bytes 580
  30.8 17.2 %collective-permute-start.7 = (bf16[2,64,2048]{2,1,0:T(8,128)(2,1)}, bf16[2,64,2048]{2,1,0:T(8,128)(2,1)S(1)}, u32[]{:S(2)}, u32[]{:S(2)}) collective-permute-start(bf16[2,64,2048]{2,1,0:T(8,128)(2,1)} %get-tuple-element.41), channel_id=1, source_target_pairs={{0,8},{4,12},{8,0},{12,4},{1,9},{5,13},{9,1},{13,5},{2,10},{6,14},... | collective-permute-start | bytes 1572872 | tf_op jit(solution)/shard_map/ppermute | solution.py:407
  32.8 8.5 %collective-permute-start.8 = (bf16[14,2,4096]{2,0,1:T(8,128)(2,1)S(1)}, bf16[14,2,4096]{2,0,1:T(8,128)(2,1)}, u32[]{:S(2)}, u32[]{:S(2)}) collective-permute-start(bf16[14,2,4096]{2,0,1:T(8,128)(2,1)S(1)} %pad_maximum_fusion.1), channel_id=1, source_target_pairs={{0,1},{1,0},{2,3},{3,2},{4,5},{5,4},{6,7},{7,6},{8,9},{9,8},{10,11... | collective-permute-start | bytes 688136 | tf_op jit(solution)/shard_map/ppermute | solution.py:410
  34.5 28.2 %collective-permute-start.11 = (bf16[2,64,2048]{2,1,0:T(8,128)(2,1)}, bf16[2,64,2048]{2,1,0:T(8,128)(2,1)S(1)}, u32[]{:S(2)}, u32[]{:S(2)}) collective-permute-start(bf16[2,64,2048]{2,1,0:T(8,128)(2,1)} %get-tuple-element.61), channel_id=1, source_target_pairs={{0,8},{4,12},{8,0},{12,4},{1,9},{5,13},{9,1},{13,5},{2,10},{6,14},... | collective-permute-start | bytes 1572872 | tf_op jit(solution)/shard_map/ppermute | solution.py:407
  35.6 27.1 %collective-permute-start.12 = (bf16[4,2,64,256]{3,2,1,0:T(8,128)(2,1)}, bf16[4,2,64,256]{3,2,1,0:T(8,128)(2,1)S(1)}, u32[]{:S(2)}, u32[]{:S(2)}) collective-permute-start(bf16[4,2,64,256]{3,2,1,0:T(8,128)(2,1)} %get-tuple-element.62), channel_id=1, source_target_pairs={{0,8},{4,12},{8,0},{12,4},{1,9},{5,13},{9,1},{13,5},{2,10},{6,14},... | collective-permute-start | bytes 786440 | tf_op jit(solution)/shard_map/ppermute | solution.py:407
  48.0 14.8 %copy-start.5 = (bf16[2,64,2048]{2,1,0:T(8,128)(2,1)}, bf16[2,64,2048]{2,1,0:T(8,128)(2,1)S(1)}, u32[]{:S(2)}) copy-start(bf16[2,64,2048]{2,1,0:T(8,128)(2,1)S(1)} %collective-permute-done.7.f0) | copy-start | bytes 1572868
  48.0 14.8 %collective-permute-start.10 = (bf16[2,64,2048]{2,1,0:T(8,128)(2,1)}, bf16[2,64,2048]{2,1,0:T(8,128)(2,1)S(1)}, u32[]{:S(2)}, u32[]{:S(2)}) collective-permute-start(bf16[2,64,2048]{2,1,0:T(8,128)(2,1)} %collective-permute-done.4.z2), channel_id=1, source_target_pairs={{0,4},{4,0},{8,12},{12,8},{1,5},{5,1},{9,13},{13,9},{2,6},{6,2},{1... | collective-permute-start | bytes 1572872 | tf_op jit(solution)/shard_map/ppermute | solution.py:407
  48.0 14.8 %collective-permute-start.9 = (bf16[2,64,2048]{2,1,0:T(8,128)(2,1)}, bf16[2,64,2048]{2,1,0:T(8,128)(2,1)}, u32[]{:S(2)}, u32[]{:S(2)}) collective-permute-start(bf16[2,64,2048]{2,1,0:T(8,128)(2,1)} %get-tuple-element.58), channel_id=1, source_target_pairs={{0,4},{4,0},{8,12},{12,8},{1,5},{5,1},{9,13},{13,9},{2,6},{6,2},{1... | collective-permute-start | bytes 1572872 | tf_op jit(solution)/shard_map/ppermute | solution.py:407
  53.9 1.6 %collective-permute-start.3 = (bf16[128,2,256]{2,1,0:T(2,128)(2,1)}, bf16[128,2,256]{2,1,0:T(2,128)(2,1)S(1)}, u32[]{:S(2)}, u32[]{:S(2)}) collective-permute-start(bf16[128,2,256]{2,1,0:T(2,128)(2,1)} %get-tuple-element.45), channel_id=1, source_target_pairs={{0,4},{4,0},{8,12},{12,8},{1,5},{5,1},{9,13},{13,9},{2,6},{6,2},{1... | collective-permute-start | bytes 393224 | tf_op jit(solution)/shard_map/ppermute | solution.py:407
  56.1 20.0 %collective-permute-start.15 = (bf16[2,64,2048]{2,1,0:T(8,128)(2,1)}, bf16[2,64,2048]{2,1,0:T(8,128)(2,1)}, u32[]{:S(2)}, u32[]{:S(2)}) collective-permute-start(bf16[2,64,2048]{2,1,0:T(8,128)(2,1)} %get-tuple-element.66), channel_id=1, source_target_pairs={{0,8},{4,12},{8,0},{12,4},{1,9},{5,13},{9,1},{13,5},{2,10},{6,14},... | collective-permute-start | bytes 1572872 | tf_op jit(solution)/shard_map/ppermute | solution.py:407
  67.9 4.7 %collective-permute-start.13 = (f32[28,128]{1,0:T(8,128)S(1)}, f32[28,128]{1,0:T(8,128)S(1)}, u32[]{:S(2)}, u32[]{:S(2)}) collective-permute-start(f32[28,128]{1,0:T(8,128)S(1)} %pad_maximum_fusion.2), channel_id=1, source_target_pairs={{0,2},{1,3},{2,0},{3,1},{4,6},{5,7},{6,4},{7,5},{8,10},{9,11},{10,... | collective-permute-start | bytes 43016 | tf_op jit(solution)/shard_map/ppermute | solution.py:410
  72.7 6.9 %collective-permute-start.14 = (f32[28,128]{1,0:T(8,128)S(1)}, f32[28,128]{1,0:T(8,128)S(1)}, u32[]{:S(2)}, u32[]{:S(2)}) collective-permute-start(f32[28,128]{1,0:T(8,128)S(1)} %fusion.49), channel_id=1, source_target_pairs={{0,1},{1,0},{2,3},{3,2},{4,5},{5,4},{6,7},{7,6},{8,9},{9,8},{10,11... | collective-permute-start | bytes 43016 | tf_op jit(solution)/shard_map/ppermute | solution.py:410
  (14 other events, 37.1 us)

commit v6 on v5

--- a/solution.py
+++ b/solution.py
@@ -445,8 +445,6 @@
     is_own = own_adapter[:, None] == jnp.arange(slots, dtype=jnp.int32)[None, :]
     part_own = jnp.sum(jnp.where(is_own[:, None, :, None, None], every, 0.0), axis=2)
     part_own, core_u = lax.optimization_barrier((part_own, core_u))
-    _, sent = lax.optimization_barrier((core_b, hidden))
-    other = mirror(sent, 2)
 
     def pick(places, copies, core):
         out = pl.pallas_call(
@@ -469,7 +467,10 @@
     z2, far, to1, to_b = lax.optimization_barrier((z2, far, to1, to_b))
     f1, far_b = swap(to1, 2), swap(to_b, 2)
 
-    _, other, lengths, queries, k1 = lax.optimization_barrier((to0, other, lengths, queries, k1))
+    _, hidden, lengths, queries, k1, kv_cache, arrival_from, arrival_slot, own_adapter = lax.optimization_barrier(
+        (to0, hidden, lengths, queries, k1, kv_cache, arrival_from, arrival_slot, own_adapter)
+    )
+    other = mirror(hidden, 2)
     near = swap(k1, 1)
 
     def total(part):
@@ -479,7 +480,7 @@
         return out.astype(jnp.bfloat16)
 
     high, low = tensor_index >= 2, tensor_index % 2 == 1
-    halves = jnp.concatenate([jnp.where(high, other, sent), jnp.where(high, sent, other)], axis=2)
+    halves = jnp.concatenate([jnp.where(high, other, hidden), jnp.where(high, hidden, other)], axis=2)
     other = mirror(halves, 1)
     even, odd = jnp.where(low, other, halves), jnp.where(low, halves, other)
     whole = jnp.concatenate([even[..., :width], odd[..., :width], even[..., width:], odd[..., width:]], axis=2)

time: 84.9 us -> 77.2 us (0.909)
  local copies, waits for them, and re-layouts: 17.5 us -> 9.69 us
  other arithmetic: 10.9 us -> 6.09 us
  starting transfers between devices: 16.1 us -> 19 us
  waiting for transfers between devices: 11.8 us -> 13.6 us
    ppermute x4, starting transfers between devices: 6.38 us -> 9.53 us  [mirror(): return lax.ppermute(array, 'tensor', [(i, i ^ k) for i in range(TENSORS)])]
    unnamed x45 -> x58, local copies, waits for them, and re-layouts: 6.4 us -> 4.05 us
    optimization_barrier x2, local copies, waits for them, and re-layouts: 3.14 us -> 1.34 us  [paired(): z2, far, to1, to_b = lax.optimization_barrier((z2, far, to1, to_b))]
    lt x1, other arithmetic: 1.33 us -> 0.07 us  [paired(): row_ids[None, :] < arrival_len[:, None]]
    ppermute x4, waiting for transfers between devices: 6.47 us -> 7.64 us  [mirror(): return lax.ppermute(array, 'tensor', [(i, i ^ k) for i in range(TENSORS)])]
    select_n x1, other arithmetic: 1.15 us -> 0.11 us  [paired(): jnp.where((row_ids[None, :] < arrival_len[:, None])[:, :, None, None], ar...]
    select_n x1, other arithmetic: 1.01 us -> 0.05 us  [paired(): jnp.where(high, other, hidden)]
    select_n x1, other arithmetic: 1.05 us -> 0.1 us  [paired(): even, odd = (jnp.where(low, other, halves), jnp.where(low, halves, other))]
  transfers between devices with their start and end apart: 16 -> 16, of which waited for: 4 -> 5; matrix products, arithmetic and copies ran while one was open for 41% -> 28% of each run, Pallas kernels for 12% -> 13%
where the time goes in v6:
time: 77.2 us; the launch traced here: 76.5 us
  starting transfers between devices  19 us (25%)
  Pallas kernels  13.8 us (18%)
  waiting for transfers between devices  13.6 us (18%)
  matrix products  13.1 us (17%)
  local copies, waits for them, and re-layouts  9.69 us (13%)
  other arithmetic  6.09 us (8%)
  between operations  1.16 us (2%)
    ppermute x4, starting transfers between devices, mirror(): return lax.ppermute(array, 'tensor', [(i, i ^ k) for i in range(TENSORS)])  9.53 us
    ppermute x12, starting transfers between devices, swap(): return lax.ppermute(array, 'replica', [(i, i ^ k) for i in range(PAIRED)])  9.5 us
    ppermute x4, waiting for transfers between devices, mirror(): return lax.ppermute(array, 'tensor', [(i, i ^ k) for i in range(TENSORS)])  7.64 us
    ppermute x12, waiting for transfers between devices, swap(): return lax.ppermute(array, 'replica', [(i, i ^ k) for i in range(PAIRED)])  5.96 us
    dot_general x1, matrix products, paired(): jnp.einsum('msd,dgc->msgc', whole, w_kv, preferred_element_type=jnp.float32)  5.69 us
    dot_general x1, matrix products, paired(): jnp.einsum('msd,epkd->msepk', hidden[:resident], store_a, preferred_eleme...  4.23 us
    unnamed x58, local copies, waits for them, and re-layouts  4.05 us
    pallas_call x1, Pallas kernels, paired(): pl.pallas_call(functools.partial(pack_kernel, spans, slots), out_shape=(s...  3.87 us
  transfers between devices with their start and end apart: 16, of which 5 were waited for; matrix products, arithmetic and copies ran while one was open for 28% of the time, Pallas kernels for 13%

profile of v6, /device:TPU:0, one launch (start us, length us, event | category | flops | bytes accessed | tf_op | source)
XLA Modules:
  0.0 76.5 jit_solution(1097348447150999587)
XLA Ops:
  0.7 3.9 %shard_map.164 = (bf16[2,64,2048]{2,1,0:T(8,128)(2,1)}, bf16[3,2,64,2048]{3,2,1,0:T(8,128)(2,1)}, bf16[4,2,64,256]{3,2,1,0:T(8,128)(2,1)}, bf16[128,2,256]{2,1,0...) custom-call(s32[2,4]{1,0:T(2,128)} %bitcast.77, s32[2,4]{1,0:T(2,128)} %bitcast.78, ...), custom_call_target="tpu_custom_call" | custom-call | bytes 4718592 | tf_op jit(solution)/shard_map/pallas_call | solution.py:420
  5.1 2.8 %collective-permute-start.3 = (bf16[2,64,2048]{2,1,0:T(8,128)(2,1)}, bf16[2,64,2048]{2,1,0:T(8,128)(2,1)}, u32[]{:S(2)}, u32[]{:S(2)}) collective-permute-start(bf16[2,64,2048]{2,1,0:T(8,128)(2,1)} %get-tuple-element.64), channel_id=1, source_target_pairs={{0,8},{4,12},{8,0},{12,4},{1,9},{5,13},{9,1},{13,5},{2,10},{6,14},... | collective-permute-start | bytes 1572872 | tf_op jit(solution)/shard_map/ppermute | solution.py:407
  7.9 1.1 %collective-permute-start.5 = (bf16[128,2,256]{2,1,0:T(2,128)(2,1)}, bf16[128,2,256]{2,1,0:T(2,128)(2,1)S(1)}, u32[]{:S(2)}, u32[]{:S(2)}) collective-permute-start(bf16[128,2,256]{2,1,0:T(2,128)(2,1)} %get-tuple-element.53), channel_id=1, source_target_pairs={{0,12},{4,8},{8,4},{12,0},{1,13},{5,9},{9,5},{13,1},{2,14},{6,10},... | collective-permute-start | bytes 393224 | tf_op jit(solution)/shard_map/ppermute | solution.py:407
  9.2 4.2 %fusion.11 = f32[12,2,2,64]{3,0,2,1:T(8,128)S(1)} fusion(bf16[8,2,64,2048]{3,2,1,0:T(8,128)(2,1)} %a_ref.3, bf16[14,2,2048]{2,0,1:T(8,128)(2,1)S(1)} %copy.96, pred[12,8]{0,1:T(8,128)(4,1)S(1)} %iota_compare_fusion.1), kind=kOutput, calls=%fused_computation.15 | convolution fusion | flops 100709376 | bytes 4321376 | tf_op jit(solution)/shard_map/msd,epkd->msepk/dot_general | solution.py:444
  14.6 1.2 %copy-done.2 = bf16[3,2,64,2048]{3,2,1,0:T(8,128)(2,1)} copy-done((bf16[3,2,64,2048]{3,2,1,0:T(8,128)(2,1)}, bf16[3,2,64,2048]{3,2,1,0:T(8,128)(2,1)S(1)}, u32[]{:S(2)}) %copy-start.2) | copy-done | bytes 1572888
  15.9 3.2 %shard_map.165 = (bf16[2,64,2048]{2,1,0:T(8,128)(2,1)}, bf16[2,64,2048]{2,1,0:T(8,128)(2,1)}, bf16[2,64,2048]{2,1,0:T(8,128)(2,1)}, bf16[4,2,64,256]{3,2,1,0:T(8,128)(2,1)}) custom-call(s32[2,4]{1,0:T(2,128)} %bitcast.74, s32[16]{0:T(128)} %holder_ref.5, s32[1,16]{1,0:T(1,128)} %bitcast.79, bf16[8,2,64,2048]{3,2,1,0:T(8,128)(2,1)} %a_ref.3, ...), custom_call_target="tpu_custom_call" | custom-call | bytes 3670016 | tf_op jit(solution)/shard_map/pallas_call | solution.py:450
  19.2 0.9 %collective-permute-start.6 = (bf16[2,64,2048]{2,1,0:T(8,128)(2,1)}, bf16[2,64,2048]{2,1,0:T(8,128)(2,1)S(1)}, u32[]{:S(2)}, u32[]{:S(2)}) collective-permute-start(bf16[2,64,2048]{2,1,0:T(8,128)(2,1)} %get-tuple-element.44), channel_id=1, source_target_pairs={{0,8},{4,12},{8,0},{12,4},{1,9},{5,13},{9,1},{13,5},{2,10},{6,14},... | collective-permute-start | bytes 1572872 | tf_op jit(solution)/shard_map/ppermute | solution.py:407
  20.1 2.7 %collective-permute-start.7 = (bf16[14,2,2048]{2,0,1:T(8,128)(2,1)S(1)}, bf16[14,2,2048]{2,0,1:T(8,128)(2,1)S(1)}, u32[]{:S(2)}, u32[]{:S(2)}) collective-permute-start(bf16[14,2,2048]{2,0,1:T(8,128)(2,1)S(1)} %copy.103), channel_id=1, source_target_pairs={{0,2},{1,3},{2,0},{3,1},{4,6},{5,7},{6,4},{7,5},{8,10},{9,11},{10,... | collective-permute-start | bytes 344072 | tf_op jit(solution)/shard_map/ppermute | solution.py:410
  22.8 0.8 %collective-permute-done.4 = bf16[128,2,256]{2,1,0:T(2,128)(2,1)S(1)} collective-permute-done((bf16[128,2,256]{2,1,0:T(2,128)(2,1)}, bf16[128,2,256]{2,1,0:T(2,128)(2,1)S(1)}, u32[]{:S(2)}, u32[]{:S(2)}) %collective-permute-start.4) | collective-permute-done | bytes 131104 | tf_op jit(solution)/shard_map/ppermute | solution.py:407
  23.6 2.5 %collective-permute-done.5 = bf16[128,2,256]{2,1,0:T(2,128)(2,1)S(1)} collective-permute-done((bf16[128,2,256]{2,1,0:T(2,128)(2,1)}, bf16[128,2,256]{2,1,0:T(2,128)(2,1)S(1)}, u32[]{:S(2)}, u32[]{:S(2)}) %collective-permute-start.5) | collective-permute-done | bytes 131104 | tf_op jit(solution)/shard_map/ppermute | solution.py:407
  26.8 1.4 %collective-permute-start.12 = (bf16[4,2,64,256]{3,2,1,0:T(8,128)(2,1)}, bf16[4,2,64,256]{3,2,1,0:T(8,128)(2,1)}, u32[]{:S(2)}, u32[]{:S(2)}) collective-permute-start(bf16[4,2,64,256]{3,2,1,0:T(8,128)(2,1)} %get-tuple-element.68), channel_id=1, source_target_pairs={{0,8},{4,12},{8,0},{12,4},{1,9},{5,13},{9,1},{13,5},{2,10},{6,14},... | collective-permute-start | bytes 786440 | tf_op jit(solution)/shard_map/ppermute | solution.py:407
  29.0 1.1 %broadcast_select_fusion = bf16[12,2,64,256]{3,2,1,0:T(8,128)(2,1)} fusion(bf16[12,2,64,256]{3,2,1,0:T(8,128)(2,1)S(1)} %gather_fusion.1, pred[12]{0:T(512)(128)(4,1)S(1)} %compare_and_fusion), kind=kLoop, calls=%fused_computation.30 | loop fusion | flops 393216 | bytes 1572876 | tf_op jit(solution)/shard_map/jit(_take)/select_n | solution.py:509
  31.2 1.6 %collective-permute-start.8 = (bf16[14,2,4096]{2,0,1:T(8,128)(2,1)S(1)}, bf16[14,2,4096]{2,0,1:T(8,128)(2,1)S(1)}, u32[]{:S(2)}, u32[]{:S(2)}) collective-permute-start(bf16[14,2,4096]{2,0,1:T(8,128)(2,1)S(1)} %pad_maximum_fusion.1), channel_id=1, source_target_pairs={{0,1},{1,0},{2,3},{3,2},{4,5},{5,4},{6,7},{7,6},{8,9},{9,8},{10,11... | collective-permute-start | bytes 688136 | tf_op jit(solution)/shard_map/ppermute | solution.py:410
  33.8 6.0 %collective-permute-done.8 = bf16[14,2,4096]{2,0,1:T(8,128)(2,1)S(1)} collective-permute-done((bf16[14,2,4096]{2,0,1:T(8,128)(2,1)S(1)}, bf16[14,2,4096]{2,0,1:T(8,128)(2,1)S(1)}, u32[]{:S(2)}, u32[]{:S(2)}) %collective-permute-start.8) | collective-permute-done | bytes 229408 | tf_op jit(solution)/shard_map/ppermute | solution.py:410
  40.0 5.7 %fusion = f32[14,2,2,256]{3,0,2,1:T(8,128)} fusion(bf16[8192,2,256]{2,1,0:T(2,128)(2,1)} %param.16, bf16[14,2,2048]{2,0,1:T(8,128)(2,1)S(1)} %get-tuple-element.120, bf16[14,2,2048]{2,0,1:T(8,128)(2,1)S(1)} %get-tuple-element.105, bf16[14,2,2048]{2,0,1:T(8,128)(2,1)S(1)} %get-tuple-element.121, bf16[14,2,2048]{2,0,1:T(8,128)(2,1)S(1)} %get-tuple-element.104), kind=kOutput, calls=%fused_computation.2 | convolution fusion | flops 236716032 | bytes 8904704 | tf_op jit(solution)/shard_map/msd,dgc->msgc/dot_general | solution.py:487
  50.3 1.5 %collective-permute-start.15 = (bf16[2,64,2048]{2,1,0:T(8,128)(2,1)}, bf16[2,64,2048]{2,1,0:T(8,128)(2,1)S(1)}, u32[]{:S(2)}, u32[]{:S(2)}) collective-permute-start(bf16[2,64,2048]{2,1,0:T(8,128)(2,1)} %get-tuple-element.72), channel_id=1, source_target_pairs={{0,8},{4,12},{8,0},{12,4},{1,9},{5,13},{9,1},{13,5},{2,10},{6,14},... | collective-permute-start | bytes 1572872 | tf_op jit(solution)/shard_map/ppermute | solution.py:407
  51.8 2.6 %collective-permute-done.12.xb = bf16[4,2,64,256]{3,2,1,0:T(8,128)(2,1)} collective-permute-done((bf16[4,2,64,256]{3,2,1,0:T(8,128)(2,1)}, bf16[4,2,64,256]{3,2,1,0:T(8,128)(2,1)}, u32[]{:S(2)}, u32[]{:S(2)}) %collective-permute-start.12) | collective-permute-done | bytes 262176 | tf_op jit(solution)/shard_map/ppermute | solution.py:407
  54.4 3.4 %shard_map.166 = (f32[2,16,128]{2,1,0:T(8,128)}, bf16[2,2,64,256]{3,2,1,0:T(8,128)(2,1)}) custom-call(s32[2,4]{1,0:T(2,128)} %bitcast.75, s32[16]{0:T(128)} %holder_ref.5, s32[1,16]{1,0:T(1,128)} %bitcast.80, bf16[16,2048]{1,0:T(8,128)(2,1)} %pad.5.hid_ref, bf16[2,64,2048]{2,1,0:T(8,128)(2,1)} %collective-permute-done.9.z1, ...), custom_call_target="tpu_custom_call" | custom-call | flops 16777216 | bytes 1310720 | tf_op jit(solution)/shard_map/pallas_call | solution.py:517
  58.5 3.3 %collective-permute-start.13 = (f32[28,128]{1,0:T(8,128)S(1)}, f32[28,128]{1,0:T(8,128)S(1)}, u32[]{:S(2)}, u32[]{:S(2)}) collective-permute-start(f32[28,128]{1,0:T(8,128)S(1)} %pad_maximum_fusion.2), channel_id=1, source_target_pairs={{0,2},{1,3},{2,0},{3,1},{4,6},{5,7},{6,4},{7,5},{8,10},{9,11},{10,... | collective-permute-start | bytes 43016 | tf_op jit(solution)/shard_map/ppermute | solution.py:410
  62.0 1.6 %collective-permute-done.13 = f32[28,128]{1,0:T(8,128)S(1)} collective-permute-done((f32[28,128]{1,0:T(8,128)S(1)}, f32[28,128]{1,0:T(8,128)S(1)}, u32[]{:S(2)}, u32[]{:S(2)}) %collective-permute-start.13) | collective-permute-done | bytes 14368 | tf_op jit(solution)/shard_map/ppermute | solution.py:410
  63.6 2.0 %collective-permute-start.14 = (f32[28,128]{1,0:T(8,128)S(1)}, f32[28,128]{1,0:T(8,128)S(1)}, u32[]{:S(2)}, u32[]{:S(2)}) collective-permute-start(f32[28,128]{1,0:T(8,128)S(1)} %fusion.49), channel_id=1, source_target_pairs={{0,1},{1,0},{2,3},{3,2},{4,5},{5,4},{6,7},{7,6},{8,9},{9,8},{10,11... | collective-permute-start | bytes 43016 | tf_op jit(solution)/shard_map/ppermute | solution.py:410
  66.3 1.0 %copy.116 = bf16[2,128,2,256]{3,2,1,0:T(2,128)(2,1)} copy(bf16[2,128,2,256]{3,1,2,0:T(8,128)(2,1)S(1)} %select_select_fusion) | data formatting | bytes 524288
  68.1 3.3 %shard_map.167 = (bf16[4,2,64,2048]{3,2,1,0:T(8,128)(2,1)}, bf16[4,2,64,256]{3,2,1,0:T(8,128)(2,1)}) custom-call(s32[2,4]{1,0:T(2,128)} %bitcast.76, s32[16]{0:T(128)} %holder_ref.5, s32[1,16]{1,0:T(1,128)} %bitcast.81, bf16[2,64,2048]{2,1,0:T(8,128)(2,1)} %collective-permute-done.9.z1, bf16[2,64,2048]{2,1,0:T(8,128)(2,1)} %collective-permute-done.3.z2, ...), custom_call_target="tpu_custom_call" | custom-call | bytes 4718592 | tf_op jit(solution)/shard_map/pallas_call | solution.py:538
  71.5 1.2 %fusion.16 = f32[14,2,2,256]{3,1,2,0:T(2,128)S(1)} fusion(bf16[2,2,64,256]{3,2,1,0:T(8,128)(2,1)} %get-tuple-element.69, bf16[12,2,64,256]{3,2,1,0:T(8,128)(2,1)S(1)} %copy-done.8, bf16[14,2,2,64]{3,2,1,0:T(2,128)(2,1)S(1)} %reshape.238), kind=kOutput, calls=%fused_computation.20 | convolution fusion | flops 2308096 | bytes 982016 | tf_op jit(solution)/shard_map/gnot,gote->gnoe/dot_general | solution.py:502
  (143 shorter events, 16.4 us)
Async XLA Ops:
  0.6 65.0 %copy-start = (bf16[14,2,16,128]{3,2,1,0:T(8,128)(2,1)S(1)}, bf16[14,2,16,128]{3,2,1,0:T(8,128)(2,1)}, u32[]{:S(2)}) copy-start(bf16[14,2,16,128]{3,2,1,0:T(8,128)(2,1)} %param.14) | copy-start | bytes 344068
  4.5 10.0 %collective-permute-start = (bf16[3,2,64,2048]{3,2,1,0:T(8,128)(2,1)}, bf16[3,2,64,2048]{3,2,1,0:T(8,128)(2,1)S(1)}, u32[]{:S(2)}, u32[]{:S(2)}) collective-permute-start(bf16[3,2,64,2048]{3,2,1,0:T(8,128)(2,1)} %get-tuple-element.40), channel_id=1, source_target_pairs={{0,4},{4,0},{8,12},{12,8},{1,5},{5,1},{9,13},{13,9},{2,6},{6,2},{1... | collective-permute-start | bytes 4718600 | tf_op jit(solution)/shard_map/ppermute | solution.py:407
  5.0 9.6 %collective-permute-start.1 = (bf16[4,2,64,256]{3,2,1,0:T(8,128)(2,1)}, bf16[4,2,64,256]{3,2,1,0:T(8,128)(2,1)S(1)}, u32[]{:S(2)}, u32[]{:S(2)}) collective-permute-start(bf16[4,2,64,256]{3,2,1,0:T(8,128)(2,1)} %get-tuple-element.43), channel_id=1, source_target_pairs={{0,4},{4,0},{8,12},{12,8},{1,5},{5,1},{9,13},{13,9},{2,6},{6,2},{1... | collective-permute-start | bytes 786440 | tf_op jit(solution)/shard_map/ppermute | solution.py:407
  5.1 21.0 %collective-permute-start.3 = (bf16[2,64,2048]{2,1,0:T(8,128)(2,1)}, bf16[2,64,2048]{2,1,0:T(8,128)(2,1)}, u32[]{:S(2)}, u32[]{:S(2)}) collective-permute-start(bf16[2,64,2048]{2,1,0:T(8,128)(2,1)} %get-tuple-element.64), channel_id=1, source_target_pairs={{0,8},{4,12},{8,0},{12,4},{1,9},{5,13},{9,1},{13,5},{2,10},{6,14},... | collective-permute-start | bytes 1572872 | tf_op jit(solution)/shard_map/ppermute | solution.py:407
  7.9 15.7 %collective-permute-start.4 = (bf16[128,2,256]{2,1,0:T(2,128)(2,1)}, bf16[128,2,256]{2,1,0:T(2,128)(2,1)S(1)}, u32[]{:S(2)}, u32[]{:S(2)}) collective-permute-start(bf16[128,2,256]{2,1,0:T(2,128)(2,1)} %get-tuple-element.52), channel_id=1, source_target_pairs={{0,8},{4,12},{8,0},{12,4},{1,9},{5,13},{9,1},{13,5},{2,10},{6,14},... | collective-permute-start | bytes 393224 | tf_op jit(solution)/shard_map/ppermute | solution.py:407
  7.9 18.2 %collective-permute-start.5 = (bf16[128,2,256]{2,1,0:T(2,128)(2,1)}, bf16[128,2,256]{2,1,0:T(2,128)(2,1)S(1)}, u32[]{:S(2)}, u32[]{:S(2)}) collective-permute-start(bf16[128,2,256]{2,1,0:T(2,128)(2,1)} %get-tuple-element.53), channel_id=1, source_target_pairs={{0,12},{4,8},{8,4},{12,0},{1,13},{5,9},{9,5},{13,1},{2,14},{6,10},... | collective-permute-start | bytes 393224 | tf_op jit(solution)/shard_map/ppermute | solution.py:407
  15.9 12.3 %copy-start.3 = (bf16[8,2,64,256]{3,2,1,0:T(8,128)(2,1)S(1)}, bf16[8,2,64,256]{3,2,1,0:T(8,128)(2,1)}, u32[]{:S(2)}) copy-start(bf16[8,2,64,256]{3,2,1,0:T(8,128)(2,1)} %b_ref.3) | copy-start | bytes 1572868
  19.1 9.7 %copy-start.17 = (s32[4,2]{0,1:T(2,128)S(1)}, s32[4,2]{0,1:T(2,128)}, u32[]{:S(2)}) copy-start(s32[4,2]{0,1:T(2,128)} %param.20) | copy-start | bytes 100
  19.1 9.7 %copy-start.18 = (s32[4,2]{0,1:T(2,128)S(1)}, s32[4,2]{0,1:T(2,128)}, u32[]{:S(2)}) copy-start(s32[4,2]{0,1:T(2,128)} %param.21) | copy-start | bytes 100
  19.1 10.9 %copy-start.1 = (s32[48]{0:T(128)S(1)}, s32[48]{0:T(128)}, u32[]{:S(2)}) copy-start(s32[48]{0:T(128)} %param.19) | copy-start | bytes 580
  19.2 26.5 %collective-permute-start.6 = (bf16[2,64,2048]{2,1,0:T(8,128)(2,1)}, bf16[2,64,2048]{2,1,0:T(8,128)(2,1)S(1)}, u32[]{:S(2)}, u32[]{:S(2)}) collective-permute-start(bf16[2,64,2048]{2,1,0:T(8,128)(2,1)} %get-tuple-element.44), channel_id=1, source_target_pairs={{0,8},{4,12},{8,0},{12,4},{1,9},{5,13},{9,1},{13,5},{2,10},{6,14},... | collective-permute-start | bytes 1572872 | tf_op jit(solution)/shard_map/ppermute | solution.py:407
  20.1 10.8 %collective-permute-start.7 = (bf16[14,2,2048]{2,0,1:T(8,128)(2,1)S(1)}, bf16[14,2,2048]{2,0,1:T(8,128)(2,1)S(1)}, u32[]{:S(2)}, u32[]{:S(2)}) collective-permute-start(bf16[14,2,2048]{2,0,1:T(8,128)(2,1)S(1)} %copy.103), channel_id=1, source_target_pairs={{0,2},{1,3},{2,0},{3,1},{4,6},{5,7},{6,4},{7,5},{8,10},{9,11},{10,... | collective-permute-start | bytes 344072 | tf_op jit(solution)/shard_map/ppermute | solution.py:410
  26.1 28.2 %collective-permute-start.11 = (bf16[2,64,2048]{2,1,0:T(8,128)(2,1)}, bf16[2,64,2048]{2,1,0:T(8,128)(2,1)}, u32[]{:S(2)}, u32[]{:S(2)}) collective-permute-start(bf16[2,64,2048]{2,1,0:T(8,128)(2,1)} %get-tuple-element.67), channel_id=1, source_target_pairs={{0,8},{4,12},{8,0},{12,4},{1,9},{5,13},{9,1},{13,5},{2,10},{6,14},... | collective-permute-start | bytes 1572872 | tf_op jit(solution)/shard_map/ppermute | solution.py:407
  26.8 27.6 %collective-permute-start.12 = (bf16[4,2,64,256]{3,2,1,0:T(8,128)(2,1)}, bf16[4,2,64,256]{3,2,1,0:T(8,128)(2,1)}, u32[]{:S(2)}, u32[]{:S(2)}) collective-permute-start(bf16[4,2,64,256]{3,2,1,0:T(8,128)(2,1)} %get-tuple-element.68), channel_id=1, source_target_pairs={{0,8},{4,12},{8,0},{12,4},{1,9},{5,13},{9,1},{13,5},{2,10},{6,14},... | collective-permute-start | bytes 786440 | tf_op jit(solution)/shard_map/ppermute | solution.py:407
  31.2 8.6 %collective-permute-start.8 = (bf16[14,2,4096]{2,0,1:T(8,128)(2,1)S(1)}, bf16[14,2,4096]{2,0,1:T(8,128)(2,1)S(1)}, u32[]{:S(2)}, u32[]{:S(2)}) collective-permute-start(bf16[14,2,4096]{2,0,1:T(8,128)(2,1)S(1)} %pad_maximum_fusion.1), channel_id=1, source_target_pairs={{0,1},{1,0},{2,3},{3,2},{4,5},{5,4},{6,7},{7,6},{8,9},{9,8},{10,11... | collective-permute-start | bytes 688136 | tf_op jit(solution)/shard_map/ppermute | solution.py:410
  45.7 8.7 %collective-permute-start.10 = (bf16[2,64,2048]{2,1,0:T(8,128)(2,1)}, bf16[2,64,2048]{2,1,0:T(8,128)(2,1)}, u32[]{:S(2)}, u32[]{:S(2)}) collective-permute-start(bf16[2,64,2048]{2,1,0:T(8,128)(2,1)} %collective-permute-done.3.z2), channel_id=1, source_target_pairs={{0,4},{4,0},{8,12},{12,8},{1,5},{5,1},{9,13},{13,9},{2,6},{6,2},{1... | collective-permute-start | bytes 1572872 | tf_op jit(solution)/shard_map/ppermute | solution.py:407
  45.7 8.7 %collective-permute-start.9 = (bf16[2,64,2048]{2,1,0:T(8,128)(2,1)}, bf16[2,64,2048]{2,1,0:T(8,128)(2,1)}, u32[]{:S(2)}, u32[]{:S(2)}) collective-permute-start(bf16[2,64,2048]{2,1,0:T(8,128)(2,1)} %get-tuple-element.64), channel_id=1, source_target_pairs={{0,4},{4,0},{8,12},{12,8},{1,5},{5,1},{9,13},{13,9},{2,6},{6,2},{1... | collective-permute-start | bytes 1572872 | tf_op jit(solution)/shard_map/ppermute | solution.py:407
  48.4 1.8 %collective-permute-start.2 = (bf16[128,2,256]{2,1,0:T(2,128)(2,1)}, bf16[128,2,256]{2,1,0:T(2,128)(2,1)S(1)}, u32[]{:S(2)}, u32[]{:S(2)}) collective-permute-start(bf16[128,2,256]{2,1,0:T(2,128)(2,1)} %get-tuple-element.50), channel_id=1, source_target_pairs={{0,4},{4,0},{8,12},{12,8},{1,5},{5,1},{9,13},{13,9},{2,6},{6,2},{1... | collective-permute-start | bytes 393224 | tf_op jit(solution)/shard_map/ppermute | solution.py:407
  50.3 11.6 %copy-start.10 = (bf16[128,2,256]{2,0,1:T(8,128)(2,1)S(1)}, bf16[128,2,256]{2,0,1:T(8,128)(2,1)}, u32[]{:S(2)}) copy-start(bf16[128,2,256]{2,0,1:T(8,128)(2,1)} %copy.100) | copy-start | bytes 393220
  50.3 11.6 %copy-start.11 = (bf16[128,2,256]{2,0,1:T(8,128)(2,1)S(1)}, bf16[128,2,256]{2,0,1:T(8,128)(2,1)}, u32[]{:S(2)}) copy-start(bf16[128,2,256]{2,0,1:T(8,128)(2,1)} %copy.99) | copy-start | bytes 393220
  50.3 15.3 %copy-start.19 = (pred[14,128]{1,0:T(8,128)(4,1)S(1)}, pred[14,128]{1,0:T(8,128)(4,1)}, u32[]{:S(2)}) copy-start(pred[14,128]{1,0:T(8,128)(4,1)} %iota_compare_fusion) | copy-start | bytes 5380
  50.3 17.0 %collective-permute-start.15 = (bf16[2,64,2048]{2,1,0:T(8,128)(2,1)}, bf16[2,64,2048]{2,1,0:T(8,128)(2,1)S(1)}, u32[]{:S(2)}, u32[]{:S(2)}) collective-permute-start(bf16[2,64,2048]{2,1,0:T(8,128)(2,1)} %get-tuple-element.72), channel_id=1, source_target_pairs={{0,8},{4,12},{8,0},{12,4},{1,9},{5,13},{9,1},{13,5},{2,10},{6,14},... | collective-permute-start | bytes 1572872 | tf_op jit(solution)/shard_map/ppermute | solution.py:407
  58.5 5.1 %collective-permute-start.13 = (f32[28,128]{1,0:T(8,128)S(1)}, f32[28,128]{1,0:T(8,128)S(1)}, u32[]{:S(2)}, u32[]{:S(2)}) collective-permute-start(f32[28,128]{1,0:T(8,128)S(1)} %pad_maximum_fusion.2), channel_id=1, source_target_pairs={{0,2},{1,3},{2,0},{3,1},{4,6},{5,7},{6,4},{7,5},{8,10},{9,11},{10,... | collective-permute-start | bytes 43016 | tf_op jit(solution)/shard_map/ppermute | solution.py:410
  63.6 7.8 %collective-permute-start.14 = (f32[28,128]{1,0:T(8,128)S(1)}, f32[28,128]{1,0:T(8,128)S(1)}, u32[]{:S(2)}, u32[]{:S(2)}) collective-permute-start(f32[28,128]{1,0:T(8,128)S(1)} %fusion.49), channel_id=1, source_target_pairs={{0,1},{1,0},{2,3},{3,2},{4,5},{5,4},{6,7},{7,6},{8,9},{9,8},{10,11... | collective-permute-start | bytes 43016 | tf_op jit(solution)/shard_map/ppermute | solution.py:410
  (21 other events, 81.8 us)
